TPU v7x, 32 devices: a whole 2x2x4 slice. The times are simulated.
32 devices in a mesh: groups: 2 (over x), node: 8 (over z, y), feat: 2 (over core).
Axes of the slice: x: 2, y: 2, z: 4, core: 2. Of those that a mesh axis runs over, the one named last changes fastest.
Arguments:
- features: bfloat16 [8192, 1024], P(('groups', 'node'), 'feat'), parts along dimension 0, may hold values from -6 to 6
- tile_list: int32 [32, 8], P('groups'), parts along dimension 0, may hold values from 0 to 15, as said below
- tile_values: bfloat16 [32, 8, 256, 256], P(('groups', 'node')), parts along dimension 0, may hold values from 0 to 1
- degree: int32 [8192], P(('groups', 'node')), parts along dimension 0, may hold values from 128 to 1024
- w_self: bfloat16 [1024, 1024], P('feat'), may hold values from -0.1875 to 0.1875
- w_neigh: bfloat16 [1024, 1024], P('feat'), may hold values from -3 to 3
- cotangent: bfloat16 [8192, 1024], P(('groups', 'node'), 'feat'), parts along dimension 0, may hold values from -6 to 6
Outputs:
- hidden: bfloat16 [8192, 1024], P(('groups', 'node'), 'feat'), parts along dimension 0
- grad_features: bfloat16 [8192, 1024], P(('groups', 'node'), 'feat'), parts along dimension 0
- grad_self: float32 [2048, 1024], P(('groups', 'feat'), 'node'), parts along dimension 0
- grad_neigh: float32 [2048, 1024], P(('groups', 'feat'), 'node'), parts along dimension 0
There are 2 independent parts, one for each index of `groups`. A program takes and returns all parts, laid end to end along the dimension named above; an argument that names none is the same for every part. Nothing has to cross between parts.
Inputs may be any that keep to these rules, and one draw needn't show every extreme that they name: `tile_list`: the 16 entries of one node device's 2 block rows name at most one block of each other node device, and blocks of exactly min(14, 7) other node devices; every other entry names one of the device's own blocks.
All inputs are finite; a program needn't handle non-finite values.
Results may differ from a plain program's by a relative error of at most 0.008.
Values may be sent and summed in bfloat16 or wider, within the bound.
No kernel may reach another device: no remote copies, remote signals or barrier semaphores. Data moves between devices by JAX's collectives and lax.ppermute only.
A program may use at most 128 MiB of HBM per device.

v0:
```python
import jax
import jax.numpy as jnp
from jax import lax
from jax.sharding import PartitionSpec as P

TILE = 256
TPR = 8


def on_device(features, tile_list, tile_values, degree, w_self, w_neigh, cotangent):
    node_count = lax.axis_size("node")
    own_index = lax.axis_index("node")
    own_rows, half_width = features.shape
    own_blocks = own_rows // TILE
    slot_count = own_blocks * TPR
    mine = lax.dynamic_slice_in_dim(tile_list, own_index * own_blocks, own_blocks, 0).reshape(
        slot_count
    )
    owner = mine // own_blocks
    inside = owner == own_index
    inverse = (1.0 / degree.astype(jnp.float32)).reshape(own_blocks, TILE, 1)
    device_ids = jnp.arange(node_count, dtype=jnp.int32)
    my_ids = own_index * own_blocks + jnp.arange(own_blocks, dtype=jnp.int32)
    everyone = tile_list.reshape(node_count, slot_count)
    wanted = jnp.any(everyone[:, :, None] == my_ids[None, None, :], axis=1)
    wanted = wanted & (device_ids != own_index)[:, None]
    whole = lax.all_gather(features, "node", axis=0, tiled=True)
    gathered = whole.reshape(-1, TILE, half_width)[mine]
    gathered = gathered.reshape(own_blocks, TPR, TILE, half_width)
    total = jnp.einsum("btij,btjf->bif", tile_values, gathered, preferred_element_type=jnp.float32)
    aggregated = (total * inverse).astype(jnp.bfloat16).reshape(own_rows, half_width)
    partial_sum = jnp.dot(features, w_self, preferred_element_type=jnp.float32) + jnp.dot(
        aggregated, w_neigh, preferred_element_type=jnp.float32
    )
    pre_act = lax.psum_scatter(partial_sum, "feat", scatter_dimension=1, tiled=True)
    sigmoid_z = jax.nn.sigmoid(pre_act)
    hidden = (pre_act * sigmoid_z).astype(jnp.bfloat16)
    slope_half = (
        cotangent.astype(jnp.float32) * sigmoid_z * (1.0 + pre_act * (1.0 - sigmoid_z))
    ).astype(jnp.bfloat16)
    slope = lax.all_gather(slope_half, "feat", axis=1, tiled=True)
    contract_out = (((1,), (1,)), ((), ()))
    contract_rows = (((0,), (0,)), ((), ()))
    back_self = lax.dot_general(slope, w_self, contract_out, preferred_element_type=jnp.float32)
    back_neigh = lax.dot_general(slope, w_neigh, contract_out, preferred_element_type=jnp.float32)
    self_term = lax.dot_general(features, slope, contract_rows, preferred_element_type=jnp.float32)
    neigh_term = lax.dot_general(
        aggregated, slope, contract_rows, preferred_element_type=jnp.float32
    )
    grad_self, grad_neigh = (
        lax.psum_scatter(self_term, "node", scatter_dimension=1, tiled=True),
        lax.psum_scatter(neigh_term, "node", scatter_dimension=1, tiled=True),
    )
    scaled = (back_neigh.reshape(own_blocks, TILE, half_width) * inverse).astype(jnp.bfloat16)
    pieces = jnp.einsum(
        "btij,bif->btjf", tile_values, scaled, preferred_element_type=jnp.float32
    ).reshape(slot_count, TILE, half_width)
    remote_hot = ((owner[None, :] == device_ids[:, None]) & ~inside[None, :]).astype(jnp.float32)
    outgoing_back = jnp.einsum("ns,srf->nrf", remote_hot, pieces).astype(jnp.bfloat16)
    returned = lax.all_to_all(outgoing_back, "node", split_axis=0, concat_axis=0, tiled=True)
    received = jnp.einsum("nb,nrf->brf", wanted.astype(jnp.float32), returned.astype(jnp.float32))
    local_hot = ((mine[None, :] == my_ids[:, None]) & inside[None, :]).astype(jnp.float32)
    local_sum = jnp.einsum("bs,srf->brf", local_hot, pieces)
    grad_features = (back_self + (local_sum + received).reshape(own_rows, half_width)).astype(
        jnp.bfloat16
    )
    return (hidden, grad_features, grad_self, grad_neigh)


def solution(mesh):
    return jax.shard_map(
        on_device,
        mesh=mesh,
        in_specs=(
            P(("groups", "node"), "feat"),
            P("groups", None),
            P(("groups", "node"), None, None, None),
            P(("groups", "node")),
            P("feat", None),
            P("feat", None),
            P(("groups", "node"), "feat"),
        ),
        out_specs=(
            P(("groups", "node"), "feat"),
            P(("groups", "node"), "feat"),
            P(("groups", "feat"), "node"),
            P(("groups", "feat"), "node"),
        ),
        check_vma=False,
    )
```

profile of v0, /device:TPU:0, one launch (start us, length us, event | category | flops | bytes accessed | tf_op | source)
XLA Modules:
  0.0 300.1 jit_solution(10948242182255859917)
XLA Ops:
  9.6 3.5 %fusion.29 = f32[512,1024]{1,0:T(8,128)} fusion(bf16[512,512]{1,0:T(8,128)(2,1)} %param.7, bf16[512,1024]{1,0:T(8,128)(2,1)} %param.11), kind=kOutput, calls=%fused_computation.48 | convolution fusion | flops 536870912 | bytes 3670016 | tf_op jit(solution)/shard_map/dot_general | solution.py:32
  13.1 73.2 %all-gather.3.cloned.1.call-done = bf16[4096,512]{1,0:T(8,128)(2,1)} async-done(((bf16[512,512]{1,0:T(8,128)(2,1)}), bf16[4096,512]{1,0:T(8,128)(2,1)}) %all-gather.3.cloned.1.call-update) | async-done | bytes 4194320 | tf_op jit(solution)/shard_map/all_gather | solution.py:27
  86.3 5.0 %gather_fusion = bf16[16,256,512]{2,1,0:T(8,128)(2,1)} fusion(bf16[16,256,512]{2,1,0:T(8,128)(2,1)} %bitcast.53, s32[1024]{0:T(1024)S(1)} %pad_clamp_fusion), kind=kCustom, calls=%fused_computation | custom fusion | bytes 8388672 | tf_op jit(solution)/shard_map/gather | solution.py:28
  91.3 3.6 %fusion.6 = bf16[2,512,256]{1,2,0:T(8,128)(2,1)S(1)} fusion(bf16[2,8,256,256]{3,2,1,0:T(8,128)(2,1)S(1)} %copy-done, bf16[2,8,256,512]{3,2,1,0:T(8,128)(2,1)} %bitcast.54, f32[2,256]{1,0:T(2,128)S(1)} %mul.36), kind=kOutput, calls=%fused_computation.10 | convolution fusion | flops 1074266112 | bytes 6817792 | tf_op jit(solution)/shard_map/btij,btjf->bif/dot_general | solution.py:30
  95.7 2.0 convolution_add_fusion
  97.8 7.9 %reduce-scatter.4.cloned.1.call-done = f32[512,512]{1,0:T(8,128)} async-done(((f32[512,1024]{1,0:T(8,128)}), f32[512,512]{1,0:T(8,128)}) %reduce-scatter.4.cloned.1.call-update) | async-done | bytes 1048592 | tf_op jit(solution)/shard_map/reduce_scatter | solution.py:35
  105.8 2.7 multiply_convert_fusion.1
  108.5 10.3 %all-gather.5.cloned.1.call-done = bf16[512,1024]{1,0:T(8,128)(2,1)} async-done(((bf16[512,512]{1,0:T(8,128)(2,1)}), bf16[512,1024]{1,0:T(8,128)(2,1)}) %all-gather.5.cloned.1.call-update) | async-done | bytes 1048592 | tf_op jit(solution)/shard_map/all_gather | solution.py:41
  118.9 3.3 %convolution_bitcast_fusion = f32[512,1024]{0,1:T(8,128)} fusion(bf16[512,1024]{1,0:T(8,128)(2,1)} %all-gather.5.cloned.1.call-done, bf16[512,512]{1,0:T(8,128)(2,1)S(1)} %copy-done.2), kind=kOutput, calls=%fused_computation.4 | convolution fusion | flops 536870912 | bytes 3670016 | tf_op jit(solution)/shard_map/dot_general | solution.py:46
  123.4 3.0 fusion.30
  126.4 2.5 copy.37
  128.9 4.5 %fusion.9 = bf16[2,512,8,256]{3,1,2,0:T(8,128)(2,1)} fusion(bf16[2,8,256,256]{3,2,1,0:T(8,128)(2,1)S(1)} %copy-done, f32[2,256,512]{1,2,0:T(8,128)} %copy.37, f32[2,256]{1,0:T(2,128)S(1)} %mul.36), kind=kOutput, calls=%fused_computation.17 | convolution fusion | flops 1074266112 | bytes 7342080 | tf_op jit(solution)/shard_map/btij,bif->btjf/dot_general | solution.py:55
  133.4 7.9 %copy.38 = bf16[16,256,512]{2,0,1:T(8,128)(2,1)} copy(bf16[16,256,512]{1,2,0:T(8,128)(2,1)} %bitcast.52) | data formatting | bytes 8388608 | tf_op jit(solution)/shard_map/reshape | solution.py:57
  141.3 2.9 convolution_convert_fusion
  144.2 2.0 copy.41
  146.3 5.9 %all-to-all-start = ((bf16[8,256,512]{2,1,0:T(8,128)(2,1)}), bf16[8,256,512]{2,1,0:T(8,128)(2,1)}, u32[]{:S(2)}, u32[]{:S(2)}) async-start(bf16[8,256,512]{2,1,0:T(8,128)(2,1)} %copy.41), calls=%async_computation.1 | async-start | bytes 4194304 | tf_op jit(solution)/shard_map/all_to_all | solution.py:60
  152.4 3.1 %fusion.31 = f32[512,1024]{1,0:T(8,128)} fusion(bf16[512,512]{1,0:T(8,128)(2,1)} %bitcast.56, bf16[512,1024]{1,0:T(8,128)(2,1)S(1)} %copy-done.3), kind=kOutput, calls=%fused_computation.50 | convolution fusion | flops 536870912 | bytes 3670016 | tf_op jit(solution)/shard_map/dot_general | solution.py:47
  155.9 4.1 %fusion.17 = f32[2,256,512]{2,0,1:T(2,128)} fusion(bf16[16,256,512]{2,0,1:T(8,128)(2,1)} %copy.38, pred[16]{0:T(512)(128)(4,1)S(1)} %get-tuple-element.21, s32[16]{0:T(128)S(1)} %eq.56, s32[2]{0:T(128)S(1)} %iota_add_fusion), kind=kOutput, calls=%fused_computation.28 | convolution fusion | flops 8388672 | bytes 5242968 | tf_op jit(solution)/shard_map/bs,srf->brf/dot_general | solution.py:63
  160.0 41.4 %all-to-all-done = bf16[8,256,512]{2,1,0:T(8,128)(2,1)} async-done(((bf16[8,256,512]{2,1,0:T(8,128)(2,1)}), bf16[8,256,512]{2,1,0:T(8,128)(2,1)}, u32[]{:S(2)}, u32[]{:S(2)}) %all-to-all-start) | async-done | bytes 2097184 | tf_op jit(solution)/shard_map/all_to_all | solution.py:60
  201.4 3.4 %fusion.2 = f32[2,256,512]{2,0,1:T(2,128)S(1)} fusion(f32[2,256,512]{2,0,1:T(2,128)} %fusion.17, bf16[8,256,512]{2,1,0:T(8,128)(2,1)} %all-to-all-done, pred[8,2]{0,1:T(4,128)(4,1)S(1)} %compare_reduce_fusion, pred[8]{0:T(512)(128)(4,1)S(1)} %iota_compare_fusion.1), kind=kOutput, calls=%fused_computation.6 | convolution fusion | flops 4456464 | bytes 4194328 | tf_op jit(solution)/shard_map/nb,nrf->brf/dot_general | solution.py:61
  206.0 1.6 fusion.7
  207.6 14.2 %reduce-scatter.6.cloned.1.call-done = f32[512,128]{0,1:T(8,128)} async-done(((f32[512,1024]{0,1:T(8,128)}), f32[512,128]{0,1:T(8,128)}) %reduce-scatter.6.cloned.1.call-update) | async-done | bytes 262160 | tf_op jit(solution)/shard_map/reduce_scatter | solution.py:51
  221.8 1.8 copy.44
  223.6 70.0 %reduce-scatter.8.cloned.1.call-done = f32[512,128]{1,0:T(8,128)} async-done(((f32[512,1024]{1,0:T(8,128)}), f32[512,128]{1,0:T(8,128)}) %reduce-scatter.8.cloned.1.call-update) | async-done | bytes 262160 | tf_op jit(solution)/shard_map/reduce_scatter | solution.py:52
  (43 shorter events, 6.4 us)
Async XLA Ops:
  7.2 84.1 %copy-start = (bf16[2,8,256,256]{3,2,1,0:T(8,128)(2,1)S(1)}, bf16[2,8,256,256]{3,2,1,0:T(8,128)(2,1)}, u32[]{:S(2)}) copy-start(bf16[2,8,256,256]{3,2,1,0:T(8,128)(2,1)} %param.9) | copy-start | bytes 6291460
  7.2 79.1 %all-gather.3.cloned.1.call-start = ((), (), s32[]{:S(2)}) async-start(), calls=%async_computation.4 | async-start | bytes 4718592 | tf_op jit(solution)/shard_map/all_gather | solution.py:27
  7.9 97.9 %reduce-scatter.4.cloned.1.call-start = ((), (), s32[]{:S(2)}) async-start(), calls=%async_computation.5 | async-start | bytes 3145728 | tf_op jit(solution)/shard_map/reduce_scatter | solution.py:35
  91.3 4.4 %copy-start.1 = (f32[512,1024]{1,0:T(8,128)S(1)}, f32[512,1024]{1,0:T(8,128)}, u32[]{:S(2)}) copy-start(f32[512,1024]{1,0:T(8,128)} %fusion.29) | copy-start | bytes 6291460
  91.3 4.4 %copy-start.6 = (bf16[512,1024]{1,0:T(8,128)(2,1)S(1)}, bf16[512,1024]{1,0:T(8,128)(2,1)}, u32[]{:S(2)}) copy-start(bf16[512,1024]{1,0:T(8,128)(2,1)} %param.12) | copy-start | bytes 3145732
  94.9 0.8 copy-start.4
  97.7 8.0 %copy-start.7 = (bf16[512,512]{1,0:T(8,128)(2,1)S(1)}, bf16[512,512]{1,0:T(8,128)(2,1)}, u32[]{:S(2)}) copy-start(bf16[512,512]{1,0:T(8,128)(2,1)} %param.13) | copy-start | bytes 1572868
  97.8 21.1 %copy-start.2 = (bf16[512,512]{1,0:T(8,128)(2,1)S(1)}, bf16[512,512]{1,0:T(8,128)(2,1)}, u32[]{:S(2)}) copy-start(bf16[512,512]{1,0:T(8,128)(2,1)} %param.7) | copy-start | bytes 1572868
  97.8 21.1 %all-gather.5.cloned.1.call-start = ((), (), s32[]{:S(2)}) async-start(), calls=%async_computation.6 | async-start | bytes 1572864 | tf_op jit(solution)/shard_map/all_gather | solution.py:41
  108.5 113.3 %reduce-scatter.6.cloned.1.call-start = ((), (), s32[]{:S(2)}) async-start(), calls=%async_computation.7 | async-start | bytes 2359296 | tf_op jit(solution)/shard_map/reduce_scatter | solution.py:51
  122.2 1.2 copy-start.3
  146.3 55.1 %all-to-all-start = ((bf16[8,256,512]{2,1,0:T(8,128)(2,1)}), bf16[8,256,512]{2,1,0:T(8,128)(2,1)}, u32[]{:S(2)}, u32[]{:S(2)}) async-start(bf16[8,256,512]{2,1,0:T(8,128)(2,1)} %copy.41), calls=%async_computation.1 | async-start | bytes 4194304 | tf_op jit(solution)/shard_map/all_to_all | solution.py:60
  152.1 3.4 %copy-start.8 = (s32[16,8]{0,1:T(8,128)S(1)}, s32[16,8]{0,1:T(8,128)}, u32[]{:S(2)}) copy-start(s32[16,8]{0,1:T(8,128)} %param.8) | copy-start | bytes 1540
  152.1 141.5 %reduce-scatter.8.cloned.1.call-start = ((), (), s32[]{:S(2)}) async-start(), calls=%async_computation.8 | async-start | bytes 2359296 | tf_op jit(solution)/shard_map/reduce_scatter | solution.py:52
  204.8 1.2 copy-start.5
Sparse Core Ops, SparseCore 0:
  10.1 76.0 all-gather.2
  97.9 7.8 reduce-scatter.3
  108.6 10.2 all-gather.4
  122.7 99.0 reduce-scatter.5
  226.2 67.3 reduce-scatter.7
where the time goes:
time: 301 us; the launch traced here: 300 us
  waiting for transfers between devices  218 us (72%)
  matrix products  35 us (12%)
  local copies, waits for them, and re-layouts  23.6 us (8%)
  between operations  13.9 us (5%)
  starting transfers between devices  6.25 us (2%)
  other arithmetic  3.6 us (1%)
    all_gather x1, waiting for transfers between devices, on_device(): whole = lax.all_gather(features, 'node', axis=0, tiled=True)  73.2 us
    reduce_scatter x1, waiting for transfers between devices, on_device(): lax.psum_scatter(neigh_term, 'node', scatter_dimension=1, tiled=True)  70 us
    all_to_all x1, waiting for transfers between devices, on_device(): lax.all_to_all(outgoing_back, 'node', split_axis=0, concat_axis=0, tiled=...  41.4 us
    reduce_scatter x1, waiting for transfers between devices, on_device(): lax.psum_scatter(self_term, 'node', scatter_dimension=1, tiled=True)  14.2 us
    all_gather x1, waiting for transfers between devices, on_device(): slope = lax.all_gather(slope_half, 'feat', axis=1, tiled=True)  10.3 us
    reduce_scatter x1, waiting for transfers between devices, on_device(): lax.psum_scatter(partial_sum, 'feat', scatter_dimension=1, tiled=True)  7.94 us
    reshape x1, local copies, waits for them, and re-layouts, on_device(): pieces = jnp.einsum('btij,bif->btjf', tile_values, scaled, preferred_elem...  7.93 us
  transfers between devices with their start and end apart: 6, of which 6 were waited for; matrix products, arithmetic and copies ran while one was open for 14% of the time, Pallas kernels for 0%

commit v1 on v0

v1 whole, which is shorter than its diff:
```python
import functools

import jax
import jax.numpy as jnp
from jax import lax
from jax.experimental import pallas as pl
from jax.experimental.pallas import tpu as pltpu
from jax.sharding import PartitionSpec as P

TILE = 256
TPR = 8
BF16, F32 = jnp.bfloat16, jnp.float32
SMEM = pl.BlockSpec(memory_space=pltpu.SMEM)
VMEM = pl.BlockSpec(memory_space=pltpu.VMEM)
ROWS_BY_COLS = (((1,), (0,)), ((), ()))
COLS_BY_COLS = (((1,), (1,)), ((), ()))


def mul(a, b, dims=ROWS_BY_COLS):
    return lax.dot_general(a, b, dims, preferred_element_type=F32)


def block(index):
    return pl.ds(pl.multiple_of(index * TILE, TILE), TILE)


def local_call(kernel, outs, ins, flops, scratch=(), scalars=1):
    moved = sum(a.size * a.dtype.itemsize for a in ins)
    moved += sum(o.size * o.dtype.itemsize for o in outs)
    return pl.pallas_call(
        kernel,
        out_shape=outs,
        in_specs=[SMEM] * scalars + [VMEM] * (len(ins) - scalars),
        out_specs=[VMEM] * len(outs),
        scratch_shapes=list(scratch),
        compiler_params=pltpu.CompilerParams(vmem_limit_bytes=44 * 1024 * 1024),
        cost_estimate=pl.CostEstimate(flops=flops, bytes_accessed=moved, transcendentals=0),
    )(*ins)


def combine(code, tiles, first, count):
    own_blocks = tiles.shape[0]
    rows = own_blocks * TILE

    def kernel(code_ref, tiles_ref, out_ref, flipped_ref, total):
        source = pl.program_id(0) + first
        for r in range(own_blocks):
            total[...] = jnp.zeros_like(total)
            for t in range(TPR):

                @pl.when(code_ref[r * TPR + t] == source)
                def _():
                    total[...] += tiles_ref[r, t].astype(F32)

            whole = total[...]
            out_ref[0, r * TILE : (r + 1) * TILE, :] = whole.astype(BF16)
            flipped_ref[0, :, r * TILE : (r + 1) * TILE] = whole.T.astype(BF16)

    return pl.pallas_call(
        kernel,
        grid=(count,),
        out_shape=[
            jax.ShapeDtypeStruct((count, rows, TILE), BF16),
            jax.ShapeDtypeStruct((count, TILE, rows), BF16),
        ],
        in_specs=[SMEM, pl.BlockSpec(tiles.shape, lambda j: (0, 0, 0, 0))],
        out_specs=[
            pl.BlockSpec((1, rows, TILE), lambda j: (j, 0, 0)),
            pl.BlockSpec((1, TILE, rows), lambda j: (j, 0, 0)),
        ],
        scratch_shapes=[pltpu.VMEM((TILE, TILE), F32)],
        compiler_params=pltpu.CompilerParams(vmem_limit_bytes=32 * 1024 * 1024),
        cost_estimate=pl.CostEstimate(
            flops=0, bytes_accessed=2 * tiles.size + 4 * count * rows * TILE, transcendentals=0
        ),
    )(code, tiles)


def early_kernel(info, matrix, own, partner, *rest):
    *direct, out = rest
    count = len(direct)
    total = mul(matrix[0], own[:TILE]) + mul(matrix[1], own[TILE:])
    for k in range(count):
        total += mul(matrix[2 + k], direct[k][...])
    out[...] = total + mul(matrix[2 + count], partner[block(info[2, count + 1]), :])


def late_kernel(info, matrix, early, inverse, *rest):
    *passed, out, away = rest
    total = early[...]
    for k, piece in enumerate(passed):
        total += mul(matrix[k], piece[...])
    out[...] = (total * inverse[...]).astype(BF16)
    away[...] = out[block(1 - info[3, 0]), :]


def slope_kernel(info, self_part, agg, agg_in, w_own, w_other, cot_own, cot_in, slope, keep, away, cot, hid):
    feat = info[3, 0]
    width = cot_own.shape[1]
    mine = pl.ds(pl.multiple_of(feat * width, width), width)
    other = pl.ds(pl.multiple_of((1 - feat) * width, width), width)
    cot[:, mine] = cot_own[...]
    cot[:, other] = cot_in[...]
    own_rows = agg[block(feat), :]
    step = 256
    for c in range(0, slope.shape[1], step):
        cols = slice(c, c + step)
        pre = self_part[:, cols] + mul(own_rows, w_own[:, cols]) + mul(agg_in[...], w_other[:, cols])
        s = jax.nn.sigmoid(pre)
        hid[:, cols] = (pre * s).astype(BF16)
        slope[:, cols] = (cot[:, cols].astype(F32) * s * (1.0 + pre * (1.0 - s))).astype(BF16)
    keep[...] = hid[:, mine]
    away[...] = hid[:, other]


def pieces_kernel(count, info, slope_own, slope_in, w_neigh, inverse, early, late, slope, scaled, partner, *outs):
    feat = info[3, 0]
    slope[block(feat), :] = slope_own[...]
    slope[block(1 - feat), :] = slope_in[...]
    scaled[...] = (mul(slope[...], w_neigh[...], COLS_BY_COLS) * inverse[...]).astype(BF16)
    for k in range(count):
        outs[k][...] = mul(late[k], scaled[...]).astype(BF16)
    for k in range(count):
        outs[count + k][...] = mul(early[2 + k], scaled[...]).astype(BF16)
    partner[...] = mul(early[2 + count], scaled[...])


def terms_kernel(info, slope, features_t, agg_t, keep, away):
    node = info[3, 1]
    low = node % 2
    high = node // 2
    width = keep.shape[3]
    for which, left in enumerate((features_t, agg_t)):
        for p in range(keep.shape[0]):
            both = mul(left[...], slope[:, 2 * p * width : 2 * (p + 1) * width])
            a, b = both[:, :width], both[:, width:]
            at = jnp.bitwise_xor(high, p)
            keep[at, which] = jnp.where(low == 0, a, b)
            away[at, which] = jnp.where(low == 0, b, a).astype(BF16)


def base_kernel(info, slope, w_self, scaled, early, out):
    back = mul(slope[...], w_self[...], COLS_BY_COLS)
    for b in range(2):
        rows = slice(b * TILE, (b + 1) * TILE)
        out[rows, :] = back[rows] + mul(early[b], scaled[...])


def partner_kernel(info, own, *rest):
    *passed, out, total = rest
    total[...] = jnp.zeros_like(total)
    total[block(info[2, len(passed) + 1]), :] = own[...]
    for k, piece in enumerate(passed):
        total[block(info[1, k + 1]), :] += piece[...].astype(F32)
    out[...] = total[...].astype(BF16)


def final_kernel(info, base, partner, *rest):
    *direct, out, total = rest
    total[...] = base[...] + partner[...].astype(F32)
    for k, piece in enumerate(direct):
        total[block(info[0, k + 1]), :] += piece[...].astype(F32)
    out[...] = total[...].astype(BF16)


def on_device(features, tile_list, tile_values, degree, w_self, w_neigh, cotangent):
    nodes = lax.axis_size("node")
    me = lax.axis_index("node")
    feat = lax.axis_index("feat")
    own_rows, width = features.shape
    hidden_width = w_self.shape[1]
    own_blocks = own_rows // TILE
    slots = own_blocks * TPR
    across = nodes // 2
    near = range(1, across)

    def swap(x):
        return lax.ppermute(x, "feat", [(0, 1), (1, 0)])

    def hop(x, k):
        return lax.ppermute(x, "node", [(i, i ^ k) for i in range(nodes)])

    def halves(x):
        a, b = x[:TILE], x[TILE:]
        first = feat == 0
        return jnp.where(first, a, b), jnp.where(first, b, a)

    shape = jax.ShapeDtypeStruct

    ids = jnp.arange(nodes, dtype=jnp.int32)
    everyone = tile_list.reshape(1, nodes, slots)
    at = (ids ^ me)[:, None, None]
    that = ids[None, :, None] == at
    this = ids[None, :, None] == me
    far = me ^ across
    def seen(mask):
        return jnp.any(mask, axis=(1, 2)).astype(jnp.int32)
    info = jnp.stack(
        [
            seen(that & (everyone == 2 * me + 1)),
            seen(that & (everyone == 2 * far + 1)),
            seen(this & (everyone == 2 * at + 1)),
            jnp.where(ids == 0, feat, me).astype(jnp.int32),
        ]
    )

    partner = hop(features, across)
    direct = [hop(lax.dynamic_slice_in_dim(features, info[0, k] * TILE, TILE, 0), k) for k in near]

    mine = lax.dynamic_slice_in_dim(tile_list, me * own_blocks, own_blocks, 0).reshape(slots)
    owner = mine // own_blocks
    code = jnp.where(owner == me, mine % own_blocks, 1 + (owner ^ me))
    early, early_t = combine(code, tile_values, 0, across + 2)
    late, late_t = combine(code, tile_values, across + 2, across - 1)
    inverse = (1.0 / degree.astype(F32)).reshape(own_rows, 1)

    rows_own, rows_away = halves(features)
    cot_own, cot_away = halves(cotangent)
    rows_in, cot_in = swap(rows_away), swap(cot_away)
    w_self_in, w_neigh_in = swap(w_self), swap(w_neigh)
    self_part = mul(rows_own, w_self) + mul(rows_in, w_self_in)
    features_t = features.T

    passed = [hop(lax.dynamic_slice_in_dim(partner, info[1, k] * TILE, TILE, 0), k) for k in near]
    tile_flops = 2 * own_rows * TILE * width
    (summed,) = local_call(
        early_kernel,
        [shape((own_rows, width), F32)],
        [info, early, features, partner, *direct],
        (across + 2) * tile_flops,
    )
    agg, agg_away = local_call(
        late_kernel,
        [shape((own_rows, width), BF16), shape((TILE, width), BF16)],
        [info, late, summed, inverse, *passed],
        across * tile_flops,
    )
    agg_in = swap(agg_away)
    agg_t = agg.T
    slope_own, hid_keep, hid_away = local_call(
        slope_kernel,
        [shape((TILE, hidden_width), BF16), shape((TILE, width), BF16), shape((TILE, width), BF16)],
        [info, self_part, agg, agg_in, w_neigh, w_neigh_in, cot_own, cot_in],
        4 * TILE * width * hidden_width,
        [pltpu.VMEM((TILE, hidden_width), BF16)] * 2,
    )
    slope_in = swap(slope_own)
    hid_in = swap(hid_away)
    hidden = jnp.where(feat == 0, jnp.concatenate([hid_keep, hid_in]), jnp.concatenate([hid_in, hid_keep]))

    count = across - 1
    piece = shape((TILE, width), BF16)
    slope, scaled, own_piece, *pieces = local_call(
        functools.partial(pieces_kernel, count),
        [shape((own_rows, hidden_width), BF16), shape((own_rows, width), BF16), shape((TILE, width), F32)]
        + [piece] * (2 * count),
        [info, slope_own, slope_in, w_neigh, inverse, early_t, late_t],
        2 * own_rows * hidden_width * width + (nodes - 1) * tile_flops,
    )
    back_passed = [hop(pieces[k - 1], k) for k in near]
    back_direct = [hop(pieces[count + k - 1], k) for k in near]

    columns = hidden_width // nodes
    if columns % 128 == 0:
        groups = nodes // 2
        keep, away = local_call(
            terms_kernel,
            [shape((groups, 2, width, columns), F32), shape((groups, 2, width, columns), BF16)],
            [info, slope, features_t, agg_t],
            4 * own_rows * width * hidden_width,
        )
        bit = 1
        while True:
            keep = keep + hop(away, bit).astype(F32)
            bit *= 2
            if bit == nodes:
                break
            keep, away = keep[0::2], keep[1::2].astype(BF16)
        grad_self, grad_neigh = keep[0, 0], keep[0, 1]
    else:
        grad_self, grad_neigh = (
            lax.psum_scatter(mul(left, slope), "node", scatter_dimension=1, tiled=True)
            for left in (features_t, agg_t)
        )

    (base,) = local_call(
        base_kernel,
        [shape((own_rows, width), F32)],
        [info, slope, w_self, scaled, early_t],
        2 * own_rows * hidden_width * width + 2 * tile_flops,
    )
    (to_partner,) = local_call(
        partner_kernel,
        [shape((own_rows, width), BF16)],
        [info, own_piece, *back_passed],
        0,
        [pltpu.VMEM((own_rows, width), F32)],
    )
    from_partner = hop(to_partner, across)
    (grad_features,) = local_call(
        final_kernel,
        [shape((own_rows, width), BF16)],
        [info, base, from_partner, *back_direct],
        0,
        [pltpu.VMEM((own_rows, width), F32)],
    )
    return (hidden, grad_features, grad_self, grad_neigh)


def solution(mesh):
    return jax.shard_map(
        on_device,
        mesh=mesh,
        in_specs=(
            P(("groups", "node"), "feat"),
            P("groups", None),
            P(("groups", "node"), None, None, None),
            P(("groups", "node")),
            P("feat", None),
            P("feat", None),
            P(("groups", "node"), "feat"),
        ),
        out_specs=(
            P(("groups", "node"), "feat"),
            P(("groups", "node"), "feat"),
            P(("groups", "feat"), "node"),
            P(("groups", "feat"), "node"),
        ),
        check_vma=False,
    )
```

time: 301 us -> 166 us (0.55)
  waiting for transfers between devices: 218 us -> 87.6 us
  matrix products: 35 us -> 3.19 us
  starting transfers between devices: 6.25 us -> 26.8 us
  Pallas kernels: 0 us -> 20.5 us
  between operations: 13.9 us -> 4.82 us
  local copies, waits for them, and re-layouts: 23.6 us -> 15.5 us
  other arithmetic: 3.6 us -> 6.61 us
    reduce_scatter x3 -> x0, waiting for transfers between devices: 92.1 us -> none  [the longest x1 70 us: on_device(): lax.psum_scatter(neigh_term, 'node', scatter_dimension=1, tiled=True)]
    ppermute x0 -> x24, waiting for transfers between devices: none -> 87.6 us  [the longest x17 86.8 us: hop(): return lax.ppermute(x, 'node', [(i, i ^ k) for i in range(nodes)])]
    all_gather x2 -> x0, waiting for transfers between devices: 83.5 us -> none  [the longest x1 73.2 us: on_device(): whole = lax.all_gather(features, 'node', axis=0, tiled=True)]
    all_to_all x1 -> x0, waiting for transfers between devices: 41.4 us -> none  [on_device(): lax.all_to_all(outgoing_back, 'node', split_axis=0, concat_axis=0, tiled=...]
    dot_general x11 -> x2, matrix products: 35 us -> 3.19 us  [mul(): return lax.dot_general(a, b, dims, preferred_element_type=F32)]
    ppermute x0 -> x24, starting transfers between devices: none -> 26.8 us  [the longest x17 25.2 us: hop(): return lax.ppermute(x, 'node', [(i, i ^ k) for i in range(nodes)])]
    pallas_call x0 -> x10, Pallas kernels: none -> 20.5 us  [the longest x8 16 us: local_call(): pl.pallas_call(kernel, out_shape=outs, in_specs=[SMEM] * scalars + [VMEM]...]
    reshape x3, local copies, waits for them, and re-layouts: 10.6 us -> 0.3 us  [the longest x1 0.14 us: on_device(): inverse = (1.0 / degree.astype(F32)).reshape(own_rows, 1)]
  transfers between devices with their start and end apart: 6 -> 24, of which waited for: 6 -> 12; matrix products, arithmetic and copies ran while one was open for 14% -> 8% of each run, Pallas kernels for 0% -> 8%
where the time goes in v1:
time: 166 us; the launch traced here: 165 us
  waiting for transfers between devices  87.6 us (53%)
  starting transfers between devices  26.8 us (16%)
  Pallas kernels  20.5 us (12%)
  local copies, waits for them, and re-layouts  15.5 us (9%)
  other arithmetic  6.61 us (4%)
  between operations  4.82 us (3%)
  matrix products  3.19 us (2%)
    ppermute x17, waiting for transfers between devices, hop(): return lax.ppermute(x, 'node', [(i, i ^ k) for i in range(nodes)])  86.8 us
    ppermute x17, starting transfers between devices, hop(): return lax.ppermute(x, 'node', [(i, i ^ k) for i in range(nodes)])  25.2 us
    pallas_call x8, Pallas kernels, local_call(): pl.pallas_call(kernel, out_shape=outs, in_specs=[SMEM] * scalars + [VMEM]...  16 us
    unnamed x54, local copies, waits for them, and re-layouts  11.1 us
    pallas_call x2, Pallas kernels, combine(): pl.pallas_call(kernel, grid=(count,), out_shape=[jax.ShapeDtypeStruct((co...  4.53 us
  transfers between devices with their start and end apart: 24, of which 12 were waited for; matrix products, arithmetic and copies ran while one was open for 8% of the time, Pallas kernels for 8%

profile of v1, /device:TPU:0, one launch (start us, length us, event | category | flops | bytes accessed | tf_op | source)
XLA Modules:
  0.0 165.0 jit_solution(10017648099284497252)
XLA Ops:
  1.2 3.7 %collective-permute-start.2 = (bf16[512,512]{1,0:T(8,128)(2,1)}, bf16[512,512]{1,0:T(8,128)(2,1)S(1)}, u32[]{:S(2)}, u32[]{:S(2)}) collective-permute-start(bf16[512,512]{1,0:T(8,128)(2,1)} %own.1), channel_id=1, source_target_pairs={{0,8},{2,10},{4,12},{6,14},{8,0},{10,2},{12,4},{14,6},{1,9},{3,11}... | collective-permute-start | bytes 1572872 | tf_op jit(solution)/shard_map/ppermute | solution.py:181
  8.8 2.4 %constant_dynamic-slice_fusion.3 = (bf16[256,512]{1,0:T(8,128)(2,1)}, bf16[256,512]{1,0:T(8,128)(2,1)}, bf16[256,512]{1,0:T(8,128)(2,1)}, bf16[256,512]{1,0:T(8,128)(2,1)}) fusion(bf16[512,512]{1,0:T(8,128)(2,1)} %own.1, s32[]{:T(128)S(6)} %select_n.86, s32[]{:T(128)S(6)} %select_n.85, s32[]{:T(128)S(6)} %select_n.84, pred[]{:T(512)S(6)} %eq.85), kind=kLoop, calls=%fused_computation.31 | loop fusion | flops 131072 | bytes 2359309 | tf_op jit(solution)/shard_map/dynamic_slice | solution.py:208
  19.2 9.7 %collective-permute-done.2.partner = bf16[512,512]{1,0:T(8,128)(2,1)S(1)} collective-permute-done((bf16[512,512]{1,0:T(8,128)(2,1)}, bf16[512,512]{1,0:T(8,128)(2,1)S(1)}, u32[]{:S(2)}, u32[]{:S(2)}) %collective-permute-start.2) | collective-permute-done | bytes 524320 | tf_op jit(solution)/shard_map/ppermute | solution.py:181
  31.4 1.9 %broadcast_select_fusion = (bf16[256,512]{1,0:T(8,128)(2,1)}, bf16[256,512]{1,0:T(8,128)(2,1)}) fusion(pred[]{:T(512)S(6)} %eq.85, bf16[512,512]{1,0:T(8,128)(2,1)} %param.13), kind=kLoop, calls=%fused_computation.10 | loop fusion | flops 262144 | bytes 1048577 | tf_op jit(solution)/shard_map/jit(_where)/select_n | solution.py:186
  33.4 3.5 %collective-permute-done.5.rest_2_ = bf16[256,512]{1,0:T(8,128)(2,1)} collective-permute-done((bf16[256,512]{1,0:T(8,128)(2,1)}, bf16[256,512]{1,0:T(8,128)(2,1)}, u32[]{:S(2)}, u32[]{:S(2)}) %collective-permute-start.5) | collective-permute-done | bytes 262176 | tf_op jit(solution)/shard_map/ppermute | solution.py:181
  36.9 5.4 %collective-permute-done.6.rest_0_ = bf16[256,512]{1,0:T(8,128)(2,1)S(1)} collective-permute-done((bf16[256,512]{1,0:T(8,128)(2,1)S(1)}, bf16[256,512]{1,0:T(8,128)(2,1)S(1)}, u32[]{:S(2)}, u32[]{:S(2)}) %collective-permute-start.6) | collective-permute-done | bytes 262176 | tf_op jit(solution)/shard_map/ppermute | solution.py:181
  46.6 2.9 %shard_map.103 = (bf16[6,512,256]{2,1,0:T(8,128)(2,1)S(1)}, bf16[6,256,512]{2,1,0:T(8,128)(2,1)S(1)}) custom-call(s32[16]{0:T(128)S(1)} %compare_select_fusion.code_ref, bf16[2,8,256,256]{3,2,1,0:T(8,128)(2,1)S(1)} %copy-done.1), custom_call_target="tpu_custom_call" | custom-call | bytes 5242880 | tf_op jit(solution)/shard_map/pallas_call | solution.py:59
  53.4 2.1 %shard_map.104.early = f32[512,512]{1,0:T(8,128)S(1)} custom-call(s32[4,8]{1,0:T(4,128)S(1)} %pad_add_fusion.info, bf16[6,512,256]{2,1,0:T(8,128)(2,1)S(1)} %copy-done.7, bf16[512,512]{1,0:T(8,128)(2,1)S(1)} %copy-done, bf16[512,512]{1,0:T(8,128)(2,1)S(1)} %collective-permute-done.2.partner, bf16[256,512]{1,0:T(8,128)(2,1)S(1)} %collective-permute-done.3.rest_0_, ...), custom_call_target="tpu_custom_call" | custom-call | flops 805306368 | bytes 4456576 | tf_op jit(solution)/shard_map/pallas_call | solution.py:30
  57.8 1.8 %convolution_add_fusion.self_part = f32[256,1024]{1,0:T(8,128)S(1)} fusion(f32[256,1024]{1,0:T(8,128)S(1)} %copy-done.22, bf16[256,512]{1,0:T(8,128)(2,1)} %collective-permute-done, bf16[512,1024]{1,0:T(8,128)(2,1)} %collective-permute-done.1), kind=kOutput, calls=%fused_computation.1 | convolution fusion | flops 268697600 | bytes 3407872 | tf_op jit(solution)/shard_map/dot_general | solution.py:20
  59.6 3.0 %shard_map.106 = (bf16[256,1024]{1,0:T(8,128)(2,1)}, bf16[256,512]{1,0:T(8,128)(2,1)S(1)}, bf16[256,512]{1,0:T(8,128)(2,1)S(1)}) custom-call(s32[4,8]{1,0:T(4,128)S(1)} %pad_add_fusion.info, f32[256,1024]{1,0:T(8,128)S(1)} %convolution_add_fusion.self_part, bf16[512,512]{1,0:T(8,128)(2,1)S(1)} %get-tuple-element.26.agg, ...), custom_call_target="tpu_custom_call" | custom-call | flops 536870912 | bytes 5505152 | tf_op jit(solution)/shard_map/pallas_call | solution.py:30
  68.7 3.0 %shard_map.107 = (bf16[512,1024]{1,0:T(8,128)(2,1)S(1)}, bf16[512,512]{1,0:T(8,128)(2,1)S(1)}, f32[256,512]{1,0:T(8,128)S(1)}, bf16[256,512]{1,0:T(8,128)(2,1)S(...) custom-call(s32[4,8]{1,0:T(4,128)S(1)} %pad_add_fusion.info, ...), custom_call_target="tpu_custom_call" | custom-call | flops 1476395008 | bytes 8128640 | tf_op jit(solution)/shard_map/pallas_call | solution.py:30
  71.8 2.0 %shard_map.111 = (f32[4,2,512,128]{3,2,1,0:T(8,128)S(1)}, bf16[4,2,512,128]{3,2,1,0:T(8,128)(2,1)S(1)}) custom-call(s32[4,8]{1,0:T(4,128)S(1)} %pad_add_fusion.info, bf16[512,1024]{1,0:T(8,128)(2,1)S(1)} %get-tuple-element.33.slope, bf16[512,512]{1,0:T(8,128)(2,1)S(1)} %bitcast.22, bf16[512,512]{1,0:T(8,128)(2,1)S(1)} %bitcast.23), custom_call_target="tpu_custom_call" | custom-call | flops 1073741824 | bytes 5243008 | tf_op jit(solution)/shard_map/pallas_call | solution.py:30
  75.3 23.9 %collective-permute-done.21 = bf16[4,2,512,128]{3,2,1,0:T(8,128)(2,1)S(1)} collective-permute-done((bf16[4,2,512,128]{3,2,1,0:T(8,128)(2,1)S(1)}, bf16[4,2,512,128]{3,2,1,0:T(8,128)(2,1)S(1)}, u32[]{:S(2)}, u32[]{:S(2)}) %collective-permute-start.21) | collective-permute-done | bytes 1048608 | tf_op jit(solution)/shard_map/ppermute | solution.py:181
  99.5 2.9 %collective-permute-start.22 = (bf16[2,2,512,128]{3,2,1,0:T(8,128)(2,1)S(1)}, bf16[2,2,512,128]{3,2,1,0:T(8,128)(2,1)S(1)}, u32[]{:S(2)}, u32[]{:S(2)}) collective-permute-start(bf16[2,2,512,128]{3,2,1,0:T(8,128)(2,1)S(1)} %slice.63), channel_id=1, source_target_pairs={{0,4},{2,6},{4,0},{6,2},{8,12},{10,14},{12,8},{14,10},{1,5},{3,7},... | collective-permute-start | bytes 1572872 | tf_op jit(solution)/shard_map/ppermute | solution.py:181
  103.1 2.8 %collective-permute-start.16 = (bf16[256,512]{1,0:T(8,128)(2,1)S(1)}, bf16[256,512]{1,0:T(8,128)(2,1)S(1)}, u32[]{:S(2)}, u32[]{:S(2)}) collective-permute-start(bf16[256,512]{1,0:T(8,128)(2,1)S(1)} %get-tuple-element.38), channel_id=1, source_target_pairs={{0,6},{2,4},{4,2},{6,0},{8,14},{10,12},{12,10},{14,8},{1,7},{3,5},... | collective-permute-start | bytes 786440 | tf_op jit(solution)/shard_map/ppermute | solution.py:181
  105.9 3.8 %collective-permute-done.14.rest_0_ = bf16[256,512]{1,0:T(8,128)(2,1)S(1)} collective-permute-done((bf16[256,512]{1,0:T(8,128)(2,1)S(1)}, bf16[256,512]{1,0:T(8,128)(2,1)S(1)}, u32[]{:S(2)}, u32[]{:S(2)}) %collective-permute-start.14) | collective-permute-done | bytes 262176 | tf_op jit(solution)/shard_map/ppermute | solution.py:181
  110.3 10.6 %collective-permute-done.15.rest_1_ = bf16[256,512]{1,0:T(8,128)(2,1)S(1)} collective-permute-done((bf16[256,512]{1,0:T(8,128)(2,1)S(1)}, bf16[256,512]{1,0:T(8,128)(2,1)S(1)}, u32[]{:S(2)}, u32[]{:S(2)}) %collective-permute-start.15) | collective-permute-done | bytes 262176 | tf_op jit(solution)/shard_map/ppermute | solution.py:181
  120.9 2.0 %collective-permute-start.19 = (bf16[256,512]{1,0:T(8,128)(2,1)S(1)}, bf16[256,512]{1,0:T(8,128)(2,1)S(1)}, u32[]{:S(2)}, u32[]{:S(2)}) collective-permute-start(bf16[256,512]{1,0:T(8,128)(2,1)S(1)} %get-tuple-element.40), channel_id=1, source_target_pairs={{0,4},{2,6},{4,0},{6,2},{8,12},{10,14},{12,8},{14,10},{1,5},{3,7},... | collective-permute-start | bytes 786440 | tf_op jit(solution)/shard_map/ppermute | solution.py:181
  122.9 3.7 %collective-permute-done.16.rest_2_ = bf16[256,512]{1,0:T(8,128)(2,1)S(1)} collective-permute-done((bf16[256,512]{1,0:T(8,128)(2,1)S(1)}, bf16[256,512]{1,0:T(8,128)(2,1)S(1)}, u32[]{:S(2)}, u32[]{:S(2)}) %collective-permute-start.16) | collective-permute-done | bytes 262176 | tf_op jit(solution)/shard_map/ppermute | solution.py:181
  126.6 2.8 %collective-permute-start.20 = (bf16[256,512]{1,0:T(8,128)(2,1)S(1)}, bf16[256,512]{1,0:T(8,128)(2,1)S(1)}, u32[]{:S(2)}, u32[]{:S(2)}) collective-permute-start(bf16[256,512]{1,0:T(8,128)(2,1)S(1)} %get-tuple-element.41), channel_id=1, source_target_pairs={{0,6},{2,4},{4,2},{6,0},{8,14},{10,12},{12,10},{14,8},{1,7},{3,5},... | collective-permute-start | bytes 786440 | tf_op jit(solution)/shard_map/ppermute | solution.py:181
  131.5 2.1 %collective-permute-start.23 = (bf16[1,2,512,128]{3,2,1,0:T(8,128)(2,1)S(1)}, bf16[1,2,512,128]{3,2,1,0:T(8,128)(2,1)S(1)}, u32[]{:S(2)}, u32[]{:S(2)}) collective-permute-start(bf16[1,2,512,128]{3,2,1,0:T(8,128)(2,1)S(1)} %slice.91), channel_id=1, source_target_pairs={{0,8},{2,10},{4,12},{6,14},{8,0},{10,2},{12,4},{14,6},{1,9},{3,11}... | collective-permute-start | bytes 786440 | tf_op jit(solution)/shard_map/ppermute | solution.py:181
  136.1 4.0 %collective-permute-done.19.rest_1_ = bf16[256,512]{1,0:T(8,128)(2,1)S(1)} collective-permute-done((bf16[256,512]{1,0:T(8,128)(2,1)S(1)}, bf16[256,512]{1,0:T(8,128)(2,1)S(1)}, u32[]{:S(2)}, u32[]{:S(2)}) %collective-permute-start.19) | collective-permute-done | bytes 262176 | tf_op jit(solution)/shard_map/ppermute | solution.py:181
  140.2 4.5 %collective-permute-done.20.rest_2_ = bf16[256,512]{1,0:T(8,128)(2,1)S(1)} collective-permute-done((bf16[256,512]{1,0:T(8,128)(2,1)S(1)}, bf16[256,512]{1,0:T(8,128)(2,1)S(1)}, u32[]{:S(2)}, u32[]{:S(2)}) %collective-permute-start.20) | collective-permute-done | bytes 262176 | tf_op jit(solution)/shard_map/ppermute | solution.py:181
  144.6 16.7 %collective-permute-done.17.partner = bf16[512,512]{1,0:T(8,128)(2,1)S(1)} collective-permute-done((bf16[512,512]{1,0:T(8,128)(2,1)S(1)}, bf16[512,512]{1,0:T(8,128)(2,1)S(1)}, u32[]{:S(2)}, u32[]{:S(2)}) %collective-permute-start.17) | collective-permute-done | bytes 524320 | tf_op jit(solution)/shard_map/ppermute | solution.py:181
  (121 shorter events, 39.2 us)
Async XLA Ops:
  0.7 57.2 %collective-permute-start.1 = (bf16[512,1024]{1,0:T(8,128)(2,1)}, bf16[512,1024]{1,0:T(8,128)(2,1)}, u32[]{:S(2)}, u32[]{:S(2)}) collective-permute-start(bf16[512,1024]{1,0:T(8,128)(2,1)} %w_self.1), channel_id=1, source_target_pairs={{0,1},{1,0},{2,3},{3,2},{4,5},{5,4},{6,7},{7,6},{8,9},{9,8},{10,11... | collective-permute-start | bytes 3145736 | tf_op jit(solution)/shard_map/ppermute | solution.py:178
  1.2 27.7 %collective-permute-start.2 = (bf16[512,512]{1,0:T(8,128)(2,1)}, bf16[512,512]{1,0:T(8,128)(2,1)S(1)}, u32[]{:S(2)}, u32[]{:S(2)}) collective-permute-start(bf16[512,512]{1,0:T(8,128)(2,1)} %own.1), channel_id=1, source_target_pairs={{0,8},{2,10},{4,12},{6,14},{8,0},{10,2},{12,4},{14,6},{1,9},{3,11}... | collective-permute-start | bytes 1572872 | tf_op jit(solution)/shard_map/ppermute | solution.py:181
  11.2 18.6 %collective-permute-start.3 = (bf16[256,512]{1,0:T(8,128)(2,1)}, bf16[256,512]{1,0:T(8,128)(2,1)S(1)}, u32[]{:S(2)}, u32[]{:S(2)}) collective-permute-start(bf16[256,512]{1,0:T(8,128)(2,1)} %get-tuple-element.57), channel_id=1, source_target_pairs={{0,2},{2,0},{4,6},{6,4},{8,10},{10,8},{12,14},{14,12},{1,3},{3,1},... | collective-permute-start | bytes 786440 | tf_op jit(solution)/shard_map/ppermute | solution.py:181
  12.7 20.5 %collective-permute-start.4 = (bf16[256,512]{1,0:T(8,128)(2,1)}, bf16[256,512]{1,0:T(8,128)(2,1)}, u32[]{:S(2)}, u32[]{:S(2)}) collective-permute-start(bf16[256,512]{1,0:T(8,128)(2,1)} %get-tuple-element.56), channel_id=1, source_target_pairs={{0,4},{2,6},{4,0},{6,2},{8,12},{10,14},{12,8},{14,10},{1,5},{3,7},... | collective-permute-start | bytes 786440 | tf_op jit(solution)/shard_map/ppermute | solution.py:181
  14.3 22.6 %collective-permute-start.5 = (bf16[256,512]{1,0:T(8,128)(2,1)}, bf16[256,512]{1,0:T(8,128)(2,1)}, u32[]{:S(2)}, u32[]{:S(2)}) collective-permute-start(bf16[256,512]{1,0:T(8,128)(2,1)} %get-tuple-element.55), channel_id=1, source_target_pairs={{0,6},{2,4},{4,2},{6,0},{8,14},{10,12},{12,10},{14,8},{1,7},{3,5},... | collective-permute-start | bytes 786440 | tf_op jit(solution)/shard_map/ppermute | solution.py:181
  28.9 30.7 %collective-permute-start.10 = (bf16[512,1024]{1,0:T(8,128)(2,1)}, bf16[512,1024]{1,0:T(8,128)(2,1)}, u32[]{:S(2)}, u32[]{:S(2)}) collective-permute-start(bf16[512,1024]{1,0:T(8,128)(2,1)} %w_neigh.1), channel_id=1, source_target_pairs={{0,1},{1,0},{2,3},{3,2},{4,5},{5,4},{6,7},{7,6},{8,9},{9,8},{10,11... | collective-permute-start | bytes 3145736 | tf_op jit(solution)/shard_map/ppermute | solution.py:178
  29.8 12.6 %collective-permute-start.6 = (bf16[256,512]{1,0:T(8,128)(2,1)S(1)}, bf16[256,512]{1,0:T(8,128)(2,1)S(1)}, u32[]{:S(2)}, u32[]{:S(2)}) collective-permute-start(bf16[256,512]{1,0:T(8,128)(2,1)S(1)} %get-tuple-element.54), channel_id=1, source_target_pairs={{0,2},{2,0},{4,6},{6,4},{8,10},{10,8},{12,14},{14,12},{1,3},{3,1},... | collective-permute-start | bytes 786440 | tf_op jit(solution)/shard_map/ppermute | solution.py:181
  33.2 24.6 %collective-permute-start = (bf16[256,512]{1,0:T(8,128)(2,1)}, bf16[256,512]{1,0:T(8,128)(2,1)}, u32[]{:S(2)}, u32[]{:S(2)}) collective-permute-start(bf16[256,512]{1,0:T(8,128)(2,1)} %get-tuple-element.58), channel_id=1, source_target_pairs={{0,1},{1,0},{2,3},{3,2},{4,5},{5,4},{6,7},{7,6},{8,9},{9,8},{10,11... | collective-permute-start | bytes 786440 | tf_op jit(solution)/shard_map/ppermute | solution.py:178
  36.9 18.6 %collective-permute-start.7 = (bf16[256,512]{1,0:T(8,128)(2,1)}, bf16[256,512]{1,0:T(8,128)(2,1)}, u32[]{:S(2)}, u32[]{:S(2)}) collective-permute-start(bf16[256,512]{1,0:T(8,128)(2,1)} %get-tuple-element.53), channel_id=1, source_target_pairs={{0,4},{2,6},{4,0},{6,2},{8,12},{10,14},{12,8},{14,10},{1,5},{3,7},... | collective-permute-start | bytes 786440 | tf_op jit(solution)/shard_map/ppermute | solution.py:181
  43.0 12.7 %collective-permute-start.8 = (bf16[256,512]{1,0:T(8,128)(2,1)}, bf16[256,512]{1,0:T(8,128)(2,1)}, u32[]{:S(2)}, u32[]{:S(2)}) collective-permute-start(bf16[256,512]{1,0:T(8,128)(2,1)} %get-tuple-element.52), channel_id=1, source_target_pairs={{0,6},{2,4},{4,2},{6,0},{8,14},{10,12},{12,10},{14,8},{1,7},{3,5},... | collective-permute-start | bytes 786440 | tf_op jit(solution)/shard_map/ppermute | solution.py:181
  55.5 4.1 %collective-permute-start.11 = (bf16[256,512]{1,0:T(8,128)(2,1)S(1)}, bf16[256,512]{1,0:T(8,128)(2,1)S(1)}, u32[]{:S(2)}, u32[]{:S(2)}) collective-permute-start(bf16[256,512]{1,0:T(8,128)(2,1)S(1)} %copy-done.23), channel_id=1, source_target_pairs={{0,1},{1,0},{2,3},{3,2},{4,5},{5,4},{6,7},{7,6},{8,9},{9,8},{10,11... | collective-permute-start | bytes 786440 | tf_op jit(solution)/shard_map/ppermute | solution.py:178
  57.4 2.1 %collective-permute-start.9 = (bf16[256,512]{1,0:T(8,128)(2,1)S(1)}, bf16[256,512]{1,0:T(8,128)(2,1)S(1)}, u32[]{:S(2)}, u32[]{:S(2)}) collective-permute-start(bf16[256,512]{1,0:T(8,128)(2,1)S(1)} %get-tuple-element.27), channel_id=1, source_target_pairs={{0,1},{1,0},{2,3},{3,2},{4,5},{5,4},{6,7},{7,6},{8,9},{9,8},{10,11... | collective-permute-start | bytes 786440 | tf_op jit(solution)/shard_map/ppermute | solution.py:178
  64.1 2.3 %collective-permute-start.13 = (bf16[256,1024]{1,0:T(8,128)(2,1)}, bf16[256,1024]{1,0:T(8,128)(2,1)}, u32[]{:S(2)}, u32[]{:S(2)}) collective-permute-start(bf16[256,1024]{1,0:T(8,128)(2,1)} %get-tuple-element.30.slope_own), channel_id=1, source_target_pairs={{0,1},{1,0},{2,3},{3,2},{4,5},{5,4},{6,7},{7,6},{8,9},{9,8},{10,11... | collective-permute-start | bytes 1572872 | tf_op jit(solution)/shard_map/ppermute | solution.py:178
  73.7 25.4 %collective-permute-start.21 = (bf16[4,2,512,128]{3,2,1,0:T(8,128)(2,1)S(1)}, bf16[4,2,512,128]{3,2,1,0:T(8,128)(2,1)S(1)}, u32[]{:S(2)}, u32[]{:S(2)}) collective-permute-start(bf16[4,2,512,128]{3,2,1,0:T(8,128)(2,1)S(1)} %get-tuple-element.43), channel_id=1, source_target_pairs={{0,2},{2,0},{4,6},{6,4},{8,10},{10,8},{12,14},{14,12},{1,3},{3,1},... | collective-permute-start | bytes 3145736 | tf_op jit(solution)/shard_map/ppermute | solution.py:181
  99.5 30.8 %collective-permute-start.22 = (bf16[2,2,512,128]{3,2,1,0:T(8,128)(2,1)S(1)}, bf16[2,2,512,128]{3,2,1,0:T(8,128)(2,1)S(1)}, u32[]{:S(2)}, u32[]{:S(2)}) collective-permute-start(bf16[2,2,512,128]{3,2,1,0:T(8,128)(2,1)S(1)} %slice.63), channel_id=1, source_target_pairs={{0,4},{2,6},{4,0},{6,2},{8,12},{10,14},{12,8},{14,10},{1,5},{3,7},... | collective-permute-start | bytes 1572872 | tf_op jit(solution)/shard_map/ppermute | solution.py:181
  102.4 7.3 %collective-permute-start.14 = (bf16[256,512]{1,0:T(8,128)(2,1)S(1)}, bf16[256,512]{1,0:T(8,128)(2,1)S(1)}, u32[]{:S(2)}, u32[]{:S(2)}) collective-permute-start(bf16[256,512]{1,0:T(8,128)(2,1)S(1)} %get-tuple-element.36), channel_id=1, source_target_pairs={{0,2},{2,0},{4,6},{6,4},{8,10},{10,8},{12,14},{14,12},{1,3},{3,1},... | collective-permute-start | bytes 786440 | tf_op jit(solution)/shard_map/ppermute | solution.py:181
  103.0 17.9 %collective-permute-start.15 = (bf16[256,512]{1,0:T(8,128)(2,1)S(1)}, bf16[256,512]{1,0:T(8,128)(2,1)S(1)}, u32[]{:S(2)}, u32[]{:S(2)}) collective-permute-start(bf16[256,512]{1,0:T(8,128)(2,1)S(1)} %get-tuple-element.37), channel_id=1, source_target_pairs={{0,4},{2,6},{4,0},{6,2},{8,12},{10,14},{12,8},{14,10},{1,5},{3,7},... | collective-permute-start | bytes 786440 | tf_op jit(solution)/shard_map/ppermute | solution.py:181
  103.1 23.5 %collective-permute-start.16 = (bf16[256,512]{1,0:T(8,128)(2,1)S(1)}, bf16[256,512]{1,0:T(8,128)(2,1)S(1)}, u32[]{:S(2)}, u32[]{:S(2)}) collective-permute-start(bf16[256,512]{1,0:T(8,128)(2,1)S(1)} %get-tuple-element.38), channel_id=1, source_target_pairs={{0,6},{2,4},{4,2},{6,0},{8,14},{10,12},{12,10},{14,8},{1,7},{3,5},... | collective-permute-start | bytes 786440 | tf_op jit(solution)/shard_map/ppermute | solution.py:181
  105.9 25.5 %collective-permute-start.12 = (bf16[256,512]{1,0:T(8,128)(2,1)S(1)}, bf16[256,512]{1,0:T(8,128)(2,1)S(1)}, u32[]{:S(2)}, u32[]{:S(2)}) collective-permute-start(bf16[256,512]{1,0:T(8,128)(2,1)S(1)} %copy-done.21), channel_id=1, source_target_pairs={{0,1},{1,0},{2,3},{3,2},{4,5},{5,4},{6,7},{7,6},{8,9},{9,8},{10,11... | collective-permute-start | bytes 786440 | tf_op jit(solution)/shard_map/ppermute | solution.py:178
  109.8 26.4 %collective-permute-start.18 = (bf16[256,512]{1,0:T(8,128)(2,1)S(1)}, bf16[256,512]{1,0:T(8,128)(2,1)S(1)}, u32[]{:S(2)}, u32[]{:S(2)}) collective-permute-start(bf16[256,512]{1,0:T(8,128)(2,1)S(1)} %get-tuple-element.39), channel_id=1, source_target_pairs={{0,2},{2,0},{4,6},{6,4},{8,10},{10,8},{12,14},{14,12},{1,3},{3,1},... | collective-permute-start | bytes 786440 | tf_op jit(solution)/shard_map/ppermute | solution.py:181
  120.9 19.3 %collective-permute-start.19 = (bf16[256,512]{1,0:T(8,128)(2,1)S(1)}, bf16[256,512]{1,0:T(8,128)(2,1)S(1)}, u32[]{:S(2)}, u32[]{:S(2)}) collective-permute-start(bf16[256,512]{1,0:T(8,128)(2,1)S(1)} %get-tuple-element.40), channel_id=1, source_target_pairs={{0,4},{2,6},{4,0},{6,2},{8,12},{10,14},{12,8},{14,10},{1,5},{3,7},... | collective-permute-start | bytes 786440 | tf_op jit(solution)/shard_map/ppermute | solution.py:181
  126.6 18.0 %collective-permute-start.20 = (bf16[256,512]{1,0:T(8,128)(2,1)S(1)}, bf16[256,512]{1,0:T(8,128)(2,1)S(1)}, u32[]{:S(2)}, u32[]{:S(2)}) collective-permute-start(bf16[256,512]{1,0:T(8,128)(2,1)S(1)} %get-tuple-element.41), channel_id=1, source_target_pairs={{0,6},{2,4},{4,2},{6,0},{8,14},{10,12},{12,10},{14,8},{1,7},{3,5},... | collective-permute-start | bytes 786440 | tf_op jit(solution)/shard_map/ppermute | solution.py:181
  130.3 31.0 %collective-permute-start.17 = (bf16[512,512]{1,0:T(8,128)(2,1)S(1)}, bf16[512,512]{1,0:T(8,128)(2,1)S(1)}, u32[]{:S(2)}, u32[]{:S(2)}) collective-permute-start(bf16[512,512]{1,0:T(8,128)(2,1)S(1)} %shard_map.109), channel_id=1, source_target_pairs={{0,8},{2,10},{4,12},{6,14},{8,0},{10,2},{12,4},{14,6},{1,9},{3,11}... | collective-permute-start | bytes 1572872 | tf_op jit(solution)/shard_map/ppermute | solution.py:181
  131.5 32.7 %collective-permute-start.23 = (bf16[1,2,512,128]{3,2,1,0:T(8,128)(2,1)S(1)}, bf16[1,2,512,128]{3,2,1,0:T(8,128)(2,1)S(1)}, u32[]{:S(2)}, u32[]{:S(2)}) collective-permute-start(bf16[1,2,512,128]{3,2,1,0:T(8,128)(2,1)S(1)} %slice.91), channel_id=1, source_target_pairs={{0,8},{2,10},{4,12},{6,14},{8,0},{10,2},{12,4},{14,6},{1,9},{3,11}... | collective-permute-start | bytes 786440 | tf_op jit(solution)/shard_map/ppermute | solution.py:181
  (26 other events, 116.4 us)

commit v2 on v1

--- a/solution.py
+++ b/solution.py
@@ -24,16 +24,21 @@
     return pl.ds(pl.multiple_of(index * TILE, TILE), TILE)
 
 
+def after(x, *earlier):
+    return lax.optimization_barrier((x, earlier))[0]
+
+
 def local_call(kernel, outs, ins, flops, scratch=(), scalars=1):
     moved = sum(a.size * a.dtype.itemsize for a in ins)
     moved += sum(o.size * o.dtype.itemsize for o in outs)
+    held = moved + 8 * 1024 * 1024
     return pl.pallas_call(
         kernel,
         out_shape=outs,
         in_specs=[SMEM] * scalars + [VMEM] * (len(ins) - scalars),
         out_specs=[VMEM] * len(outs),
         scratch_shapes=list(scratch),
-        compiler_params=pltpu.CompilerParams(vmem_limit_bytes=44 * 1024 * 1024),
+        compiler_params=pltpu.CompilerParams(vmem_limit_bytes=held),
         cost_estimate=pl.CostEstimate(flops=flops, bytes_accessed=moved, transcendentals=0),
     )(*ins)
 
@@ -69,7 +74,7 @@
             pl.BlockSpec((1, TILE, rows), lambda j: (j, 0, 0)),
         ],
         scratch_shapes=[pltpu.VMEM((TILE, TILE), F32)],
-        compiler_params=pltpu.CompilerParams(vmem_limit_bytes=32 * 1024 * 1024),
+        compiler_params=pltpu.CompilerParams(vmem_limit_bytes=16 * 1024 * 1024),
         cost_estimate=pl.CostEstimate(
             flops=0, bytes_accessed=2 * tiles.size + 4 * count * rows * TILE, transcendentals=0
         ),
@@ -125,18 +130,18 @@
     partner[...] = mul(early[2 + count], scaled[...])
 
 
-def terms_kernel(info, slope, features_t, agg_t, keep, away):
+def terms_kernel(info, slope, features_t, agg_t, keep_self, away_self, keep_neigh, away_neigh):
     node = info[3, 1]
     low = node % 2
     high = node // 2
-    width = keep.shape[3]
-    for which, left in enumerate((features_t, agg_t)):
+    width = keep_self.shape[2]
+    for left, keep, away in ((features_t, keep_self, away_self), (agg_t, keep_neigh, away_neigh)):
         for p in range(keep.shape[0]):
             both = mul(left[...], slope[:, 2 * p * width : 2 * (p + 1) * width])
             a, b = both[:, :width], both[:, width:]
             at = jnp.bitwise_xor(high, p)
-            keep[at, which] = jnp.where(low == 0, a, b)
-            away[at, which] = jnp.where(low == 0, b, a).astype(BF16)
+            keep[at] = jnp.where(low == 0, a, b)
+            away[at] = jnp.where(low == 0, b, a).astype(BF16)
 
 
 def base_kernel(info, slope, w_self, scaled, early, out):
@@ -221,6 +226,7 @@
     self_part = mul(rows_own, w_self) + mul(rows_in, w_self_in)
     features_t = features.T
 
+    partner = after(partner, early, late, self_part, features_t)
     passed = [hop(lax.dynamic_slice_in_dim(partner, info[1, k] * TILE, TILE, 0), k) for k in near]
     tile_flops = 2 * own_rows * TILE * width
     (summed,) = local_call(
@@ -258,37 +264,6 @@
         2 * own_rows * hidden_width * width + (nodes - 1) * tile_flops,
     )
     back_passed = [hop(pieces[k - 1], k) for k in near]
-    back_direct = [hop(pieces[count + k - 1], k) for k in near]
-
-    columns = hidden_width // nodes
-    if columns % 128 == 0:
-        groups = nodes // 2
-        keep, away = local_call(
-            terms_kernel,
-            [shape((groups, 2, width, columns), F32), shape((groups, 2, width, columns), BF16)],
-            [info, slope, features_t, agg_t],
-            4 * own_rows * width * hidden_width,
-        )
-        bit = 1
-        while True:
-            keep = keep + hop(away, bit).astype(F32)
-            bit *= 2
-            if bit == nodes:
-                break
-            keep, away = keep[0::2], keep[1::2].astype(BF16)
-        grad_self, grad_neigh = keep[0, 0], keep[0, 1]
-    else:
-        grad_self, grad_neigh = (
-            lax.psum_scatter(mul(left, slope), "node", scatter_dimension=1, tiled=True)
-            for left in (features_t, agg_t)
-        )
-
-    (base,) = local_call(
-        base_kernel,
-        [shape((own_rows, width), F32)],
-        [info, slope, w_self, scaled, early_t],
-        2 * own_rows * hidden_width * width + 2 * tile_flops,
-    )
     (to_partner,) = local_call(
         partner_kernel,
         [shape((own_rows, width), BF16)],
@@ -297,6 +272,45 @@
         [pltpu.VMEM((own_rows, width), F32)],
     )
     from_partner = hop(to_partner, across)
+    back_direct = [hop(after(pieces[count + k - 1], to_partner), k) for k in near]
+
+    columns = hidden_width // nodes
+    if columns % 128 == 0:
+        groups = nodes // 2
+        keep, away = shape((groups, width, columns), F32), shape((groups, width, columns), BF16)
+        terms = local_call(
+            terms_kernel,
+            [keep, away, keep, away],
+            [info, slope, features_t, agg_t],
+            4 * own_rows * width * hidden_width,
+        )
+        keeps, aways = list(terms[0::2]), list(terms[1::2])
+        bit = 1
+        while True:
+            if bit == 1:
+                aways = [after(x, back_passed[0]) for x in aways]
+            came = [hop(x, bit) for x in aways]
+            if bit == 1:
+                came = [after(x, to_partner) for x in came]
+            keeps = [x + y.astype(F32) for x, y in zip(keeps, came)]
+            bit *= 2
+            if bit == nodes:
+                break
+            aways = [x[1::2].astype(BF16) for x in keeps]
+            keeps = [x[0::2] for x in keeps]
+        grad_self, grad_neigh = keeps[0][0], keeps[1][0]
+    else:
+        grad_self, grad_neigh = (
+            lax.psum_scatter(mul(left, slope), "node", scatter_dimension=1, tiled=True)
+            for left in (features_t, agg_t)
+        )
+
+    (base,) = local_call(
+        base_kernel,
+        [shape((own_rows, width), F32)],
+        [info, slope, w_self, scaled, early_t],
+        2 * own_rows * hidden_width * width + 2 * tile_flops,
+    )
     (grad_features,) = local_call(
         final_kernel,
         [shape((own_rows, width), BF16)],

time: 166 us -> 139 us (0.84)
  waiting for transfers between devices: 87.6 us -> 63.5 us
  local copies, waits for them, and re-layouts: 15.5 us -> 19.8 us
  starting transfers between devices: 26.8 us -> 23.7 us
  Pallas kernels: 20.5 us -> 18.3 us
    ppermute x17 -> x20, waiting for transfers between devices: 86.8 us -> 60.2 us  [hop(): return lax.ppermute(x, 'node', [(i, i ^ k) for i in range(nodes)])]
    unnamed x54 -> x82, local copies, waits for them, and re-layouts: 11.1 us -> 16.9 us
    ppermute x7, waiting for transfers between devices: 0.76 us -> 3.29 us  [swap(): return lax.ppermute(x, 'feat', [(0, 1), (1, 0)])]
    ppermute x17 -> x20, starting transfers between devices: 25.2 us -> 22.9 us  [hop(): return lax.ppermute(x, 'node', [(i, i ^ k) for i in range(nodes)])]
    pallas_call x8, Pallas kernels: 16 us -> 13.8 us  [local_call(): pl.pallas_call(kernel, out_shape=outs, in_specs=[SMEM] * scalars + [VMEM]...]
    select_n x1, other arithmetic: 1.86 us -> 0.04 us  [halves(): return (jnp.where(first, a, b), jnp.where(first, b, a))]
  transfers between devices with their start and end apart: 24 -> 27, of which waited for: 12 -> 14; matrix products, arithmetic and copies ran while one was open for 8% -> 9% of each run, Pallas kernels for 8% -> 10%
where the time goes in v2:
time: 139 us
  waiting for transfers between devices  63.5 us (46%)
  starting transfers between devices  23.7 us (17%)
  local copies, waits for them, and re-layouts  19.8 us (14%)
  Pallas kernels  18.3 us (13%)
  other arithmetic  6.1 us (4%)
  between operations  4.96 us (4%)
  matrix products  2.24 us (2%)
    ppermute x20, waiting for transfers between devices, hop(): return lax.ppermute(x, 'node', [(i, i ^ k) for i in range(nodes)])  60.2 us
    ppermute x20, starting transfers between devices, hop(): return lax.ppermute(x, 'node', [(i, i ^ k) for i in range(nodes)])  22.9 us
    unnamed x82, local copies, waits for them, and re-layouts  16.9 us
    pallas_call x8, Pallas kernels, local_call(): pl.pallas_call(kernel, out_shape=outs, in_specs=[SMEM] * scalars + [VMEM]...  13.8 us
    pallas_call x2, Pallas kernels, combine(): pl.pallas_call(kernel, grid=(count,), out_shape=[jax.ShapeDtypeStruct((co...  4.52 us
    ppermute x7, waiting for transfers between devices, swap(): return lax.ppermute(x, 'feat', [(0, 1), (1, 0)])  3.29 us
  transfers between devices with their start and end apart: 27, of which 14 were waited for; matrix products, arithmetic and copies ran while one was open for 9% of the time, Pallas kernels for 10%

profile of v2, /device:TPU:0, one launch (start us, length us, event | category | flops | bytes accessed | tf_op | source)
XLA Modules:
  0.0 138.6 jit_solution(7548871808611971139)
XLA Ops:
  0.7 4.1 %collective-permute-start.2 = (bf16[512,512]{1,0:T(8,128)(2,1)}, bf16[512,512]{1,0:T(8,128)(2,1)S(1)}, u32[]{:S(2)}, u32[]{:S(2)}) collective-permute-start(bf16[512,512]{1,0:T(8,128)(2,1)} %own.1), channel_id=1, source_target_pairs={{0,8},{2,10},{4,12},{6,14},{8,0},{10,2},{12,4},{14,6},{1,9},{3,11}... | collective-permute-start | bytes 1572872 | tf_op jit(solution)/shard_map/ppermute | solution.py:186
  8.7 2.3 %constant_dynamic-slice_fusion.3 = (bf16[256,512]{1,0:T(8,128)(2,1)}, bf16[256,512]{1,0:T(8,128)(2,1)}, bf16[256,512]{1,0:T(8,128)(2,1)}, bf16[256,512]{1,0:T(8,128)(2,1)}) fusion(bf16[512,512]{1,0:T(8,128)(2,1)} %own.1, s32[]{:T(128)S(6)} %select_n.86, s32[]{:T(128)S(6)} %select_n.85, s32[]{:T(128)S(6)} %select_n.84, pred[]{:T(512)S(6)} %eq.85), kind=kLoop, calls=%fused_computation.35 | loop fusion | flops 131072 | bytes 2359309 | tf_op jit(solution)/shard_map/dynamic_slice | solution.py:213
  14.9 1.7 %shard_map.102 = (bf16[3,512,256]{2,1,0:T(8,128)(2,1)S(1)}, bf16[3,256,512]{2,1,0:T(8,128)(2,1)S(1)}) custom-call(s32[16]{0:T(128)S(1)} %compare_select_fusion.code_ref, bf16[2,8,256,256]{3,2,1,0:T(8,128)(2,1)S(1)} %copy-done.1), custom_call_target="tpu_custom_call" | custom-call | bytes 3670016 | tf_op jit(solution)/shard_map/pallas_call | solution.py:64
  18.4 2.9 %shard_map.103 = (bf16[6,512,256]{2,1,0:T(8,128)(2,1)S(1)}, bf16[6,256,512]{2,1,0:T(8,128)(2,1)S(1)}) custom-call(s32[16]{0:T(128)S(1)} %compare_select_fusion.code_ref, bf16[2,8,256,256]{3,2,1,0:T(8,128)(2,1)S(1)} %copy-done.1), custom_call_target="tpu_custom_call" | custom-call | bytes 5242880 | tf_op jit(solution)/shard_map/pallas_call | solution.py:64
  28.7 1.8 %convolution_add_fusion.self_part = f32[256,1024]{1,0:T(8,128)S(1)} fusion(f32[256,1024]{1,0:T(8,128)S(1)} %fusion.2, bf16[256,512]{1,0:T(8,128)(2,1)} %collective-permute-done, bf16[512,1024]{1,0:T(8,128)(2,1)} %collective-permute-done.1), kind=kOutput, calls=%fused_computation | convolution fusion | flops 268697600 | bytes 3407872 | tf_op jit(solution)/shard_map/dot_general | solution.py:20
  30.6 1.6 %collective-permute-start.6 = (bf16[256,512]{1,0:T(8,128)(2,1)S(1)}, bf16[256,512]{1,0:T(8,128)(2,1)S(1)}, u32[]{:S(2)}, u32[]{:S(2)}) collective-permute-start(bf16[256,512]{1,0:T(8,128)(2,1)S(1)} %get-tuple-element.74), channel_id=1, source_target_pairs={{0,2},{2,0},{4,6},{6,4},{8,10},{10,8},{12,14},{14,12},{1,3},{3,1},... | collective-permute-start | bytes 786440 | tf_op jit(solution)/shard_map/ppermute | solution.py:186
  34.2 4.2 %collective-permute-done.5.rest_2_ = bf16[256,512]{1,0:T(8,128)(2,1)S(1)} collective-permute-done((bf16[256,512]{1,0:T(8,128)(2,1)S(1)}, bf16[256,512]{1,0:T(8,128)(2,1)S(1)}, u32[]{:S(2)}, u32[]{:S(2)}) %collective-permute-start.5) | collective-permute-done | bytes 262176 | tf_op jit(solution)/shard_map/ppermute | solution.py:186
  38.5 2.1 %shard_map.104.early = f32[512,512]{1,0:T(8,128)S(1)} custom-call(s32[4,8]{1,0:T(4,128)S(1)} %pad_add_fusion.info, bf16[6,512,256]{2,1,0:T(8,128)(2,1)S(1)} %copy-done.6, bf16[512,512]{1,0:T(8,128)(2,1)S(1)} %copy-done, bf16[512,512]{1,0:T(8,128)(2,1)S(1)} %collective-permute-done.2.partner, bf16[256,512]{1,0:T(8,128)(2,1)} %collective-permute-done.3.rest_0_, ...), custom_call_target="tpu_custom_call" | custom-call | flops 805306368 | bytes 4456576 | tf_op jit(solution)/shard_map/pallas_call | solution.py:35
  40.6 3.5 %collective-permute-done.6.rest_0_ = bf16[256,512]{1,0:T(8,128)(2,1)S(1)} collective-permute-done((bf16[256,512]{1,0:T(8,128)(2,1)S(1)}, bf16[256,512]{1,0:T(8,128)(2,1)S(1)}, u32[]{:S(2)}, u32[]{:S(2)}) %collective-permute-start.6) | collective-permute-done | bytes 262176 | tf_op jit(solution)/shard_map/ppermute | solution.py:186
  44.1 4.0 %collective-permute-done.8.rest_2_ = bf16[256,512]{1,0:T(8,128)(2,1)S(1)} collective-permute-done((bf16[256,512]{1,0:T(8,128)(2,1)S(1)}, bf16[256,512]{1,0:T(8,128)(2,1)S(1)}, u32[]{:S(2)}, u32[]{:S(2)}) %collective-permute-start.8) | collective-permute-done | bytes 262176 | tf_op jit(solution)/shard_map/ppermute | solution.py:186
  54.0 1.8 %collective-permute-done.13.slope_in = bf16[256,1024]{1,0:T(8,128)(2,1)S(1)} collective-permute-done((bf16[256,1024]{1,0:T(8,128)(2,1)S(1)}, bf16[256,1024]{1,0:T(8,128)(2,1)S(1)}, u32[]{:S(2)}, u32[]{:S(2)}) %collective-permute-start.13) | collective-permute-done | bytes 524320 | tf_op jit(solution)/shard_map/ppermute | solution.py:183
  55.8 2.8 %shard_map.107 = (bf16[512,1024]{1,0:T(8,128)(2,1)S(1)}, bf16[512,512]{1,0:T(8,128)(2,1)S(1)}, f32[256,512]{1,0:T(8,128)S(1)}, bf16[256,512]{1,0:T(8,128)(2,1)},...) custom-call(s32[4,8]{1,0:T(4,128)S(1)} %pad_add_fusion.info, ...), custom_call_target="tpu_custom_call" | custom-call | flops 1476395008 | bytes 8128640 | tf_op jit(solution)/shard_map/pallas_call | solution.py:35
  70.7 2.0 %shard_map.111 = (f32[4,512,128]{2,1,0:T(8,128)S(1)}, bf16[4,512,128]{2,1,0:T(8,128)(2,1)S(1)}, f32[4,512,128]{2,1,0:T(8,128)S(1)}, bf16[4,512,128]{2,1,0:T(8,128)(2,1)S(1)}) custom-call(s32[4,8]{1,0:T(4,128)S(1)} %pad_add_fusion.info, bf16[512,1024]{1,0:T(8,128)(2,1)S(1)} %copy-done.8, bf16[512,512]{1,0:T(8,128)(2,1)S(1)} %bitcast.22, ...), custom_call_target="tpu_custom_call" | custom-call | flops 1073741824 | bytes 5243008 | tf_op jit(solution)/shard_map/pallas_call | solution.py:35
  75.0 1.9 %collective-permute-start.16 = (bf16[256,512]{1,0:T(8,128)(2,1)S(1)}, bf16[256,512]{1,0:T(8,128)(2,1)S(1)}, u32[]{:S(2)}, u32[]{:S(2)}) collective-permute-start(bf16[256,512]{1,0:T(8,128)(2,1)S(1)} %copy-done.33), channel_id=1, source_target_pairs={{0,6},{2,4},{4,2},{6,0},{8,14},{10,12},{12,10},{14,8},{1,7},{3,5},... | collective-permute-start | bytes 786440 | tf_op jit(solution)/shard_map/ppermute | solution.py:186
  79.5 4.6 %collective-permute-done.15.rest_1_ = bf16[256,512]{1,0:T(8,128)(2,1)S(1)} collective-permute-done((bf16[256,512]{1,0:T(8,128)(2,1)S(1)}, bf16[256,512]{1,0:T(8,128)(2,1)S(1)}, u32[]{:S(2)}, u32[]{:S(2)}) %collective-permute-start.15) | collective-permute-done | bytes 262176 | tf_op jit(solution)/shard_map/ppermute | solution.py:186
  84.1 5.2 %collective-permute-done.16.rest_2_ = bf16[256,512]{1,0:T(8,128)(2,1)S(1)} collective-permute-done((bf16[256,512]{1,0:T(8,128)(2,1)S(1)}, bf16[256,512]{1,0:T(8,128)(2,1)S(1)}, u32[]{:S(2)}, u32[]{:S(2)}) %collective-permute-start.16) | collective-permute-done | bytes 262176 | tf_op jit(solution)/shard_map/ppermute | solution.py:186
  93.2 1.7 %collective-permute-start.19 = (bf16[256,512]{1,0:T(8,128)(2,1)S(1)}, bf16[256,512]{1,0:T(8,128)(2,1)S(1)}, u32[]{:S(2)}, u32[]{:S(2)}) collective-permute-start(bf16[256,512]{1,0:T(8,128)(2,1)S(1)} %copy-done.27), channel_id=1, source_target_pairs={{0,4},{2,6},{4,0},{6,2},{8,12},{10,14},{12,8},{14,10},{1,5},{3,7},... | collective-permute-start | bytes 786440 | tf_op jit(solution)/shard_map/ppermute | solution.py:186
  95.4 14.7 %collective-permute-done.24 = bf16[4,512,128]{2,1,0:T(8,128)(2,1)S(1)} collective-permute-done((bf16[4,512,128]{2,1,0:T(8,128)(2,1)S(1)}, bf16[4,512,128]{2,1,0:T(8,128)(2,1)S(1)}, u32[]{:S(2)}, u32[]{:S(2)}) %collective-permute-start.24) | collective-permute-done | bytes 524320 | tf_op jit(solution)/shard_map/ppermute | solution.py:186
  110.2 3.7 %collective-permute-done.18.rest_0_ = bf16[256,512]{1,0:T(8,128)(2,1)S(1)} collective-permute-done((bf16[256,512]{1,0:T(8,128)(2,1)S(1)}, bf16[256,512]{1,0:T(8,128)(2,1)S(1)}, u32[]{:S(2)}, u32[]{:S(2)}) %collective-permute-start.18) | collective-permute-done | bytes 262176 | tf_op jit(solution)/shard_map/ppermute | solution.py:186
  115.5 2.5 %collective-permute-done.20.rest_2_ = bf16[256,512]{1,0:T(8,128)(2,1)S(1)} collective-permute-done((bf16[256,512]{1,0:T(8,128)(2,1)S(1)}, bf16[256,512]{1,0:T(8,128)(2,1)S(1)}, u32[]{:S(2)}, u32[]{:S(2)}) %collective-permute-start.20) | collective-permute-done | bytes 262176 | tf_op jit(solution)/shard_map/ppermute | solution.py:186
  118.0 1.7 %shard_map.110 = bf16[512,512]{1,0:T(8,128)(2,1)} custom-call(s32[4,8]{1,0:T(4,128)S(1)} %pad_add_fusion.info, f32[512,512]{1,0:T(8,128)S(1)} %shard_map.108.base, bf16[512,512]{1,0:T(8,128)(2,1)S(1)} %collective-permute-done.17.partner, bf16[256,512]{1,0:T(8,128)(2,1)S(1)} %collective-permute-done.18.rest_0_, ...), custom_call_target="tpu_custom_call" | custom-call | bytes 2883712 | tf_op jit(solution)/shard_map/pallas_call | solution.py:35
  119.7 4.8 %collective-permute-done.22 = bf16[2,512,128]{2,1,0:T(8,128)(2,1)S(1)} collective-permute-done((bf16[2,512,128]{2,1,0:T(8,128)(2,1)S(1)}, bf16[2,512,128]{2,1,0:T(8,128)(2,1)S(1)}, u32[]{:S(2)}, u32[]{:S(2)}) %collective-permute-start.22) | collective-permute-done | bytes 262176 | tf_op jit(solution)/shard_map/ppermute | solution.py:186
  124.7 6.8 %collective-permute-done.25 = bf16[2,512,128]{2,1,0:T(8,128)(2,1)S(1)} collective-permute-done((bf16[2,512,128]{2,1,0:T(8,128)(2,1)S(1)}, bf16[2,512,128]{2,1,0:T(8,128)(2,1)S(1)}, u32[]{:S(2)}, u32[]{:S(2)}) %collective-permute-start.25) | collective-permute-done | bytes 262176 | tf_op jit(solution)/shard_map/ppermute | solution.py:186
  132.3 5.6 %collective-permute-done.26 = bf16[1,512,128]{2,1,0:T(8,128)(2,1)S(1)} collective-permute-done((bf16[1,512,128]{2,1,0:T(8,128)(2,1)S(1)}, bf16[1,512,128]{2,1,0:T(8,128)(2,1)S(1)}, u32[]{:S(2)}, u32[]{:S(2)}) %collective-permute-start.26) | collective-permute-done | bytes 131104 | tf_op jit(solution)/shard_map/ppermute | solution.py:186
  (159 shorter events, 45.7 us)
Async XLA Ops:
  0.7 29.9 %collective-permute-start.2 = (bf16[512,512]{1,0:T(8,128)(2,1)}, bf16[512,512]{1,0:T(8,128)(2,1)S(1)}, u32[]{:S(2)}, u32[]{:S(2)}) collective-permute-start(bf16[512,512]{1,0:T(8,128)(2,1)} %own.1), channel_id=1, source_target_pairs={{0,8},{2,10},{4,12},{6,14},{8,0},{10,2},{12,4},{14,6},{1,9},{3,11}... | collective-permute-start | bytes 1572872 | tf_op jit(solution)/shard_map/ppermute | solution.py:186
  11.0 17.2 %collective-permute-start = (bf16[256,512]{1,0:T(8,128)(2,1)}, bf16[256,512]{1,0:T(8,128)(2,1)}, u32[]{:S(2)}, u32[]{:S(2)}) collective-permute-start(bf16[256,512]{1,0:T(8,128)(2,1)} %get-tuple-element.78), channel_id=1, source_target_pairs={{0,1},{1,0},{2,3},{3,2},{4,5},{5,4},{6,7},{7,6},{8,9},{9,8},{10,11... | collective-permute-start | bytes 786440 | tf_op jit(solution)/shard_map/ppermute | solution.py:183
  11.0 17.7 %collective-permute-start.1 = (bf16[512,1024]{1,0:T(8,128)(2,1)}, bf16[512,1024]{1,0:T(8,128)(2,1)}, u32[]{:S(2)}, u32[]{:S(2)}) collective-permute-start(bf16[512,1024]{1,0:T(8,128)(2,1)} %w_self.1), channel_id=1, source_target_pairs={{0,1},{1,0},{2,3},{3,2},{4,5},{5,4},{6,7},{7,6},{8,9},{9,8},{10,11... | collective-permute-start | bytes 3145736 | tf_op jit(solution)/shard_map/ppermute | solution.py:183
  11.5 20.7 %collective-permute-start.3 = (bf16[256,512]{1,0:T(8,128)(2,1)}, bf16[256,512]{1,0:T(8,128)(2,1)}, u32[]{:S(2)}, u32[]{:S(2)}) collective-permute-start(bf16[256,512]{1,0:T(8,128)(2,1)} %get-tuple-element.77), channel_id=1, source_target_pairs={{0,2},{2,0},{4,6},{6,4},{8,10},{10,8},{12,14},{14,12},{1,3},{3,1},... | collective-permute-start | bytes 786440 | tf_op jit(solution)/shard_map/ppermute | solution.py:186
  13.1 20.7 %collective-permute-start.4 = (bf16[256,512]{1,0:T(8,128)(2,1)}, bf16[256,512]{1,0:T(8,128)(2,1)}, u32[]{:S(2)}, u32[]{:S(2)}) collective-permute-start(bf16[256,512]{1,0:T(8,128)(2,1)} %get-tuple-element.76), channel_id=1, source_target_pairs={{0,4},{2,6},{4,0},{6,2},{8,12},{10,14},{12,8},{14,10},{1,5},{3,7},... | collective-permute-start | bytes 786440 | tf_op jit(solution)/shard_map/ppermute | solution.py:186
  28.3 10.1 %collective-permute-start.5 = (bf16[256,512]{1,0:T(8,128)(2,1)S(1)}, bf16[256,512]{1,0:T(8,128)(2,1)S(1)}, u32[]{:S(2)}, u32[]{:S(2)}) collective-permute-start(bf16[256,512]{1,0:T(8,128)(2,1)S(1)} %copy-done.37), channel_id=1, source_target_pairs={{0,6},{2,4},{4,2},{6,0},{8,14},{10,12},{12,10},{14,8},{1,7},{3,5},... | collective-permute-start | bytes 786440 | tf_op jit(solution)/shard_map/ppermute | solution.py:186
  28.7 20.7 %collective-permute-start.10 = (bf16[512,1024]{1,0:T(8,128)(2,1)S(1)}, bf16[512,1024]{1,0:T(8,128)(2,1)S(1)}, u32[]{:S(2)}, u32[]{:S(2)}) collective-permute-start(bf16[512,1024]{1,0:T(8,128)(2,1)S(1)} %copy-done.10), channel_id=1, source_target_pairs={{0,1},{1,0},{2,3},{3,2},{4,5},{5,4},{6,7},{7,6},{8,9},{9,8},{10,11... | collective-permute-start | bytes 3145736 | tf_op jit(solution)/shard_map/ppermute | solution.py:183
  30.6 13.4 %collective-permute-start.6 = (bf16[256,512]{1,0:T(8,128)(2,1)S(1)}, bf16[256,512]{1,0:T(8,128)(2,1)S(1)}, u32[]{:S(2)}, u32[]{:S(2)}) collective-permute-start(bf16[256,512]{1,0:T(8,128)(2,1)S(1)} %get-tuple-element.74), channel_id=1, source_target_pairs={{0,2},{2,0},{4,6},{6,4},{8,10},{10,8},{12,14},{14,12},{1,3},{3,1},... | collective-permute-start | bytes 786440 | tf_op jit(solution)/shard_map/ppermute | solution.py:186
  32.3 11.8 %collective-permute-start.7 = (bf16[256,512]{1,0:T(8,128)(2,1)S(1)}, bf16[256,512]{1,0:T(8,128)(2,1)S(1)}, u32[]{:S(2)}, u32[]{:S(2)}) collective-permute-start(bf16[256,512]{1,0:T(8,128)(2,1)S(1)} %get-tuple-element.73), channel_id=1, source_target_pairs={{0,4},{2,6},{4,0},{6,2},{8,12},{10,14},{12,8},{14,10},{1,5},{3,7},... | collective-permute-start | bytes 786440 | tf_op jit(solution)/shard_map/ppermute | solution.py:186
  33.8 14.3 %collective-permute-start.8 = (bf16[256,512]{1,0:T(8,128)(2,1)S(1)}, bf16[256,512]{1,0:T(8,128)(2,1)S(1)}, u32[]{:S(2)}, u32[]{:S(2)}) collective-permute-start(bf16[256,512]{1,0:T(8,128)(2,1)S(1)} %get-tuple-element.72), channel_id=1, source_target_pairs={{0,6},{2,4},{4,2},{6,0},{8,14},{10,12},{12,10},{14,8},{1,7},{3,5},... | collective-permute-start | bytes 786440 | tf_op jit(solution)/shard_map/ppermute | solution.py:186
  38.5 10.9 %collective-permute-start.11 = (bf16[256,512]{1,0:T(8,128)(2,1)S(1)}, bf16[256,512]{1,0:T(8,128)(2,1)S(1)}, u32[]{:S(2)}, u32[]{:S(2)}) collective-permute-start(bf16[256,512]{1,0:T(8,128)(2,1)S(1)} %get-tuple-element.70), channel_id=1, source_target_pairs={{0,1},{1,0},{2,3},{3,2},{4,5},{5,4},{6,7},{7,6},{8,9},{9,8},{10,11... | collective-permute-start | bytes 786440 | tf_op jit(solution)/shard_map/ppermute | solution.py:183
  64.8 8.6 %collective-permute-start.14 = (bf16[256,512]{1,0:T(8,128)(2,1)}, bf16[256,512]{1,0:T(8,128)(2,1)S(1)}, u32[]{:S(2)}, u32[]{:S(2)}) collective-permute-start(bf16[256,512]{1,0:T(8,128)(2,1)} %get-tuple-element.47), channel_id=1, source_target_pairs={{0,2},{2,0},{4,6},{6,4},{8,10},{10,8},{12,14},{14,12},{1,3},{3,1},... | collective-permute-start | bytes 786440 | tf_op jit(solution)/shard_map/ppermute | solution.py:186
  73.3 21.6 %collective-permute-start.21 = (bf16[4,512,128]{2,1,0:T(8,128)(2,1)S(1)}, bf16[4,512,128]{2,1,0:T(8,128)(2,1)S(1)}, u32[]{:S(2)}, u32[]{:S(2)}) collective-permute-start(bf16[4,512,128]{2,1,0:T(8,128)(2,1)S(1)} %get-tuple-element.58), channel_id=1, source_target_pairs={{0,2},{2,0},{4,6},{6,4},{8,10},{10,8},{12,14},{14,12},{1,3},{3,1},... | collective-permute-start | bytes 1572872 | tf_op jit(solution)/shard_map/ppermute | solution.py:186
  74.9 9.2 %collective-permute-start.15 = (bf16[256,512]{1,0:T(8,128)(2,1)S(1)}, bf16[256,512]{1,0:T(8,128)(2,1)S(1)}, u32[]{:S(2)}, u32[]{:S(2)}) collective-permute-start(bf16[256,512]{1,0:T(8,128)(2,1)S(1)} %copy-done.35), channel_id=1, source_target_pairs={{0,4},{2,6},{4,0},{6,2},{8,12},{10,14},{12,8},{14,10},{1,5},{3,7},... | collective-permute-start | bytes 786440 | tf_op jit(solution)/shard_map/ppermute | solution.py:186
  75.0 14.3 %collective-permute-start.16 = (bf16[256,512]{1,0:T(8,128)(2,1)S(1)}, bf16[256,512]{1,0:T(8,128)(2,1)S(1)}, u32[]{:S(2)}, u32[]{:S(2)}) collective-permute-start(bf16[256,512]{1,0:T(8,128)(2,1)S(1)} %copy-done.33), channel_id=1, source_target_pairs={{0,6},{2,4},{4,2},{6,0},{8,14},{10,12},{12,10},{14,8},{1,7},{3,5},... | collective-permute-start | bytes 786440 | tf_op jit(solution)/shard_map/ppermute | solution.py:186
  76.9 33.1 %collective-permute-start.24 = (bf16[4,512,128]{2,1,0:T(8,128)(2,1)S(1)}, bf16[4,512,128]{2,1,0:T(8,128)(2,1)S(1)}, u32[]{:S(2)}, u32[]{:S(2)}) collective-permute-start(bf16[4,512,128]{2,1,0:T(8,128)(2,1)S(1)} %get-tuple-element.62), channel_id=1, source_target_pairs={{0,2},{2,0},{4,6},{6,4},{8,10},{10,8},{12,14},{14,12},{1,3},{3,1},... | collective-permute-start | bytes 1572872 | tf_op jit(solution)/shard_map/ppermute | solution.py:186
  90.1 27.9 %collective-permute-start.17 = (bf16[512,512]{1,0:T(8,128)(2,1)S(1)}, bf16[512,512]{1,0:T(8,128)(2,1)S(1)}, u32[]{:S(2)}, u32[]{:S(2)}) collective-permute-start(bf16[512,512]{1,0:T(8,128)(2,1)S(1)} %shard_map.109), channel_id=1, source_target_pairs={{0,8},{2,10},{4,12},{6,14},{8,0},{10,2},{12,4},{14,6},{1,9},{3,11}... | collective-permute-start | bytes 1572872 | tf_op jit(solution)/shard_map/ppermute | solution.py:186
  91.7 22.2 %collective-permute-start.18 = (bf16[256,512]{1,0:T(8,128)(2,1)S(1)}, bf16[256,512]{1,0:T(8,128)(2,1)S(1)}, u32[]{:S(2)}, u32[]{:S(2)}) collective-permute-start(bf16[256,512]{1,0:T(8,128)(2,1)S(1)} %copy-done.29), channel_id=1, source_target_pairs={{0,2},{2,0},{4,6},{6,4},{8,10},{10,8},{12,14},{14,12},{1,3},{3,1},... | collective-permute-start | bytes 786440 | tf_op jit(solution)/shard_map/ppermute | solution.py:186
  93.2 22.3 %collective-permute-start.19 = (bf16[256,512]{1,0:T(8,128)(2,1)S(1)}, bf16[256,512]{1,0:T(8,128)(2,1)S(1)}, u32[]{:S(2)}, u32[]{:S(2)}) collective-permute-start(bf16[256,512]{1,0:T(8,128)(2,1)S(1)} %copy-done.27), channel_id=1, source_target_pairs={{0,4},{2,6},{4,0},{6,2},{8,12},{10,14},{12,8},{14,10},{1,5},{3,7},... | collective-permute-start | bytes 786440 | tf_op jit(solution)/shard_map/ppermute | solution.py:186
  94.9 23.1 %collective-permute-start.20 = (bf16[256,512]{1,0:T(8,128)(2,1)S(1)}, bf16[256,512]{1,0:T(8,128)(2,1)S(1)}, u32[]{:S(2)}, u32[]{:S(2)}) collective-permute-start(bf16[256,512]{1,0:T(8,128)(2,1)S(1)} %copy-done.25), channel_id=1, source_target_pairs={{0,6},{2,4},{4,2},{6,0},{8,14},{10,12},{12,10},{14,8},{1,7},{3,5},... | collective-permute-start | bytes 786440 | tf_op jit(solution)/shard_map/ppermute | solution.py:186
  110.0 14.5 %collective-permute-start.22 = (bf16[2,512,128]{2,1,0:T(8,128)(2,1)S(1)}, bf16[2,512,128]{2,1,0:T(8,128)(2,1)S(1)}, u32[]{:S(2)}, u32[]{:S(2)}) collective-permute-start(bf16[2,512,128]{2,1,0:T(8,128)(2,1)S(1)} %slice.73), channel_id=1, source_target_pairs={{0,4},{2,6},{4,0},{6,2},{8,12},{10,14},{12,8},{14,10},{1,5},{3,7},... | collective-permute-start | bytes 786440 | tf_op jit(solution)/shard_map/ppermute | solution.py:186
  113.9 17.5 %collective-permute-start.25 = (bf16[2,512,128]{2,1,0:T(8,128)(2,1)S(1)}, bf16[2,512,128]{2,1,0:T(8,128)(2,1)S(1)}, u32[]{:S(2)}, u32[]{:S(2)}) collective-permute-start(bf16[2,512,128]{2,1,0:T(8,128)(2,1)S(1)} %slice.77), channel_id=1, source_target_pairs={{0,4},{2,6},{4,0},{6,2},{8,12},{10,14},{12,8},{14,10},{1,5},{3,7},... | collective-permute-start | bytes 786440 | tf_op jit(solution)/shard_map/ppermute | solution.py:186
  124.6 7.0 %collective-permute-start.23 = (bf16[1,512,128]{2,1,0:T(8,128)(2,1)S(1)}, bf16[1,512,128]{2,1,0:T(8,128)(2,1)S(1)}, u32[]{:S(2)}, u32[]{:S(2)}) collective-permute-start(bf16[1,512,128]{2,1,0:T(8,128)(2,1)S(1)} %slice.109), channel_id=1, source_target_pairs={{0,8},{2,10},{4,12},{6,14},{8,0},{10,2},{12,4},{14,6},{1,9},{3,11}... | collective-permute-start | bytes 393224 | tf_op jit(solution)/shard_map/ppermute | solution.py:186
  131.5 6.4 %collective-permute-start.26 = (bf16[1,512,128]{2,1,0:T(8,128)(2,1)S(1)}, bf16[1,512,128]{2,1,0:T(8,128)(2,1)S(1)}, u32[]{:S(2)}, u32[]{:S(2)}) collective-permute-start(bf16[1,512,128]{2,1,0:T(8,128)(2,1)S(1)} %slice.108), channel_id=1, source_target_pairs={{0,8},{2,10},{4,12},{6,14},{8,0},{10,2},{12,4},{14,6},{1,9},{3,11}... | collective-permute-start | bytes 393224 | tf_op jit(solution)/shard_map/ppermute | solution.py:186
  (43 other events, 223.1 us)

commit v3 on v2

--- a/solution.py
+++ b/solution.py
@@ -12,6 +12,7 @@
 BF16, F32 = jnp.bfloat16, jnp.float32
 SMEM = pl.BlockSpec(memory_space=pltpu.SMEM)
 VMEM = pl.BlockSpec(memory_space=pltpu.VMEM)
+HBM = pl.BlockSpec(memory_space=pltpu.HBM)
 ROWS_BY_COLS = (((1,), (0,)), ((), ()))
 COLS_BY_COLS = (((1,), (1,)), ((), ()))
 
@@ -28,15 +29,16 @@
     return lax.optimization_barrier((x, earlier))[0]
 
 
-def local_call(kernel, outs, ins, flops, scratch=(), scalars=1):
+def local_call(kernel, outs, ins, flops, scratch=(), scalars=1, in_hbm=()):
     moved = sum(a.size * a.dtype.itemsize for a in ins)
     moved += sum(o.size * o.dtype.itemsize for o in outs)
     held = moved + 8 * 1024 * 1024
+    placed = [pltpu.HBM(o.shape, o.dtype) if i in in_hbm else o for i, o in enumerate(outs)]
     return pl.pallas_call(
         kernel,
-        out_shape=outs,
+        out_shape=placed,
         in_specs=[SMEM] * scalars + [VMEM] * (len(ins) - scalars),
-        out_specs=[VMEM] * len(outs),
+        out_specs=[HBM if i in in_hbm else VMEM for i in range(len(outs))],
         scratch_shapes=list(scratch),
         compiler_params=pltpu.CompilerParams(vmem_limit_bytes=held),
         cost_estimate=pl.CostEstimate(flops=flops, bytes_accessed=moved, transcendentals=0),
@@ -99,7 +101,7 @@
     away[...] = out[block(1 - info[3, 0]), :]
 
 
-def slope_kernel(info, self_part, agg, agg_in, w_own, w_other, cot_own, cot_in, slope, keep, away, cot, hid):
+def slope_kernel(info, self_part, agg, agg_in, w_own, w_other, cot_own, cot_in, slope, keep, away, cot, hid, sems):
     feat = info[3, 0]
     width = cot_own.shape[1]
     mine = pl.ds(pl.multiple_of(feat * width, width), width)
@@ -114,20 +116,34 @@
         s = jax.nn.sigmoid(pre)
         hid[:, cols] = (pre * s).astype(BF16)
         slope[:, cols] = (cot[:, cols].astype(F32) * s * (1.0 + pre * (1.0 - s))).astype(BF16)
-    keep[...] = hid[:, mine]
-    away[...] = hid[:, other]
-
-
-def pieces_kernel(count, info, slope_own, slope_in, w_neigh, inverse, early, late, slope, scaled, partner, *outs):
+    copies = [
+        pltpu.make_async_copy(hid.at[:, mine], keep, sems.at[0]),
+        pltpu.make_async_copy(hid.at[:, other], away, sems.at[1]),
+    ]
+    for copy in copies:
+        copy.start()
+    for copy in copies:
+        copy.wait()
+
+
+def pieces_kernel(count, info, slope_own, slope_in, w_neigh, inverse, early, late, slope_out, scaled_out, partner_out, *rest):
+    *outs, held, slope, scaled, partner, sems = rest
     feat = info[3, 0]
     slope[block(feat), :] = slope_own[...]
     slope[block(1 - feat), :] = slope_in[...]
     scaled[...] = (mul(slope[...], w_neigh[...], COLS_BY_COLS) * inverse[...]).astype(BF16)
-    for k in range(count):
-        outs[k][...] = mul(late[k], scaled[...]).astype(BF16)
-    for k in range(count):
-        outs[count + k][...] = mul(early[2 + k], scaled[...]).astype(BF16)
+    copies = []
+    for k in range(2 * count):
+        matrix = late[k] if k < count else early[2 + k - count]
+        held[k] = mul(matrix, scaled[...]).astype(BF16)
+        copies.append(pltpu.make_async_copy(held.at[k], outs[k], sems.at[k]))
+        copies[k].start()
     partner[...] = mul(early[2 + count], scaled[...])
+    for k, (source, out) in enumerate(((slope, slope_out), (scaled, scaled_out), (partner, partner_out))):
+        copies.append(pltpu.make_async_copy(source, out, sems.at[2 * count + k]))
+        copies[-1].start()
+    for copy in copies:
+        copy.wait()
 
 
 def terms_kernel(info, slope, features_t, agg_t, keep_self, away_self, keep_neigh, away_neigh):
@@ -248,11 +264,10 @@
         [shape((TILE, hidden_width), BF16), shape((TILE, width), BF16), shape((TILE, width), BF16)],
         [info, self_part, agg, agg_in, w_neigh, w_neigh_in, cot_own, cot_in],
         4 * TILE * width * hidden_width,
-        [pltpu.VMEM((TILE, hidden_width), BF16)] * 2,
+        [pltpu.VMEM((TILE, hidden_width), BF16)] * 2 + [pltpu.SemaphoreType.DMA((2,))],
+        in_hbm=(1, 2),
     )
     slope_in = swap(slope_own)
-    hid_in = swap(hid_away)
-    hidden = jnp.where(feat == 0, jnp.concatenate([hid_keep, hid_in]), jnp.concatenate([hid_in, hid_keep]))
 
     count = across - 1
     piece = shape((TILE, width), BF16)
@@ -262,6 +277,14 @@
         + [piece] * (2 * count),
         [info, slope_own, slope_in, w_neigh, inverse, early_t, late_t],
         2 * own_rows * hidden_width * width + (nodes - 1) * tile_flops,
+        [
+            pltpu.VMEM((2 * count, TILE, width), BF16),
+            pltpu.VMEM((own_rows, hidden_width), BF16),
+            pltpu.VMEM((own_rows, width), BF16),
+            pltpu.VMEM((TILE, width), F32),
+            pltpu.SemaphoreType.DMA((2 * count + 3,)),
+        ],
+        in_hbm=range(3 + 2 * count),
     )
     back_passed = [hop(pieces[k - 1], k) for k in near]
     (to_partner,) = local_call(
@@ -273,6 +296,7 @@
     )
     from_partner = hop(to_partner, across)
     back_direct = [hop(after(pieces[count + k - 1], to_partner), k) for k in near]
+    last = to_partner
 
     columns = hidden_width // nodes
     if columns % 128 == 0:
@@ -285,25 +309,28 @@
             4 * own_rows * width * hidden_width,
         )
         keeps, aways = list(terms[0::2]), list(terms[1::2])
+        flying = [hop(after(x, *back_passed), 1) for x in aways]
+        gate = to_partner
         bit = 1
-        while True:
+        while bit < nodes:
+            for i in range(2):
+                keeps[i] = keeps[i] + after(flying[i], gate).astype(F32)
+                if bit * 2 < nodes:
+                    flying[i] = hop(keeps[i][1::2].astype(BF16), bit * 2)
+                    keeps[i] = keeps[i][0::2]
+                    gate = (flying[0], from_partner, *back_direct[1:])
             if bit == 1:
-                aways = [after(x, back_passed[0]) for x in aways]
-            came = [hop(x, bit) for x in aways]
-            if bit == 1:
-                came = [after(x, to_partner) for x in came]
-            keeps = [x + y.astype(F32) for x, y in zip(keeps, came)]
+                last = keeps[1]
             bit *= 2
-            if bit == nodes:
-                break
-            aways = [x[1::2].astype(BF16) for x in keeps]
-            keeps = [x[0::2] for x in keeps]
         grad_self, grad_neigh = keeps[0][0], keeps[1][0]
     else:
         grad_self, grad_neigh = (
             lax.psum_scatter(mul(left, slope), "node", scatter_dimension=1, tiled=True)
             for left in (features_t, agg_t)
         )
+
+    hid_in = swap(after(hid_away, last))
+    hidden = jnp.where(feat == 0, jnp.concatenate([hid_keep, hid_in]), jnp.concatenate([hid_in, hid_keep]))
 
     (base,) = local_call(
         base_kernel,

time: 139 us -> 128 us (0.921)
  waiting for transfers between devices: 63.5 us -> 53 us
  local copies, waits for them, and re-layouts: 19.8 us -> 12.3 us
  starting transfers between devices: 23.7 us -> 28.3 us
  Pallas kernels: 18.3 us -> 20.4 us
    ppermute x20, waiting for transfers between devices: 60.2 us -> 49.7 us  [hop(): return lax.ppermute(x, 'node', [(i, i ^ k) for i in range(nodes)])]
    unnamed x82 -> x58, local copies, waits for them, and re-layouts: 16.9 us -> 9.42 us
    ppermute x20, starting transfers between devices: 22.9 us -> 27.5 us  [hop(): return lax.ppermute(x, 'node', [(i, i ^ k) for i in range(nodes)])]
    pallas_call x8, Pallas kernels: 13.8 us -> 15.9 us  [local_call(): pl.pallas_call(kernel, out_shape=placed, in_specs=[SMEM] * scalars + [VME...]
  transfers between devices with their start and end apart: 27 -> 27, of which waited for: 14 -> 14; matrix products, arithmetic and copies ran while one was open for 9% -> 10% of each run, Pallas kernels for 10% -> 11%
where the time goes in v3:
time: 128 us; the launch traced here: 127 us
  waiting for transfers between devices  53 us (41%)
  starting transfers between devices  28.3 us (22%)
  Pallas kernels  20.4 us (16%)
  local copies, waits for them, and re-layouts  12.3 us (10%)
  other arithmetic  6.34 us (5%)
  between operations  4.92 us (4%)
  matrix products  2.24 us (2%)
    ppermute x20, waiting for transfers between devices, hop(): return lax.ppermute(x, 'node', [(i, i ^ k) for i in range(nodes)])  49.7 us
    ppermute x20, starting transfers between devices, hop(): return lax.ppermute(x, 'node', [(i, i ^ k) for i in range(nodes)])  27.5 us
    pallas_call x8, Pallas kernels, local_call(): pl.pallas_call(kernel, out_shape=placed, in_specs=[SMEM] * scalars + [VME...  15.9 us
    unnamed x58, local copies, waits for them, and re-layouts  9.42 us
    pallas_call x2, Pallas kernels, combine(): pl.pallas_call(kernel, grid=(count,), out_shape=[jax.ShapeDtypeStruct((co...  4.52 us
    ppermute x7, waiting for transfers between devices, swap(): return lax.ppermute(x, 'feat', [(0, 1), (1, 0)])  3.29 us
  transfers between devices with their start and end apart: 27, of which 14 were waited for; matrix products, arithmetic and copies ran while one was open for 10% of the time, Pallas kernels for 11%

profile of v3, /device:TPU:0, one launch (start us, length us, event | category | flops | bytes accessed | tf_op | source)
XLA Modules:
  0.0 127.5 jit_solution(2485206249417277244)
XLA Ops:
  0.7 4.1 %collective-permute-start.2 = (bf16[512,512]{1,0:T(8,128)(2,1)}, bf16[512,512]{1,0:T(8,128)(2,1)S(1)}, u32[]{:S(2)}, u32[]{:S(2)}) collective-permute-start(bf16[512,512]{1,0:T(8,128)(2,1)} %own.1), channel_id=1, source_target_pairs={{0,8},{2,10},{4,12},{6,14},{8,0},{10,2},{12,4},{14,6},{1,9},{3,11}... | collective-permute-start | bytes 1572872 | tf_op jit(solution)/shard_map/ppermute | solution.py:202
  8.7 2.6 %constant_dynamic-slice_fusion.3 = (bf16[256,512]{1,0:T(8,128)(2,1)}, bf16[256,512]{1,0:T(8,128)(2,1)}, bf16[256,512]{1,0:T(8,128)(2,1)}, bf16[256,512]{1,0:T(8,128)(2,1)}) fusion(bf16[512,512]{1,0:T(8,128)(2,1)} %own.1, s32[]{:T(128)S(6)} %select_n.86, s32[]{:T(128)S(6)} %select_n.85, s32[]{:T(128)S(6)} %select_n.84, pred[]{:T(512)S(6)} %eq.85), kind=kLoop, calls=%fused_computation.35 | loop fusion | flops 131072 | bytes 2359309 | tf_op jit(solution)/shard_map/dynamic_slice | solution.py:229
  18.4 2.9 %shard_map.103 = (bf16[6,512,256]{2,1,0:T(8,128)(2,1)S(1)}, bf16[6,256,512]{2,1,0:T(8,128)(2,1)S(1)}) custom-call(s32[16]{0:T(128)S(1)} %compare_select_fusion.code_ref, bf16[2,8,256,256]{3,2,1,0:T(8,128)(2,1)S(1)} %copy-done.1), custom_call_target="tpu_custom_call" | custom-call | bytes 5242880 | tf_op jit(solution)/shard_map/pallas_call | solution.py:66
  28.9 1.8 %convolution_add_fusion.self_part = f32[256,1024]{1,0:T(8,128)S(1)} fusion(f32[256,1024]{1,0:T(8,128)S(1)} %fusion.2, bf16[256,512]{1,0:T(8,128)(2,1)} %collective-permute-done, bf16[512,1024]{1,0:T(8,128)(2,1)} %collective-permute-done.1), kind=kOutput, calls=%fused_computation | convolution fusion | flops 268697600 | bytes 3407872 | tf_op jit(solution)/shard_map/dot_general | solution.py:21
  34.5 4.0 %collective-permute-done.5.rest_2_ = bf16[256,512]{1,0:T(8,128)(2,1)S(1)} collective-permute-done((bf16[256,512]{1,0:T(8,128)(2,1)S(1)}, bf16[256,512]{1,0:T(8,128)(2,1)S(1)}, u32[]{:S(2)}, u32[]{:S(2)}) %collective-permute-start.5) | collective-permute-done | bytes 262176 | tf_op jit(solution)/shard_map/ppermute | solution.py:202
  38.5 2.1 %shard_map.104.early = f32[512,512]{1,0:T(8,128)S(1)} custom-call(s32[4,8]{1,0:T(4,128)S(1)} %pad_add_fusion.info, bf16[6,512,256]{2,1,0:T(8,128)(2,1)S(1)} %copy-done.6, bf16[512,512]{1,0:T(8,128)(2,1)S(1)} %copy-done, bf16[512,512]{1,0:T(8,128)(2,1)S(1)} %collective-permute-done.2.partner, bf16[256,512]{1,0:T(8,128)(2,1)} %collective-permute-done.3.rest_0_, ...), custom_call_target="tpu_custom_call" | custom-call | flops 805306368 | bytes 4456576 | tf_op jit(solution)/shard_map/pallas_call | solution.py:37
  40.6 3.4 %collective-permute-done.6.rest_0_ = bf16[256,512]{1,0:T(8,128)(2,1)S(1)} collective-permute-done((bf16[256,512]{1,0:T(8,128)(2,1)S(1)}, bf16[256,512]{1,0:T(8,128)(2,1)S(1)}, u32[]{:S(2)}, u32[]{:S(2)}) %collective-permute-start.6) | collective-permute-done | bytes 262176 | tf_op jit(solution)/shard_map/ppermute | solution.py:202
  44.0 4.3 %collective-permute-done.8.rest_2_ = bf16[256,512]{1,0:T(8,128)(2,1)S(1)} collective-permute-done((bf16[256,512]{1,0:T(8,128)(2,1)S(1)}, bf16[256,512]{1,0:T(8,128)(2,1)S(1)}, u32[]{:S(2)}, u32[]{:S(2)}) %collective-permute-start.8) | collective-permute-done | bytes 262176 | tf_op jit(solution)/shard_map/ppermute | solution.py:202
  51.1 2.4 %shard_map.106 = (bf16[256,1024]{1,0:T(8,128)(2,1)S(1)}, bf16[256,512]{1,0:T(8,128)(2,1)}, bf16[256,512]{1,0:T(8,128)(2,1)}) custom-call(s32[4,8]{1,0:T(4,128)S(1)} %pad_add_fusion.info, f32[256,1024]{1,0:T(8,128)S(1)} %convolution_add_fusion.self_part, bf16[512,512]{1,0:T(8,128)(2,1)S(1)} %get-tuple-element.42.agg, ...), custom_call_target="tpu_custom_call" | custom-call | flops 536870912 | bytes 5505152 | tf_op jit(solution)/shard_map/pallas_call | solution.py:37
  53.7 1.8 %collective-permute-done.12.slope_in = bf16[256,1024]{1,0:T(8,128)(2,1)S(1)} collective-permute-done((bf16[256,1024]{1,0:T(8,128)(2,1)S(1)}, bf16[256,1024]{1,0:T(8,128)(2,1)S(1)}, u32[]{:S(2)}, u32[]{:S(2)}) %collective-permute-start.12) | collective-permute-done | bytes 524320 | tf_op jit(solution)/shard_map/ppermute | solution.py:199
  55.5 3.7 %shard_map.107 = (bf16[512,1024]{1,0:T(8,128)(2,1)}, bf16[512,512]{1,0:T(8,128)(2,1)}, f32[256,512]{1,0:T(8,128)}, bf16[256,512]{1,0:T(8,128)(2,1)}, bf16[256,51...) custom-call(s32[4,8]{1,0:T(4,128)S(1)} %pad_add_fusion.info, ...), custom_call_target="tpu_custom_call" | custom-call | flops 1476395008 | bytes 8128640 | tf_op jit(solution)/shard_map/pallas_call | solution.py:37
  60.5 2.2 %collective-permute-start.15 = (bf16[256,512]{1,0:T(8,128)(2,1)}, bf16[256,512]{1,0:T(8,128)(2,1)}, u32[]{:S(2)}, u32[]{:S(2)}) collective-permute-start(bf16[256,512]{1,0:T(8,128)(2,1)} %get-tuple-element.54), channel_id=1, source_target_pairs={{0,6},{2,4},{4,2},{6,0},{8,14},{10,12},{12,10},{14,8},{1,7},{3,5},... | collective-permute-start | bytes 786440 | tf_op jit(solution)/shard_map/ppermute | solution.py:202
  67.1 2.0 %shard_map.108 = (f32[4,512,128]{2,1,0:T(8,128)S(1)}, bf16[4,512,128]{2,1,0:T(8,128)(2,1)S(1)}, f32[4,512,128]{2,1,0:T(8,128)S(1)}, bf16[4,512,128]{2,1,0:T(8,128)(2,1)S(1)}) custom-call(s32[4,8]{1,0:T(4,128)S(1)} %pad_add_fusion.info, bf16[512,1024]{1,0:T(8,128)(2,1)S(1)} %copy-done.7, bf16[512,512]{1,0:T(8,128)(2,1)S(1)} %bitcast.22, ...), custom_call_target="tpu_custom_call" | custom-call | flops 1073741824 | bytes 5243008 | tf_op jit(solution)/shard_map/pallas_call | solution.py:37
  70.1 4.7 %collective-permute-done.15.rest_2_ = bf16[256,512]{1,0:T(8,128)(2,1)} collective-permute-done((bf16[256,512]{1,0:T(8,128)(2,1)}, bf16[256,512]{1,0:T(8,128)(2,1)}, u32[]{:S(2)}, u32[]{:S(2)}) %collective-permute-start.15) | collective-permute-done | bytes 262176 | tf_op jit(solution)/shard_map/ppermute | solution.py:202
  78.9 1.7 %collective-permute-start.20 = (bf16[256,512]{1,0:T(8,128)(2,1)S(1)}, bf16[256,512]{1,0:T(8,128)(2,1)S(1)}, u32[]{:S(2)}, u32[]{:S(2)}) collective-permute-start(bf16[256,512]{1,0:T(8,128)(2,1)S(1)} %copy-done.27), channel_id=1, source_target_pairs={{0,4},{2,6},{4,0},{6,2},{8,12},{10,14},{12,8},{14,10},{1,5},{3,7},... | collective-permute-start | bytes 786440 | tf_op jit(solution)/shard_map/ppermute | solution.py:202
  82.4 11.9 %collective-permute-done.17 = bf16[4,512,128]{2,1,0:T(8,128)(2,1)S(1)} collective-permute-done((bf16[4,512,128]{2,1,0:T(8,128)(2,1)S(1)}, bf16[4,512,128]{2,1,0:T(8,128)(2,1)S(1)}, u32[]{:S(2)}, u32[]{:S(2)}) %collective-permute-start.17) | collective-permute-done | bytes 524320 | tf_op jit(solution)/shard_map/ppermute | solution.py:202
  94.6 2.3 %collective-permute-done.20.rest_1_ = bf16[256,512]{1,0:T(8,128)(2,1)S(1)} collective-permute-done((bf16[256,512]{1,0:T(8,128)(2,1)S(1)}, bf16[256,512]{1,0:T(8,128)(2,1)S(1)}, u32[]{:S(2)}, u32[]{:S(2)}) %collective-permute-start.20) | collective-permute-done | bytes 262176 | tf_op jit(solution)/shard_map/ppermute | solution.py:202
  96.9 7.2 %collective-permute-done.21.rest_2_ = bf16[256,512]{1,0:T(8,128)(2,1)S(1)} collective-permute-done((bf16[256,512]{1,0:T(8,128)(2,1)S(1)}, bf16[256,512]{1,0:T(8,128)(2,1)S(1)}, u32[]{:S(2)}, u32[]{:S(2)}) %collective-permute-start.21) | collective-permute-done | bytes 262176 | tf_op jit(solution)/shard_map/ppermute | solution.py:202
  106.5 1.7 %collective-permute-done.18 = bf16[2,512,128]{2,1,0:T(8,128)(2,1)S(1)} collective-permute-done((bf16[2,512,128]{2,1,0:T(8,128)(2,1)S(1)}, bf16[2,512,128]{2,1,0:T(8,128)(2,1)S(1)}, u32[]{:S(2)}, u32[]{:S(2)}) %collective-permute-start.18) | collective-permute-done | bytes 262176 | tf_op jit(solution)/shard_map/ppermute | solution.py:202
  109.0 2.3 %collective-permute-start.24 = (bf16[1,512,128]{2,1,0:T(8,128)(2,1)S(1)}, bf16[1,512,128]{2,1,0:T(8,128)(2,1)S(1)}, u32[]{:S(2)}, u32[]{:S(2)}) collective-permute-start(bf16[1,512,128]{2,1,0:T(8,128)(2,1)S(1)} %slice.109), channel_id=1, source_target_pairs={{0,8},{2,10},{4,12},{6,14},{8,0},{10,2},{12,4},{14,6},{1,9},{3,11}... | collective-permute-start | bytes 393224 | tf_op jit(solution)/shard_map/ppermute | solution.py:202
  114.0 1.7 %shard_map.111 = bf16[512,512]{1,0:T(8,128)(2,1)} custom-call(s32[4,8]{1,0:T(4,128)S(1)} %pad_add_fusion.info, f32[512,512]{1,0:T(8,128)S(1)} %shard_map.110.base, bf16[512,512]{1,0:T(8,128)(2,1)S(1)} %collective-permute-done.19.partner, bf16[256,512]{1,0:T(8,128)(2,1)S(1)} %collective-permute-done.23.rest_0_, ...), custom_call_target="tpu_custom_call" | custom-call | bytes 2883712 | tf_op jit(solution)/shard_map/pallas_call | solution.py:37
  115.7 2.2 %collective-permute-done.25 = bf16[2,512,128]{2,1,0:T(8,128)(2,1)S(1)} collective-permute-done((bf16[2,512,128]{2,1,0:T(8,128)(2,1)S(1)}, bf16[2,512,128]{2,1,0:T(8,128)(2,1)S(1)}, u32[]{:S(2)}, u32[]{:S(2)}) %collective-permute-start.25) | collective-permute-done | bytes 262176 | tf_op jit(solution)/shard_map/ppermute | solution.py:202
  118.0 1.9 %collective-permute-start.26 = (bf16[1,512,128]{2,1,0:T(8,128)(2,1)S(1)}, bf16[1,512,128]{2,1,0:T(8,128)(2,1)S(1)}, u32[]{:S(2)}, u32[]{:S(2)}) collective-permute-start(bf16[1,512,128]{2,1,0:T(8,128)(2,1)S(1)} %slice.108), channel_id=1, source_target_pairs={{0,8},{2,10},{4,12},{6,14},{8,0},{10,2},{12,4},{14,6},{1,9},{3,11}... | collective-permute-start | bytes 393224 | tf_op jit(solution)/shard_map/ppermute | solution.py:202
  120.6 6.1 %collective-permute-done.26 = bf16[1,512,128]{2,1,0:T(8,128)(2,1)S(1)} collective-permute-done((bf16[1,512,128]{2,1,0:T(8,128)(2,1)S(1)}, bf16[1,512,128]{2,1,0:T(8,128)(2,1)S(1)}, u32[]{:S(2)}, u32[]{:S(2)}) %collective-permute-start.26) | collective-permute-done | bytes 131104 | tf_op jit(solution)/shard_map/ppermute | solution.py:202
  (135 shorter events, 41.4 us)
Async XLA Ops:
  0.7 30.1 %collective-permute-start.2 = (bf16[512,512]{1,0:T(8,128)(2,1)}, bf16[512,512]{1,0:T(8,128)(2,1)S(1)}, u32[]{:S(2)}, u32[]{:S(2)}) collective-permute-start(bf16[512,512]{1,0:T(8,128)(2,1)} %own.1), channel_id=1, source_target_pairs={{0,8},{2,10},{4,12},{6,14},{8,0},{10,2},{12,4},{14,6},{1,9},{3,11}... | collective-permute-start | bytes 1572872 | tf_op jit(solution)/shard_map/ppermute | solution.py:202
  11.2 16.9 %collective-permute-start = (bf16[256,512]{1,0:T(8,128)(2,1)}, bf16[256,512]{1,0:T(8,128)(2,1)}, u32[]{:S(2)}, u32[]{:S(2)}) collective-permute-start(bf16[256,512]{1,0:T(8,128)(2,1)} %get-tuple-element.88), channel_id=1, source_target_pairs={{0,1},{1,0},{2,3},{3,2},{4,5},{5,4},{6,7},{7,6},{8,9},{9,8},{10,11... | collective-permute-start | bytes 786440 | tf_op jit(solution)/shard_map/ppermute | solution.py:199
  11.3 17.7 %collective-permute-start.1 = (bf16[512,1024]{1,0:T(8,128)(2,1)}, bf16[512,1024]{1,0:T(8,128)(2,1)}, u32[]{:S(2)}, u32[]{:S(2)}) collective-permute-start(bf16[512,1024]{1,0:T(8,128)(2,1)} %w_self.1), channel_id=1, source_target_pairs={{0,1},{1,0},{2,3},{3,2},{4,5},{5,4},{6,7},{7,6},{8,9},{9,8},{10,11... | collective-permute-start | bytes 3145736 | tf_op jit(solution)/shard_map/ppermute | solution.py:199
  11.8 20.5 %collective-permute-start.3 = (bf16[256,512]{1,0:T(8,128)(2,1)}, bf16[256,512]{1,0:T(8,128)(2,1)}, u32[]{:S(2)}, u32[]{:S(2)}) collective-permute-start(bf16[256,512]{1,0:T(8,128)(2,1)} %get-tuple-element.87), channel_id=1, source_target_pairs={{0,2},{2,0},{4,6},{6,4},{8,10},{10,8},{12,14},{14,12},{1,3},{3,1},... | collective-permute-start | bytes 786440 | tf_op jit(solution)/shard_map/ppermute | solution.py:202
  13.1 20.7 %collective-permute-start.4 = (bf16[256,512]{1,0:T(8,128)(2,1)}, bf16[256,512]{1,0:T(8,128)(2,1)}, u32[]{:S(2)}, u32[]{:S(2)}) collective-permute-start(bf16[256,512]{1,0:T(8,128)(2,1)} %get-tuple-element.86), channel_id=1, source_target_pairs={{0,4},{2,6},{4,0},{6,2},{8,12},{10,14},{12,8},{14,10},{1,5},{3,7},... | collective-permute-start | bytes 786440 | tf_op jit(solution)/shard_map/ppermute | solution.py:202
  28.3 10.2 %collective-permute-start.5 = (bf16[256,512]{1,0:T(8,128)(2,1)S(1)}, bf16[256,512]{1,0:T(8,128)(2,1)S(1)}, u32[]{:S(2)}, u32[]{:S(2)}) collective-permute-start(bf16[256,512]{1,0:T(8,128)(2,1)S(1)} %copy-done.21), channel_id=1, source_target_pairs={{0,6},{2,4},{4,2},{6,0},{8,14},{10,12},{12,10},{14,8},{1,7},{3,5},... | collective-permute-start | bytes 786440 | tf_op jit(solution)/shard_map/ppermute | solution.py:202
  28.9 20.7 %collective-permute-start.10 = (bf16[512,1024]{1,0:T(8,128)(2,1)S(1)}, bf16[512,1024]{1,0:T(8,128)(2,1)S(1)}, u32[]{:S(2)}, u32[]{:S(2)}) collective-permute-start(bf16[512,1024]{1,0:T(8,128)(2,1)S(1)} %copy-done.9), channel_id=1, source_target_pairs={{0,1},{1,0},{2,3},{3,2},{4,5},{5,4},{6,7},{7,6},{8,9},{9,8},{10,11... | collective-permute-start | bytes 3145736 | tf_op jit(solution)/shard_map/ppermute | solution.py:199
  30.8 13.2 %collective-permute-start.6 = (bf16[256,512]{1,0:T(8,128)(2,1)S(1)}, bf16[256,512]{1,0:T(8,128)(2,1)S(1)}, u32[]{:S(2)}, u32[]{:S(2)}) collective-permute-start(bf16[256,512]{1,0:T(8,128)(2,1)S(1)} %get-tuple-element.84), channel_id=1, source_target_pairs={{0,2},{2,0},{4,6},{6,4},{8,10},{10,8},{12,14},{14,12},{1,3},{3,1},... | collective-permute-start | bytes 786440 | tf_op jit(solution)/shard_map/ppermute | solution.py:202
  32.2 11.8 %collective-permute-start.7 = (bf16[256,512]{1,0:T(8,128)(2,1)S(1)}, bf16[256,512]{1,0:T(8,128)(2,1)S(1)}, u32[]{:S(2)}, u32[]{:S(2)}) collective-permute-start(bf16[256,512]{1,0:T(8,128)(2,1)S(1)} %get-tuple-element.83), channel_id=1, source_target_pairs={{0,4},{2,6},{4,0},{6,2},{8,12},{10,14},{12,8},{14,10},{1,5},{3,7},... | collective-permute-start | bytes 786440 | tf_op jit(solution)/shard_map/ppermute | solution.py:202
  33.8 14.6 %collective-permute-start.8 = (bf16[256,512]{1,0:T(8,128)(2,1)S(1)}, bf16[256,512]{1,0:T(8,128)(2,1)S(1)}, u32[]{:S(2)}, u32[]{:S(2)}) collective-permute-start(bf16[256,512]{1,0:T(8,128)(2,1)S(1)} %get-tuple-element.82), channel_id=1, source_target_pairs={{0,6},{2,4},{4,2},{6,0},{8,14},{10,12},{12,10},{14,8},{1,7},{3,5},... | collective-permute-start | bytes 786440 | tf_op jit(solution)/shard_map/ppermute | solution.py:202
  38.5 11.1 %collective-permute-start.11 = (bf16[256,512]{1,0:T(8,128)(2,1)S(1)}, bf16[256,512]{1,0:T(8,128)(2,1)S(1)}, u32[]{:S(2)}, u32[]{:S(2)}) collective-permute-start(bf16[256,512]{1,0:T(8,128)(2,1)S(1)} %get-tuple-element.80), channel_id=1, source_target_pairs={{0,1},{1,0},{2,3},{3,2},{4,5},{5,4},{6,7},{7,6},{8,9},{9,8},{10,11... | collective-permute-start | bytes 786440 | tf_op jit(solution)/shard_map/ppermute | solution.py:199
  59.2 9.9 %collective-permute-start.13 = (bf16[256,512]{1,0:T(8,128)(2,1)}, bf16[256,512]{1,0:T(8,128)(2,1)S(1)}, u32[]{:S(2)}, u32[]{:S(2)}) collective-permute-start(bf16[256,512]{1,0:T(8,128)(2,1)} %get-tuple-element.52), channel_id=1, source_target_pairs={{0,2},{2,0},{4,6},{6,4},{8,10},{10,8},{12,14},{14,12},{1,3},{3,1},... | collective-permute-start | bytes 786440 | tf_op jit(solution)/shard_map/ppermute | solution.py:202
  60.5 9.5 %collective-permute-start.14 = (bf16[256,512]{1,0:T(8,128)(2,1)}, bf16[256,512]{1,0:T(8,128)(2,1)}, u32[]{:S(2)}, u32[]{:S(2)}) collective-permute-start(bf16[256,512]{1,0:T(8,128)(2,1)} %get-tuple-element.53), channel_id=1, source_target_pairs={{0,4},{2,6},{4,0},{6,2},{8,12},{10,14},{12,8},{14,10},{1,5},{3,7},... | collective-permute-start | bytes 786440 | tf_op jit(solution)/shard_map/ppermute | solution.py:202
  60.5 14.2 %collective-permute-start.15 = (bf16[256,512]{1,0:T(8,128)(2,1)}, bf16[256,512]{1,0:T(8,128)(2,1)}, u32[]{:S(2)}, u32[]{:S(2)}) collective-permute-start(bf16[256,512]{1,0:T(8,128)(2,1)} %get-tuple-element.54), channel_id=1, source_target_pairs={{0,6},{2,4},{4,2},{6,0},{8,14},{10,12},{12,10},{14,8},{1,7},{3,5},... | collective-permute-start | bytes 786440 | tf_op jit(solution)/shard_map/ppermute | solution.py:202
  74.7 19.6 %collective-permute-start.17 = (bf16[4,512,128]{2,1,0:T(8,128)(2,1)S(1)}, bf16[4,512,128]{2,1,0:T(8,128)(2,1)S(1)}, u32[]{:S(2)}, u32[]{:S(2)}) collective-permute-start(bf16[4,512,128]{2,1,0:T(8,128)(2,1)S(1)} %get-tuple-element.58), channel_id=1, source_target_pairs={{0,2},{2,0},{4,6},{6,4},{8,10},{10,8},{12,14},{14,12},{1,3},{3,1},... | collective-permute-start | bytes 1572872 | tf_op jit(solution)/shard_map/ppermute | solution.py:202
  77.4 28.4 %collective-permute-start.19 = (bf16[512,512]{1,0:T(8,128)(2,1)S(1)}, bf16[512,512]{1,0:T(8,128)(2,1)S(1)}, u32[]{:S(2)}, u32[]{:S(2)}) collective-permute-start(bf16[512,512]{1,0:T(8,128)(2,1)S(1)} %shard_map.109), channel_id=1, source_target_pairs={{0,8},{2,10},{4,12},{6,14},{8,0},{10,2},{12,4},{14,6},{1,9},{3,11}... | collective-permute-start | bytes 1572872 | tf_op jit(solution)/shard_map/ppermute | solution.py:202
  78.9 18.0 %collective-permute-start.20 = (bf16[256,512]{1,0:T(8,128)(2,1)S(1)}, bf16[256,512]{1,0:T(8,128)(2,1)S(1)}, u32[]{:S(2)}, u32[]{:S(2)}) collective-permute-start(bf16[256,512]{1,0:T(8,128)(2,1)S(1)} %copy-done.27), channel_id=1, source_target_pairs={{0,4},{2,6},{4,0},{6,2},{8,12},{10,14},{12,8},{14,10},{1,5},{3,7},... | collective-permute-start | bytes 786440 | tf_op jit(solution)/shard_map/ppermute | solution.py:202
  80.6 23.5 %collective-permute-start.21 = (bf16[256,512]{1,0:T(8,128)(2,1)S(1)}, bf16[256,512]{1,0:T(8,128)(2,1)S(1)}, u32[]{:S(2)}, u32[]{:S(2)}) collective-permute-start(bf16[256,512]{1,0:T(8,128)(2,1)S(1)} %copy-done.26), channel_id=1, source_target_pairs={{0,6},{2,4},{4,2},{6,0},{8,14},{10,12},{12,10},{14,8},{1,7},{3,5},... | collective-permute-start | bytes 786440 | tf_op jit(solution)/shard_map/ppermute | solution.py:202
  80.9 25.6 %collective-permute-start.16 = (bf16[4,512,128]{2,1,0:T(8,128)(2,1)S(1)}, bf16[4,512,128]{2,1,0:T(8,128)(2,1)S(1)}, u32[]{:S(2)}, u32[]{:S(2)}) collective-permute-start(bf16[4,512,128]{2,1,0:T(8,128)(2,1)S(1)} %get-tuple-element.55), channel_id=1, source_target_pairs={{0,2},{2,0},{4,6},{6,4},{8,10},{10,8},{12,14},{14,12},{1,3},{3,1},... | collective-permute-start | bytes 1572872 | tf_op jit(solution)/shard_map/ppermute | solution.py:202
  94.5 13.7 %collective-permute-start.18 = (bf16[2,512,128]{2,1,0:T(8,128)(2,1)S(1)}, bf16[2,512,128]{2,1,0:T(8,128)(2,1)S(1)}, u32[]{:S(2)}, u32[]{:S(2)}) collective-permute-start(bf16[2,512,128]{2,1,0:T(8,128)(2,1)S(1)} %slice.72), channel_id=1, source_target_pairs={{0,4},{2,6},{4,0},{6,2},{8,12},{10,14},{12,8},{14,10},{1,5},{3,7},... | collective-permute-start | bytes 786440 | tf_op jit(solution)/shard_map/ppermute | solution.py:202
  96.9 14.4 %collective-permute-start.22 = (bf16[256,512]{1,0:T(8,128)(2,1)S(1)}, bf16[256,512]{1,0:T(8,128)(2,1)S(1)}, u32[]{:S(2)}, u32[]{:S(2)}) collective-permute-start(bf16[256,512]{1,0:T(8,128)(2,1)S(1)} %copy-done.24), channel_id=1, source_target_pairs={{0,1},{1,0},{2,3},{3,2},{4,5},{5,4},{6,7},{7,6},{8,9},{9,8},{10,11... | collective-permute-start | bytes 786440 | tf_op jit(solution)/shard_map/ppermute | solution.py:199
  104.1 9.8 %collective-permute-start.23 = (bf16[256,512]{1,0:T(8,128)(2,1)S(1)}, bf16[256,512]{1,0:T(8,128)(2,1)S(1)}, u32[]{:S(2)}, u32[]{:S(2)}) collective-permute-start(bf16[256,512]{1,0:T(8,128)(2,1)S(1)} %copy-done.25), channel_id=1, source_target_pairs={{0,2},{2,0},{4,6},{6,4},{8,10},{10,8},{12,14},{14,12},{1,3},{3,1},... | collective-permute-start | bytes 786440 | tf_op jit(solution)/shard_map/ppermute | solution.py:202
  108.4 9.5 %collective-permute-start.25 = (bf16[2,512,128]{2,1,0:T(8,128)(2,1)S(1)}, bf16[2,512,128]{2,1,0:T(8,128)(2,1)S(1)}, u32[]{:S(2)}, u32[]{:S(2)}) collective-permute-start(bf16[2,512,128]{2,1,0:T(8,128)(2,1)S(1)} %slice.77), channel_id=1, source_target_pairs={{0,4},{2,6},{4,0},{6,2},{8,12},{10,14},{12,8},{14,10},{1,5},{3,7},... | collective-permute-start | bytes 786440 | tf_op jit(solution)/shard_map/ppermute | solution.py:202
  118.0 8.7 %collective-permute-start.26 = (bf16[1,512,128]{2,1,0:T(8,128)(2,1)S(1)}, bf16[1,512,128]{2,1,0:T(8,128)(2,1)S(1)}, u32[]{:S(2)}, u32[]{:S(2)}) collective-permute-start(bf16[1,512,128]{2,1,0:T(8,128)(2,1)S(1)} %slice.108), channel_id=1, source_target_pairs={{0,8},{2,10},{4,12},{6,14},{8,0},{10,2},{12,4},{14,6},{1,9},{3,11}... | collective-permute-start | bytes 393224 | tf_op jit(solution)/shard_map/ppermute | solution.py:202
  (31 other events, 162.9 us)

commit v4 on v3

--- a/solution.py
+++ b/solution.py
@@ -101,7 +101,7 @@
     away[...] = out[block(1 - info[3, 0]), :]
 
 
-def slope_kernel(info, self_part, agg, agg_in, w_own, w_other, cot_own, cot_in, slope, keep, away, cot, hid, sems):
+def slope_kernel(info, self_part, agg, agg_in, w_own, w_other, cot_own, cot_in, slope, halves, cot, hid, sems):
     feat = info[3, 0]
     width = cot_own.shape[1]
     mine = pl.ds(pl.multiple_of(feat * width, width), width)
@@ -110,18 +110,18 @@
     cot[:, other] = cot_in[...]
     own_rows = agg[block(feat), :]
     step = 256
+    copies = []
     for c in range(0, slope.shape[1], step):
         cols = slice(c, c + step)
         pre = self_part[:, cols] + mul(own_rows, w_own[:, cols]) + mul(agg_in[...], w_other[:, cols])
         s = jax.nn.sigmoid(pre)
         hid[:, cols] = (pre * s).astype(BF16)
         slope[:, cols] = (cot[:, cols].astype(F32) * s * (1.0 + pre * (1.0 - s))).astype(BF16)
-    copies = [
-        pltpu.make_async_copy(hid.at[:, mine], keep, sems.at[0]),
-        pltpu.make_async_copy(hid.at[:, other], away, sems.at[1]),
-    ]
-    for copy in copies:
-        copy.start()
+        if (c + step) % width == 0:
+            half = c // width
+            source = hid.at[:, half * width : (half + 1) * width]
+            copies.append(pltpu.make_async_copy(source, halves.at[jnp.bitwise_xor(half, feat)], sems.at[half]))
+            copies[-1].start()
     for copy in copies:
         copy.wait()
 
@@ -129,19 +129,23 @@
 def pieces_kernel(count, info, slope_own, slope_in, w_neigh, inverse, early, late, slope_out, scaled_out, partner_out, *rest):
     *outs, held, slope, scaled, partner, sems = rest
     feat = info[3, 0]
+    copies = []
+
+    def send(source, out):
+        copies.append(pltpu.make_async_copy(source, out, sems.at[len(copies)]))
+        copies[-1].start()
+
     slope[block(feat), :] = slope_own[...]
     slope[block(1 - feat), :] = slope_in[...]
+    send(slope, slope_out)
     scaled[...] = (mul(slope[...], w_neigh[...], COLS_BY_COLS) * inverse[...]).astype(BF16)
-    copies = []
+    send(scaled, scaled_out)
+    partner[...] = mul(early[2 + count], scaled[...])
+    send(partner, partner_out)
     for k in range(2 * count):
         matrix = late[k] if k < count else early[2 + k - count]
         held[k] = mul(matrix, scaled[...]).astype(BF16)
-        copies.append(pltpu.make_async_copy(held.at[k], outs[k], sems.at[k]))
-        copies[k].start()
-    partner[...] = mul(early[2 + count], scaled[...])
-    for k, (source, out) in enumerate(((slope, slope_out), (scaled, scaled_out), (partner, partner_out))):
-        copies.append(pltpu.make_async_copy(source, out, sems.at[2 * count + k]))
-        copies[-1].start()
+        send(held.at[k], outs[k])
     for copy in copies:
         copy.wait()
 
@@ -259,13 +263,13 @@
     )
     agg_in = swap(agg_away)
     agg_t = agg.T
-    slope_own, hid_keep, hid_away = local_call(
+    slope_own, hid_halves = local_call(
         slope_kernel,
-        [shape((TILE, hidden_width), BF16), shape((TILE, width), BF16), shape((TILE, width), BF16)],
+        [shape((TILE, hidden_width), BF16), shape((2, TILE, width), BF16)],
         [info, self_part, agg, agg_in, w_neigh, w_neigh_in, cot_own, cot_in],
         4 * TILE * width * hidden_width,
         [pltpu.VMEM((TILE, hidden_width), BF16)] * 2 + [pltpu.SemaphoreType.DMA((2,))],
-        in_hbm=(1, 2),
+        in_hbm=(1,),
     )
     slope_in = swap(slope_own)
 
@@ -329,7 +333,7 @@
             for left in (features_t, agg_t)
         )
 
-    hid_in = swap(after(hid_away, last))
+    hid_keep, hid_in = hid_halves[0], swap(after(hid_halves[1], last))
     hidden = jnp.where(feat == 0, jnp.concatenate([hid_keep, hid_in]), jnp.concatenate([hid_in, hid_keep]))
 
     (base,) = local_call(

time: 128 us -> 127 us (level)
  waiting for transfers between devices: 53 us -> 51.6 us
    ppermute x20, waiting for transfers between devices: 49.7 us -> 48.3 us  [hop(): return lax.ppermute(x, 'node', [(i, i ^ k) for i in range(nodes)])]
    unnamed x58 -> x56, local copies, waits for them, and re-layouts: 9.42 us -> 10.2 us
where the time goes in v4:
time: 127 us
  waiting for transfers between devices  51.6 us (41%)
  starting transfers between devices  28.9 us (23%)
  Pallas kernels  19.8 us (16%)
  local copies, waits for them, and re-layouts  13.1 us (10%)
  other arithmetic  6.16 us (5%)
  between operations  4.93 us (4%)
  matrix products  2.24 us (2%)
    ppermute x20, waiting for transfers between devices, hop(): return lax.ppermute(x, 'node', [(i, i ^ k) for i in range(nodes)])  48.3 us
    ppermute x20, starting transfers between devices, hop(): return lax.ppermute(x, 'node', [(i, i ^ k) for i in range(nodes)])  28.1 us
    pallas_call x8, Pallas kernels, local_call(): pl.pallas_call(kernel, out_shape=placed, in_specs=[SMEM] * scalars + [VME...  15.3 us
    unnamed x56, local copies, waits for them, and re-layouts  10.2 us
    pallas_call x2, Pallas kernels, combine(): pl.pallas_call(kernel, grid=(count,), out_shape=[jax.ShapeDtypeStruct((co...  4.52 us
    ppermute x7, waiting for transfers between devices, swap(): return lax.ppermute(x, 'feat', [(0, 1), (1, 0)])  3.29 us
  transfers between devices with their start and end apart: 27, of which 14 were waited for; matrix products, arithmetic and copies ran while one was open for 10% of the time, Pallas kernels for 11%

profile of v4, /device:TPU:0, one launch (start us, length us, event | category | flops | bytes accessed | tf_op | source)
XLA Modules:
  0.0 126.7 jit_solution(14249908425456603042)
XLA Ops:
  0.7 4.1 %collective-permute-start.2 = (bf16[512,512]{1,0:T(8,128)(2,1)}, bf16[512,512]{1,0:T(8,128)(2,1)S(1)}, u32[]{:S(2)}, u32[]{:S(2)}) collective-permute-start(bf16[512,512]{1,0:T(8,128)(2,1)} %own.1), channel_id=1, source_target_pairs={{0,8},{2,10},{4,12},{6,14},{8,0},{10,2},{12,4},{14,6},{1,9},{3,11}... | collective-permute-start | bytes 1572872 | tf_op jit(solution)/shard_map/ppermute | solution.py:206
  8.7 2.4 %constant_dynamic-slice_fusion.3 = (bf16[256,512]{1,0:T(8,128)(2,1)}, bf16[256,512]{1,0:T(8,128)(2,1)}, bf16[256,512]{1,0:T(8,128)(2,1)}, bf16[256,512]{1,0:T(8,128)(2,1)}) fusion(bf16[512,512]{1,0:T(8,128)(2,1)} %own.1, s32[]{:T(128)S(6)} %select_n.86, s32[]{:T(128)S(6)} %select_n.85, s32[]{:T(128)S(6)} %select_n.84, pred[]{:T(512)S(6)} %eq.85), kind=kLoop, calls=%fused_computation.37 | loop fusion | flops 131072 | bytes 2359309 | tf_op jit(solution)/shard_map/dynamic_slice | solution.py:233
  18.4 2.9 %shard_map.103 = (bf16[6,512,256]{2,1,0:T(8,128)(2,1)S(1)}, bf16[6,256,512]{2,1,0:T(8,128)(2,1)S(1)}) custom-call(s32[16]{0:T(128)S(1)} %compare_select_fusion.code_ref, bf16[2,8,256,256]{3,2,1,0:T(8,128)(2,1)S(1)} %copy-done.1), custom_call_target="tpu_custom_call" | custom-call | bytes 5242880 | tf_op jit(solution)/shard_map/pallas_call | solution.py:66
  28.8 1.8 %convolution_add_fusion.self_part = f32[256,1024]{1,0:T(8,128)S(1)} fusion(f32[256,1024]{1,0:T(8,128)S(1)} %fusion.2, bf16[256,512]{1,0:T(8,128)(2,1)} %collective-permute-done, bf16[512,1024]{1,0:T(8,128)(2,1)} %collective-permute-done.1), kind=kOutput, calls=%fused_computation | convolution fusion | flops 268697600 | bytes 3407872 | tf_op jit(solution)/shard_map/dot_general | solution.py:21
  34.3 4.2 %collective-permute-done.5.rest_2_ = bf16[256,512]{1,0:T(8,128)(2,1)S(1)} collective-permute-done((bf16[256,512]{1,0:T(8,128)(2,1)S(1)}, bf16[256,512]{1,0:T(8,128)(2,1)S(1)}, u32[]{:S(2)}, u32[]{:S(2)}) %collective-permute-start.5) | collective-permute-done | bytes 262176 | tf_op jit(solution)/shard_map/ppermute | solution.py:206
  38.5 2.1 %shard_map.104.early = f32[512,512]{1,0:T(8,128)S(1)} custom-call(s32[4,8]{1,0:T(4,128)S(1)} %pad_add_fusion.info, bf16[6,512,256]{2,1,0:T(8,128)(2,1)S(1)} %copy-done.6, bf16[512,512]{1,0:T(8,128)(2,1)S(1)} %copy-done, bf16[512,512]{1,0:T(8,128)(2,1)S(1)} %collective-permute-done.2.partner, bf16[256,512]{1,0:T(8,128)(2,1)} %collective-permute-done.3.rest_0_, ...), custom_call_target="tpu_custom_call" | custom-call | flops 805306368 | bytes 4456576 | tf_op jit(solution)/shard_map/pallas_call | solution.py:37
  40.6 3.5 %collective-permute-done.6.rest_0_ = bf16[256,512]{1,0:T(8,128)(2,1)S(1)} collective-permute-done((bf16[256,512]{1,0:T(8,128)(2,1)S(1)}, bf16[256,512]{1,0:T(8,128)(2,1)S(1)}, u32[]{:S(2)}, u32[]{:S(2)}) %collective-permute-start.6) | collective-permute-done | bytes 262176 | tf_op jit(solution)/shard_map/ppermute | solution.py:206
  44.1 4.1 %collective-permute-done.8.rest_2_ = bf16[256,512]{1,0:T(8,128)(2,1)S(1)} collective-permute-done((bf16[256,512]{1,0:T(8,128)(2,1)S(1)}, bf16[256,512]{1,0:T(8,128)(2,1)S(1)}, u32[]{:S(2)}, u32[]{:S(2)}) %collective-permute-start.8) | collective-permute-done | bytes 262176 | tf_op jit(solution)/shard_map/ppermute | solution.py:206
  51.0 2.3 %shard_map.106 = (bf16[256,1024]{1,0:T(8,128)(2,1)S(1)}, bf16[2,256,512]{2,1,0:T(8,128)(2,1)}) custom-call(s32[4,8]{1,0:T(4,128)S(1)} %pad_add_fusion.info, f32[256,1024]{1,0:T(8,128)S(1)} %convolution_add_fusion.self_part, bf16[512,512]{1,0:T(8,128)(2,1)S(1)} %get-tuple-element.41.agg, bf16[256,512]{1,0:T(8,128)(2,1)S(1)} %collective-permute-done.9.agg_in, ...), custom_call_target="tpu_custom_call" | custom-call | flops 536870912 | bytes 5505152 | tf_op jit(solution)/shard_map/pallas_call | solution.py:37
  53.5 1.8 %collective-permute-done.12.slope_in = bf16[256,1024]{1,0:T(8,128)(2,1)S(1)} collective-permute-done((bf16[256,1024]{1,0:T(8,128)(2,1)S(1)}, bf16[256,1024]{1,0:T(8,128)(2,1)S(1)}, u32[]{:S(2)}, u32[]{:S(2)}) %collective-permute-start.12) | collective-permute-done | bytes 524320 | tf_op jit(solution)/shard_map/ppermute | solution.py:203
  55.2 3.2 %shard_map.107 = (bf16[512,1024]{1,0:T(8,128)(2,1)}, bf16[512,512]{1,0:T(8,128)(2,1)}, f32[256,512]{1,0:T(8,128)}, bf16[256,512]{1,0:T(8,128)(2,1)}, bf16[256,51...) custom-call(s32[4,8]{1,0:T(4,128)S(1)} %pad_add_fusion.info, ...), custom_call_target="tpu_custom_call" | custom-call | flops 1476395008 | bytes 8128640 | tf_op jit(solution)/shard_map/pallas_call | solution.py:37
  60.0 2.0 %collective-permute-start.15 = (bf16[256,512]{1,0:T(8,128)(2,1)}, bf16[256,512]{1,0:T(8,128)(2,1)}, u32[]{:S(2)}, u32[]{:S(2)}) collective-permute-start(bf16[256,512]{1,0:T(8,128)(2,1)} %get-tuple-element.52), channel_id=1, source_target_pairs={{0,6},{2,4},{4,2},{6,0},{8,14},{10,12},{12,10},{14,8},{1,7},{3,5},... | collective-permute-start | bytes 786440 | tf_op jit(solution)/shard_map/ppermute | solution.py:206
  66.3 2.0 %shard_map.108 = (f32[4,512,128]{2,1,0:T(8,128)S(1)}, bf16[4,512,128]{2,1,0:T(8,128)(2,1)S(1)}, f32[4,512,128]{2,1,0:T(8,128)S(1)}, bf16[4,512,128]{2,1,0:T(8,128)(2,1)S(1)}) custom-call(s32[4,8]{1,0:T(4,128)S(1)} %pad_add_fusion.info, bf16[512,1024]{1,0:T(8,128)(2,1)S(1)} %copy-done.7, bf16[512,512]{1,0:T(8,128)(2,1)S(1)} %bitcast.26, ...), custom_call_target="tpu_custom_call" | custom-call | flops 1073741824 | bytes 5243008 | tf_op jit(solution)/shard_map/pallas_call | solution.py:37
  69.5 4.5 %collective-permute-done.15.rest_2_ = bf16[256,512]{1,0:T(8,128)(2,1)} collective-permute-done((bf16[256,512]{1,0:T(8,128)(2,1)}, bf16[256,512]{1,0:T(8,128)(2,1)}, u32[]{:S(2)}, u32[]{:S(2)}) %collective-permute-start.15) | collective-permute-done | bytes 262176 | tf_op jit(solution)/shard_map/ppermute | solution.py:206
  78.3 1.7 %collective-permute-start.20 = (bf16[256,512]{1,0:T(8,128)(2,1)S(1)}, bf16[256,512]{1,0:T(8,128)(2,1)S(1)}, u32[]{:S(2)}, u32[]{:S(2)}) collective-permute-start(bf16[256,512]{1,0:T(8,128)(2,1)S(1)} %copy-done.26), channel_id=1, source_target_pairs={{0,4},{2,6},{4,0},{6,2},{8,12},{10,14},{12,8},{14,10},{1,5},{3,7},... | collective-permute-start | bytes 786440 | tf_op jit(solution)/shard_map/ppermute | solution.py:206
  81.8 11.6 %collective-permute-done.17 = bf16[4,512,128]{2,1,0:T(8,128)(2,1)S(1)} collective-permute-done((bf16[4,512,128]{2,1,0:T(8,128)(2,1)S(1)}, bf16[4,512,128]{2,1,0:T(8,128)(2,1)S(1)}, u32[]{:S(2)}, u32[]{:S(2)}) %collective-permute-start.17) | collective-permute-done | bytes 524320 | tf_op jit(solution)/shard_map/ppermute | solution.py:206
  94.5 1.8 %collective-permute-done.20.rest_1_ = bf16[256,512]{1,0:T(8,128)(2,1)S(1)} collective-permute-done((bf16[256,512]{1,0:T(8,128)(2,1)S(1)}, bf16[256,512]{1,0:T(8,128)(2,1)S(1)}, u32[]{:S(2)}, u32[]{:S(2)}) %collective-permute-start.20) | collective-permute-done | bytes 262176 | tf_op jit(solution)/shard_map/ppermute | solution.py:206
  96.3 7.2 %collective-permute-done.21.rest_2_ = bf16[256,512]{1,0:T(8,128)(2,1)S(1)} collective-permute-done((bf16[256,512]{1,0:T(8,128)(2,1)S(1)}, bf16[256,512]{1,0:T(8,128)(2,1)S(1)}, u32[]{:S(2)}, u32[]{:S(2)}) %collective-permute-start.21) | collective-permute-done | bytes 262176 | tf_op jit(solution)/shard_map/ppermute | solution.py:206
  103.5 1.8 %collective-permute-start.23 = (bf16[256,512]{1,0:T(8,128)(2,1)S(1)}, bf16[256,512]{1,0:T(8,128)(2,1)S(1)}, u32[]{:S(2)}, u32[]{:S(2)}) collective-permute-start(bf16[256,512]{1,0:T(8,128)(2,1)S(1)} %copy-done.24), channel_id=1, source_target_pairs={{0,2},{2,0},{4,6},{6,4},{8,10},{10,8},{12,14},{14,12},{1,3},{3,1},... | collective-permute-start | bytes 786440 | tf_op jit(solution)/shard_map/ppermute | solution.py:206
  105.4 2.2 %collective-permute-done.18 = bf16[2,512,128]{2,1,0:T(8,128)(2,1)S(1)} collective-permute-done((bf16[2,512,128]{2,1,0:T(8,128)(2,1)S(1)}, bf16[2,512,128]{2,1,0:T(8,128)(2,1)S(1)}, u32[]{:S(2)}, u32[]{:S(2)}) %collective-permute-start.18) | collective-permute-done | bytes 262176 | tf_op jit(solution)/shard_map/ppermute | solution.py:206
  108.4 2.3 %collective-permute-start.24 = (bf16[1,512,128]{2,1,0:T(8,128)(2,1)S(1)}, bf16[1,512,128]{2,1,0:T(8,128)(2,1)S(1)}, u32[]{:S(2)}, u32[]{:S(2)}) collective-permute-start(bf16[1,512,128]{2,1,0:T(8,128)(2,1)S(1)} %slice.119), channel_id=1, source_target_pairs={{0,8},{2,10},{4,12},{6,14},{8,0},{10,2},{12,4},{14,6},{1,9},{3,11}... | collective-permute-start | bytes 393224 | tf_op jit(solution)/shard_map/ppermute | solution.py:206
  115.1 2.1 %collective-permute-done.25 = bf16[2,512,128]{2,1,0:T(8,128)(2,1)S(1)} collective-permute-done((bf16[2,512,128]{2,1,0:T(8,128)(2,1)S(1)}, bf16[2,512,128]{2,1,0:T(8,128)(2,1)S(1)}, u32[]{:S(2)}, u32[]{:S(2)}) %collective-permute-start.25) | collective-permute-done | bytes 262176 | tf_op jit(solution)/shard_map/ppermute | solution.py:206
  117.2 2.1 %collective-permute-start.26 = (bf16[1,512,128]{2,1,0:T(8,128)(2,1)S(1)}, bf16[1,512,128]{2,1,0:T(8,128)(2,1)S(1)}, u32[]{:S(2)}, u32[]{:S(2)}) collective-permute-start(bf16[1,512,128]{2,1,0:T(8,128)(2,1)S(1)} %slice.118), channel_id=1, source_target_pairs={{0,8},{2,10},{4,12},{6,14},{8,0},{10,2},{12,4},{14,6},{1,9},{3,11}... | collective-permute-start | bytes 393224 | tf_op jit(solution)/shard_map/ppermute | solution.py:206
  120.0 5.9 %collective-permute-done.26 = bf16[1,512,128]{2,1,0:T(8,128)(2,1)S(1)} collective-permute-done((bf16[1,512,128]{2,1,0:T(8,128)(2,1)S(1)}, bf16[1,512,128]{2,1,0:T(8,128)(2,1)S(1)}, u32[]{:S(2)}, u32[]{:S(2)}) %collective-permute-start.26) | collective-permute-done | bytes 131104 | tf_op jit(solution)/shard_map/ppermute | solution.py:206
  (134 shorter events, 42.3 us)
Async XLA Ops:
  0.7 30.0 %collective-permute-start.2 = (bf16[512,512]{1,0:T(8,128)(2,1)}, bf16[512,512]{1,0:T(8,128)(2,1)S(1)}, u32[]{:S(2)}, u32[]{:S(2)}) collective-permute-start(bf16[512,512]{1,0:T(8,128)(2,1)} %own.1), channel_id=1, source_target_pairs={{0,8},{2,10},{4,12},{6,14},{8,0},{10,2},{12,4},{14,6},{1,9},{3,11}... | collective-permute-start | bytes 1572872 | tf_op jit(solution)/shard_map/ppermute | solution.py:206
  11.1 17.1 %collective-permute-start = (bf16[256,512]{1,0:T(8,128)(2,1)}, bf16[256,512]{1,0:T(8,128)(2,1)}, u32[]{:S(2)}, u32[]{:S(2)}) collective-permute-start(bf16[256,512]{1,0:T(8,128)(2,1)} %get-tuple-element.88), channel_id=1, source_target_pairs={{0,1},{1,0},{2,3},{3,2},{4,5},{5,4},{6,7},{7,6},{8,9},{9,8},{10,11... | collective-permute-start | bytes 786440 | tf_op jit(solution)/shard_map/ppermute | solution.py:203
  11.1 17.7 %collective-permute-start.1 = (bf16[512,1024]{1,0:T(8,128)(2,1)}, bf16[512,1024]{1,0:T(8,128)(2,1)}, u32[]{:S(2)}, u32[]{:S(2)}) collective-permute-start(bf16[512,1024]{1,0:T(8,128)(2,1)} %w_self.1), channel_id=1, source_target_pairs={{0,1},{1,0},{2,3},{3,2},{4,5},{5,4},{6,7},{7,6},{8,9},{9,8},{10,11... | collective-permute-start | bytes 3145736 | tf_op jit(solution)/shard_map/ppermute | solution.py:203
  11.6 20.7 %collective-permute-start.3 = (bf16[256,512]{1,0:T(8,128)(2,1)}, bf16[256,512]{1,0:T(8,128)(2,1)}, u32[]{:S(2)}, u32[]{:S(2)}) collective-permute-start(bf16[256,512]{1,0:T(8,128)(2,1)} %get-tuple-element.87), channel_id=1, source_target_pairs={{0,2},{2,0},{4,6},{6,4},{8,10},{10,8},{12,14},{14,12},{1,3},{3,1},... | collective-permute-start | bytes 786440 | tf_op jit(solution)/shard_map/ppermute | solution.py:206
  13.1 20.7 %collective-permute-start.4 = (bf16[256,512]{1,0:T(8,128)(2,1)}, bf16[256,512]{1,0:T(8,128)(2,1)}, u32[]{:S(2)}, u32[]{:S(2)}) collective-permute-start(bf16[256,512]{1,0:T(8,128)(2,1)} %get-tuple-element.86), channel_id=1, source_target_pairs={{0,4},{2,6},{4,0},{6,2},{8,12},{10,14},{12,8},{14,10},{1,5},{3,7},... | collective-permute-start | bytes 786440 | tf_op jit(solution)/shard_map/ppermute | solution.py:206
  28.3 10.2 %collective-permute-start.5 = (bf16[256,512]{1,0:T(8,128)(2,1)S(1)}, bf16[256,512]{1,0:T(8,128)(2,1)S(1)}, u32[]{:S(2)}, u32[]{:S(2)}) collective-permute-start(bf16[256,512]{1,0:T(8,128)(2,1)S(1)} %copy-done.21), channel_id=1, source_target_pairs={{0,6},{2,4},{4,2},{6,0},{8,14},{10,12},{12,10},{14,8},{1,7},{3,5},... | collective-permute-start | bytes 786440 | tf_op jit(solution)/shard_map/ppermute | solution.py:206
  28.8 20.7 %collective-permute-start.10 = (bf16[512,1024]{1,0:T(8,128)(2,1)S(1)}, bf16[512,1024]{1,0:T(8,128)(2,1)S(1)}, u32[]{:S(2)}, u32[]{:S(2)}) collective-permute-start(bf16[512,1024]{1,0:T(8,128)(2,1)S(1)} %copy-done.9), channel_id=1, source_target_pairs={{0,1},{1,0},{2,3},{3,2},{4,5},{5,4},{6,7},{7,6},{8,9},{9,8},{10,11... | collective-permute-start | bytes 3145736 | tf_op jit(solution)/shard_map/ppermute | solution.py:203
  30.7 13.4 %collective-permute-start.6 = (bf16[256,512]{1,0:T(8,128)(2,1)S(1)}, bf16[256,512]{1,0:T(8,128)(2,1)S(1)}, u32[]{:S(2)}, u32[]{:S(2)}) collective-permute-start(bf16[256,512]{1,0:T(8,128)(2,1)S(1)} %get-tuple-element.84), channel_id=1, source_target_pairs={{0,2},{2,0},{4,6},{6,4},{8,10},{10,8},{12,14},{14,12},{1,3},{3,1},... | collective-permute-start | bytes 786440 | tf_op jit(solution)/shard_map/ppermute | solution.py:206
  32.3 11.8 %collective-permute-start.7 = (bf16[256,512]{1,0:T(8,128)(2,1)S(1)}, bf16[256,512]{1,0:T(8,128)(2,1)S(1)}, u32[]{:S(2)}, u32[]{:S(2)}) collective-permute-start(bf16[256,512]{1,0:T(8,128)(2,1)S(1)} %get-tuple-element.83), channel_id=1, source_target_pairs={{0,4},{2,6},{4,0},{6,2},{8,12},{10,14},{12,8},{14,10},{1,5},{3,7},... | collective-permute-start | bytes 786440 | tf_op jit(solution)/shard_map/ppermute | solution.py:206
  33.8 14.4 %collective-permute-start.8 = (bf16[256,512]{1,0:T(8,128)(2,1)S(1)}, bf16[256,512]{1,0:T(8,128)(2,1)S(1)}, u32[]{:S(2)}, u32[]{:S(2)}) collective-permute-start(bf16[256,512]{1,0:T(8,128)(2,1)S(1)} %get-tuple-element.82), channel_id=1, source_target_pairs={{0,6},{2,4},{4,2},{6,0},{8,14},{10,12},{12,10},{14,8},{1,7},{3,5},... | collective-permute-start | bytes 786440 | tf_op jit(solution)/shard_map/ppermute | solution.py:206
  38.5 11.0 %collective-permute-start.11 = (bf16[256,512]{1,0:T(8,128)(2,1)S(1)}, bf16[256,512]{1,0:T(8,128)(2,1)S(1)}, u32[]{:S(2)}, u32[]{:S(2)}) collective-permute-start(bf16[256,512]{1,0:T(8,128)(2,1)S(1)} %get-tuple-element.80), channel_id=1, source_target_pairs={{0,1},{1,0},{2,3},{3,2},{4,5},{5,4},{6,7},{7,6},{8,9},{9,8},{10,11... | collective-permute-start | bytes 786440 | tf_op jit(solution)/shard_map/ppermute | solution.py:203
  58.4 9.9 %collective-permute-start.13 = (bf16[256,512]{1,0:T(8,128)(2,1)}, bf16[256,512]{1,0:T(8,128)(2,1)S(1)}, u32[]{:S(2)}, u32[]{:S(2)}) collective-permute-start(bf16[256,512]{1,0:T(8,128)(2,1)} %get-tuple-element.50), channel_id=1, source_target_pairs={{0,2},{2,0},{4,6},{6,4},{8,10},{10,8},{12,14},{14,12},{1,3},{3,1},... | collective-permute-start | bytes 786440 | tf_op jit(solution)/shard_map/ppermute | solution.py:206
  60.0 9.5 %collective-permute-start.14 = (bf16[256,512]{1,0:T(8,128)(2,1)}, bf16[256,512]{1,0:T(8,128)(2,1)}, u32[]{:S(2)}, u32[]{:S(2)}) collective-permute-start(bf16[256,512]{1,0:T(8,128)(2,1)} %get-tuple-element.51), channel_id=1, source_target_pairs={{0,4},{2,6},{4,0},{6,2},{8,12},{10,14},{12,8},{14,10},{1,5},{3,7},... | collective-permute-start | bytes 786440 | tf_op jit(solution)/shard_map/ppermute | solution.py:206
  60.0 14.0 %collective-permute-start.15 = (bf16[256,512]{1,0:T(8,128)(2,1)}, bf16[256,512]{1,0:T(8,128)(2,1)}, u32[]{:S(2)}, u32[]{:S(2)}) collective-permute-start(bf16[256,512]{1,0:T(8,128)(2,1)} %get-tuple-element.52), channel_id=1, source_target_pairs={{0,6},{2,4},{4,2},{6,0},{8,14},{10,12},{12,10},{14,8},{1,7},{3,5},... | collective-permute-start | bytes 786440 | tf_op jit(solution)/shard_map/ppermute | solution.py:206
  73.9 19.5 %collective-permute-start.17 = (bf16[4,512,128]{2,1,0:T(8,128)(2,1)S(1)}, bf16[4,512,128]{2,1,0:T(8,128)(2,1)S(1)}, u32[]{:S(2)}, u32[]{:S(2)}) collective-permute-start(bf16[4,512,128]{2,1,0:T(8,128)(2,1)S(1)} %get-tuple-element.56), channel_id=1, source_target_pairs={{0,2},{2,0},{4,6},{6,4},{8,10},{10,8},{12,14},{14,12},{1,3},{3,1},... | collective-permute-start | bytes 1572872 | tf_op jit(solution)/shard_map/ppermute | solution.py:206
  76.8 28.6 %collective-permute-start.19 = (bf16[512,512]{1,0:T(8,128)(2,1)S(1)}, bf16[512,512]{1,0:T(8,128)(2,1)S(1)}, u32[]{:S(2)}, u32[]{:S(2)}) collective-permute-start(bf16[512,512]{1,0:T(8,128)(2,1)S(1)} %shard_map.109), channel_id=1, source_target_pairs={{0,8},{2,10},{4,12},{6,14},{8,0},{10,2},{12,4},{14,6},{1,9},{3,11}... | collective-permute-start | bytes 1572872 | tf_op jit(solution)/shard_map/ppermute | solution.py:206
  78.3 18.0 %collective-permute-start.20 = (bf16[256,512]{1,0:T(8,128)(2,1)S(1)}, bf16[256,512]{1,0:T(8,128)(2,1)S(1)}, u32[]{:S(2)}, u32[]{:S(2)}) collective-permute-start(bf16[256,512]{1,0:T(8,128)(2,1)S(1)} %copy-done.26), channel_id=1, source_target_pairs={{0,4},{2,6},{4,0},{6,2},{8,12},{10,14},{12,8},{14,10},{1,5},{3,7},... | collective-permute-start | bytes 786440 | tf_op jit(solution)/shard_map/ppermute | solution.py:206
  80.1 23.4 %collective-permute-start.21 = (bf16[256,512]{1,0:T(8,128)(2,1)S(1)}, bf16[256,512]{1,0:T(8,128)(2,1)S(1)}, u32[]{:S(2)}, u32[]{:S(2)}) collective-permute-start(bf16[256,512]{1,0:T(8,128)(2,1)S(1)} %copy-done.25), channel_id=1, source_target_pairs={{0,6},{2,4},{4,2},{6,0},{8,14},{10,12},{12,10},{14,8},{1,7},{3,5},... | collective-permute-start | bytes 786440 | tf_op jit(solution)/shard_map/ppermute | solution.py:206
  80.2 25.2 %collective-permute-start.16 = (bf16[4,512,128]{2,1,0:T(8,128)(2,1)S(1)}, bf16[4,512,128]{2,1,0:T(8,128)(2,1)S(1)}, u32[]{:S(2)}, u32[]{:S(2)}) collective-permute-start(bf16[4,512,128]{2,1,0:T(8,128)(2,1)S(1)} %get-tuple-element.53), channel_id=1, source_target_pairs={{0,2},{2,0},{4,6},{6,4},{8,10},{10,8},{12,14},{14,12},{1,3},{3,1},... | collective-permute-start | bytes 1572872 | tf_op jit(solution)/shard_map/ppermute | solution.py:206
  93.6 14.0 %collective-permute-start.18 = (bf16[2,512,128]{2,1,0:T(8,128)(2,1)S(1)}, bf16[2,512,128]{2,1,0:T(8,128)(2,1)S(1)}, u32[]{:S(2)}, u32[]{:S(2)}) collective-permute-start(bf16[2,512,128]{2,1,0:T(8,128)(2,1)S(1)} %slice.80), channel_id=1, source_target_pairs={{0,4},{2,6},{4,0},{6,2},{8,12},{10,14},{12,8},{14,10},{1,5},{3,7},... | collective-permute-start | bytes 786440 | tf_op jit(solution)/shard_map/ppermute | solution.py:206
  96.3 14.4 %collective-permute-start.22 = (bf16[256,512]{1,0:T(8,128)(2,1)S(1)}, bf16[256,512]{1,0:T(8,128)(2,1)S(1)}, u32[]{:S(2)}, u32[]{:S(2)}) collective-permute-start(bf16[256,512]{1,0:T(8,128)(2,1)S(1)} %get-tuple-element.64), channel_id=1, source_target_pairs={{0,1},{1,0},{2,3},{3,2},{4,5},{5,4},{6,7},{7,6},{8,9},{9,8},{10,11... | collective-permute-start | bytes 786440 | tf_op jit(solution)/shard_map/ppermute | solution.py:203
  103.5 9.8 %collective-permute-start.23 = (bf16[256,512]{1,0:T(8,128)(2,1)S(1)}, bf16[256,512]{1,0:T(8,128)(2,1)S(1)}, u32[]{:S(2)}, u32[]{:S(2)}) collective-permute-start(bf16[256,512]{1,0:T(8,128)(2,1)S(1)} %copy-done.24), channel_id=1, source_target_pairs={{0,2},{2,0},{4,6},{6,4},{8,10},{10,8},{12,14},{14,12},{1,3},{3,1},... | collective-permute-start | bytes 786440 | tf_op jit(solution)/shard_map/ppermute | solution.py:206
  107.8 9.3 %collective-permute-start.25 = (bf16[2,512,128]{2,1,0:T(8,128)(2,1)S(1)}, bf16[2,512,128]{2,1,0:T(8,128)(2,1)S(1)}, u32[]{:S(2)}, u32[]{:S(2)}) collective-permute-start(bf16[2,512,128]{2,1,0:T(8,128)(2,1)S(1)} %slice.85), channel_id=1, source_target_pairs={{0,4},{2,6},{4,0},{6,2},{8,12},{10,14},{12,8},{14,10},{1,5},{3,7},... | collective-permute-start | bytes 786440 | tf_op jit(solution)/shard_map/ppermute | solution.py:206
  117.2 8.7 %collective-permute-start.26 = (bf16[1,512,128]{2,1,0:T(8,128)(2,1)S(1)}, bf16[1,512,128]{2,1,0:T(8,128)(2,1)S(1)}, u32[]{:S(2)}, u32[]{:S(2)}) collective-permute-start(bf16[1,512,128]{2,1,0:T(8,128)(2,1)S(1)} %slice.118), channel_id=1, source_target_pairs={{0,8},{2,10},{4,12},{6,14},{8,0},{10,2},{12,4},{14,6},{1,9},{3,11}... | collective-permute-start | bytes 393224 | tf_op jit(solution)/shard_map/ppermute | solution.py:206
  (30 other events, 158.5 us)

commit v5 on v4

--- a/solution.py
+++ b/solution.py
@@ -230,19 +230,21 @@
     )
 
     partner = hop(features, across)
-    direct = [hop(lax.dynamic_slice_in_dim(features, info[0, k] * TILE, TILE, 0), k) for k in near]
+    rows_own, rows_away = halves(features)
+    rows_in, w_self_in = swap(rows_away), swap(w_self)
+    picked = [lax.dynamic_slice_in_dim(features, info[0, k] * TILE, TILE, 0) for k in near]
+    direct = [hop(x, k) for x, k in zip(picked, near)]
 
     mine = lax.dynamic_slice_in_dim(tile_list, me * own_blocks, own_blocks, 0).reshape(slots)
     owner = mine // own_blocks
     code = jnp.where(owner == me, mine % own_blocks, 1 + (owner ^ me))
+    code = after(code, rows_in, w_self_in)
     early, early_t = combine(code, tile_values, 0, across + 2)
     late, late_t = combine(code, tile_values, across + 2, across - 1)
     inverse = (1.0 / degree.astype(F32)).reshape(own_rows, 1)
 
-    rows_own, rows_away = halves(features)
     cot_own, cot_away = halves(cotangent)
-    rows_in, cot_in = swap(rows_away), swap(cot_away)
-    w_self_in, w_neigh_in = swap(w_self), swap(w_neigh)
+    cot_in, w_neigh_in = swap(cot_away), swap(w_neigh)
     self_part = mul(rows_own, w_self) + mul(rows_in, w_self_in)
     features_t = features.T
 

time: 127 us -> 127 us (level)
  waiting for transfers between devices: 51.6 us -> 60.5 us
  local copies, waits for them, and re-layouts: 13.1 us -> 5.87 us
  starting transfers between devices: 28.9 us -> 26.5 us
    ppermute x20, waiting for transfers between devices: 48.3 us -> 57.2 us  [hop(): return lax.ppermute(x, 'node', [(i, i ^ k) for i in range(nodes)])]
    unnamed x56 -> x38, local copies, waits for them, and re-layouts: 10.2 us -> 3.82 us
    ppermute x20, starting transfers between devices: 28.1 us -> 25.7 us  [hop(): return lax.ppermute(x, 'node', [(i, i ^ k) for i in range(nodes)])]
    dot_general x2, matrix products: 2.24 us -> 3.51 us  [mul(): return lax.dot_general(a, b, dims, preferred_element_type=F32)]
  transfers between devices with their start and end apart: 27 -> 27, of which waited for: 14 -> 19; matrix products, arithmetic and copies ran while one was open for 10% -> 10% of each run, Pallas kernels for 11% -> 11%
where the time goes in v5:
time: 127 us
  waiting for transfers between devices  60.5 us (48%)
  starting transfers between devices  26.5 us (21%)
  Pallas kernels  19.3 us (15%)
  other arithmetic  6.25 us (5%)
  local copies, waits for them, and re-layouts  5.87 us (5%)
  between operations  4.89 us (4%)
  matrix products  3.51 us (3%)
    ppermute x20, waiting for transfers between devices, hop(): return lax.ppermute(x, 'node', [(i, i ^ k) for i in range(nodes)])  57.2 us
    ppermute x20, starting transfers between devices, hop(): return lax.ppermute(x, 'node', [(i, i ^ k) for i in range(nodes)])  25.7 us
    pallas_call x8, Pallas kernels, local_call(): pl.pallas_call(kernel, out_shape=placed, in_specs=[SMEM] * scalars + [VME...  14.7 us
    pallas_call x2, Pallas kernels, combine(): pl.pallas_call(kernel, grid=(count,), out_shape=[jax.ShapeDtypeStruct((co...  4.55 us
    unnamed x38, local copies, waits for them, and re-layouts  3.82 us
    dot_general x2, matrix products, mul(): return lax.dot_general(a, b, dims, preferred_element_type=F32)  3.51 us
    ppermute x7, waiting for transfers between devices, swap(): return lax.ppermute(x, 'feat', [(0, 1), (1, 0)])  3.28 us
  transfers between devices with their start and end apart: 27, of which 19 were waited for; matrix products, arithmetic and copies ran while one was open for 10% of the time, Pallas kernels for 11%

profile of v5, /device:TPU:0, one launch (start us, length us, event | category | flops | bytes accessed | tf_op | source)
XLA Modules:
  0.0 126.8 jit_solution(15164498652920301703)
XLA Ops:
  0.7 4.1 %collective-permute-start.2 = (bf16[512,512]{1,0:T(8,128)(2,1)}, bf16[512,512]{1,0:T(8,128)(2,1)S(1)}, u32[]{:S(2)}, u32[]{:S(2)}) collective-permute-start(bf16[512,512]{1,0:T(8,128)(2,1)} %own.1), channel_id=1, source_target_pairs={{0,8},{2,10},{4,12},{6,14},{8,0},{10,2},{12,4},{14,6},{1,9},{3,11}... | collective-permute-start | bytes 1572872 | tf_op jit(solution)/shard_map/ppermute | solution.py:206
  8.7 2.5 %constant_dynamic-slice_fusion.3 = (bf16[256,512]{1,0:T(8,128)(2,1)}, bf16[256,512]{1,0:T(8,128)(2,1)}, bf16[256,512]{1,0:T(8,128)(2,1)}, bf16[256,512]{1,0:T(8,128)(2,1)}) fusion(bf16[512,512]{1,0:T(8,128)(2,1)} %own.1, s32[]{:T(128)S(6)} %select_n.86, s32[]{:T(128)S(6)} %select_n.85, s32[]{:T(128)S(6)} %select_n.84, pred[]{:T(512)S(6)} %eq.85), kind=kLoop, calls=%fused_computation.37 | loop fusion | flops 131072 | bytes 2359309 | tf_op jit(solution)/shard_map/dynamic_slice | solution.py:235
  21.0 2.1 %convolution_add_fusion.self_part = f32[256,1024]{1,0:T(8,128)S(1)} fusion(f32[256,1024]{1,0:T(8,128)} %fusion.2, bf16[256,512]{1,0:T(8,128)(2,1)} %collective-permute-done, bf16[512,1024]{1,0:T(8,128)(2,1)} %collective-permute-done.1), kind=kOutput, calls=%fused_computation | convolution fusion | flops 268697600 | bytes 3407872 | tf_op jit(solution)/shard_map/dot_general | solution.py:21
  24.8 2.9 %shard_map.103 = (bf16[6,512,256]{2,1,0:T(8,128)(2,1)S(1)}, bf16[6,256,512]{2,1,0:T(8,128)(2,1)S(1)}) custom-call(s32[16]{0:T(128)S(1)} %compare_select_fusion.code_ref, bf16[2,8,256,256]{3,2,1,0:T(8,128)(2,1)S(1)} %copy-done.1), custom_call_target="tpu_custom_call" | custom-call | bytes 5242880 | tf_op jit(solution)/shard_map/pallas_call | solution.py:66
  30.8 1.9 %collective-permute-done.4.rest_1_ = bf16[256,512]{1,0:T(8,128)(2,1)} collective-permute-done((bf16[256,512]{1,0:T(8,128)(2,1)}, bf16[256,512]{1,0:T(8,128)(2,1)}, u32[]{:S(2)}, u32[]{:S(2)}) %collective-permute-start.4) | collective-permute-done | bytes 262176 | tf_op jit(solution)/shard_map/ppermute | solution.py:206
  32.7 5.6 %collective-permute-done.5.rest_2_ = bf16[256,512]{1,0:T(8,128)(2,1)S(1)} collective-permute-done((bf16[256,512]{1,0:T(8,128)(2,1)}, bf16[256,512]{1,0:T(8,128)(2,1)S(1)}, u32[]{:S(2)}, u32[]{:S(2)}) %collective-permute-start.5) | collective-permute-done | bytes 262176 | tf_op jit(solution)/shard_map/ppermute | solution.py:206
  38.3 2.0 %shard_map.104.early = f32[512,512]{1,0:T(8,128)S(1)} custom-call(s32[4,8]{1,0:T(4,128)S(1)} %pad_add_fusion.info, bf16[6,512,256]{2,1,0:T(8,128)(2,1)S(1)} %get-tuple-element.41.matrix, bf16[512,512]{1,0:T(8,128)(2,1)S(1)} %copy-done, bf16[512,512]{1,0:T(8,128)(2,1)S(1)} %collective-permute-done.2.partner, bf16[256,512]{1,0:T(8,128)(2,1)} %collective-permute-done.3.rest_0_, ...), custom_call_target="tpu_custom_call" | custom-call | flops 805306368 | bytes 4456576 | tf_op jit(solution)/shard_map/pallas_call | solution.py:37
  40.4 1.7 %collective-permute-done.6.rest_0_ = bf16[256,512]{1,0:T(8,128)(2,1)S(1)} collective-permute-done((bf16[256,512]{1,0:T(8,128)(2,1)S(1)}, bf16[256,512]{1,0:T(8,128)(2,1)S(1)}, u32[]{:S(2)}, u32[]{:S(2)}) %collective-permute-start.6) | collective-permute-done | bytes 262176 | tf_op jit(solution)/shard_map/ppermute | solution.py:206
  42.1 1.7 %collective-permute-done.7.rest_1_ = bf16[256,512]{1,0:T(8,128)(2,1)S(1)} collective-permute-done((bf16[256,512]{1,0:T(8,128)(2,1)S(1)}, bf16[256,512]{1,0:T(8,128)(2,1)S(1)}, u32[]{:S(2)}, u32[]{:S(2)}) %collective-permute-start.7) | collective-permute-done | bytes 262176 | tf_op jit(solution)/shard_map/ppermute | solution.py:206
  43.8 4.6 %collective-permute-done.8.rest_2_ = bf16[256,512]{1,0:T(8,128)(2,1)S(1)} collective-permute-done((bf16[256,512]{1,0:T(8,128)(2,1)S(1)}, bf16[256,512]{1,0:T(8,128)(2,1)S(1)}, u32[]{:S(2)}, u32[]{:S(2)}) %collective-permute-start.8) | collective-permute-done | bytes 262176 | tf_op jit(solution)/shard_map/ppermute | solution.py:206
  51.1 2.3 %shard_map.106 = (bf16[256,1024]{1,0:T(8,128)(2,1)S(1)}, bf16[2,256,512]{2,1,0:T(8,128)(2,1)}) custom-call(s32[4,8]{1,0:T(4,128)S(1)} %pad_add_fusion.info, f32[256,1024]{1,0:T(8,128)S(1)} %convolution_add_fusion.self_part, bf16[512,512]{1,0:T(8,128)(2,1)S(1)} %get-tuple-element.43.agg, bf16[256,512]{1,0:T(8,128)(2,1)S(1)} %collective-permute-done.9.agg_in, ...), custom_call_target="tpu_custom_call" | custom-call | flops 536870912 | bytes 5505152 | tf_op jit(solution)/shard_map/pallas_call | solution.py:37
  53.7 1.8 %collective-permute-done.12.slope_in = bf16[256,1024]{1,0:T(8,128)(2,1)S(1)} collective-permute-done((bf16[256,1024]{1,0:T(8,128)(2,1)S(1)}, bf16[256,1024]{1,0:T(8,128)(2,1)S(1)}, u32[]{:S(2)}, u32[]{:S(2)}) %collective-permute-start.12) | collective-permute-done | bytes 524320 | tf_op jit(solution)/shard_map/ppermute | solution.py:203
  55.4 3.1 %shard_map.107 = (bf16[512,1024]{1,0:T(8,128)(2,1)}, bf16[512,512]{1,0:T(8,128)(2,1)}, f32[256,512]{1,0:T(8,128)}, bf16[256,512]{1,0:T(8,128)(2,1)}, bf16[256,51...) custom-call(s32[4,8]{1,0:T(4,128)S(1)} %pad_add_fusion.info, ...), custom_call_target="tpu_custom_call" | custom-call | flops 1476395008 | bytes 8128640 | tf_op jit(solution)/shard_map/pallas_call | solution.py:37
  60.0 2.2 %collective-permute-start.15 = (bf16[256,512]{1,0:T(8,128)(2,1)}, bf16[256,512]{1,0:T(8,128)(2,1)S(1)}, u32[]{:S(2)}, u32[]{:S(2)}) collective-permute-start(bf16[256,512]{1,0:T(8,128)(2,1)} %get-tuple-element.54), channel_id=1, source_target_pairs={{0,6},{2,4},{4,2},{6,0},{8,14},{10,12},{12,10},{14,8},{1,7},{3,5},... | collective-permute-start | bytes 786440 | tf_op jit(solution)/shard_map/ppermute | solution.py:206
  63.6 2.0 %shard_map.108 = (f32[4,512,128]{2,1,0:T(8,128)S(1)}, bf16[4,512,128]{2,1,0:T(8,128)(2,1)S(1)}, f32[4,512,128]{2,1,0:T(8,128)S(1)}, bf16[4,512,128]{2,1,0:T(8,128)(2,1)S(1)}) custom-call(s32[4,8]{1,0:T(4,128)S(1)} %pad_add_fusion.info, bf16[512,1024]{1,0:T(8,128)(2,1)S(1)} %copy-done.5, bf16[512,512]{1,0:T(8,128)(2,1)S(1)} %bitcast.26, ...), custom_call_target="tpu_custom_call" | custom-call | flops 1073741824 | bytes 5243008 | tf_op jit(solution)/shard_map/pallas_call | solution.py:37
  67.2 2.2 %collective-permute-done.14.rest_1_ = bf16[256,512]{1,0:T(8,128)(2,1)S(1)} collective-permute-done((bf16[256,512]{1,0:T(8,128)(2,1)}, bf16[256,512]{1,0:T(8,128)(2,1)S(1)}, u32[]{:S(2)}, u32[]{:S(2)}) %collective-permute-start.14) | collective-permute-done | bytes 262176 | tf_op jit(solution)/shard_map/ppermute | solution.py:206
  69.4 4.6 %collective-permute-done.15.rest_2_ = bf16[256,512]{1,0:T(8,128)(2,1)S(1)} collective-permute-done((bf16[256,512]{1,0:T(8,128)(2,1)}, bf16[256,512]{1,0:T(8,128)(2,1)S(1)}, u32[]{:S(2)}, u32[]{:S(2)}) %collective-permute-start.15) | collective-permute-done | bytes 262176 | tf_op jit(solution)/shard_map/ppermute | solution.py:206
  77.6 1.7 %collective-permute-start.20 = (bf16[256,512]{1,0:T(8,128)(2,1)S(1)}, bf16[256,512]{1,0:T(8,128)(2,1)S(1)}, u32[]{:S(2)}, u32[]{:S(2)}) collective-permute-start(bf16[256,512]{1,0:T(8,128)(2,1)S(1)} %copy-done.17), channel_id=1, source_target_pairs={{0,4},{2,6},{4,0},{6,2},{8,12},{10,14},{12,8},{14,10},{1,5},{3,7},... | collective-permute-start | bytes 786440 | tf_op jit(solution)/shard_map/ppermute | solution.py:206
  81.1 13.4 %collective-permute-done.17 = bf16[4,512,128]{2,1,0:T(8,128)(2,1)S(1)} collective-permute-done((bf16[4,512,128]{2,1,0:T(8,128)(2,1)S(1)}, bf16[4,512,128]{2,1,0:T(8,128)(2,1)S(1)}, u32[]{:S(2)}, u32[]{:S(2)}) %collective-permute-start.17) | collective-permute-done | bytes 524320 | tf_op jit(solution)/shard_map/ppermute | solution.py:206
  95.6 5.8 %collective-permute-done.21.rest_2_ = bf16[256,512]{1,0:T(8,128)(2,1)S(1)} collective-permute-done((bf16[256,512]{1,0:T(8,128)(2,1)S(1)}, bf16[256,512]{1,0:T(8,128)(2,1)S(1)}, u32[]{:S(2)}, u32[]{:S(2)}) %collective-permute-start.21) | collective-permute-done | bytes 262176 | tf_op jit(solution)/shard_map/ppermute | solution.py:206
  103.1 2.6 %collective-permute-done.16 = bf16[4,512,128]{2,1,0:T(8,128)(2,1)S(1)} collective-permute-done((bf16[4,512,128]{2,1,0:T(8,128)(2,1)S(1)}, bf16[4,512,128]{2,1,0:T(8,128)(2,1)S(1)}, u32[]{:S(2)}, u32[]{:S(2)}) %collective-permute-start.16) | collective-permute-done | bytes 524320 | tf_op jit(solution)/shard_map/ppermute | solution.py:206
  107.7 2.3 %collective-permute-start.24 = (bf16[1,512,128]{2,1,0:T(8,128)(2,1)S(1)}, bf16[1,512,128]{2,1,0:T(8,128)(2,1)S(1)}, u32[]{:S(2)}, u32[]{:S(2)}) collective-permute-start(bf16[1,512,128]{2,1,0:T(8,128)(2,1)S(1)} %slice.119), channel_id=1, source_target_pairs={{0,8},{2,10},{4,12},{6,14},{8,0},{10,2},{12,4},{14,6},{1,9},{3,11}... | collective-permute-start | bytes 393224 | tf_op jit(solution)/shard_map/ppermute | solution.py:206
  115.7 2.2 %collective-permute-done.25 = bf16[2,512,128]{2,1,0:T(8,128)(2,1)S(1)} collective-permute-done((bf16[2,512,128]{2,1,0:T(8,128)(2,1)S(1)}, bf16[2,512,128]{2,1,0:T(8,128)(2,1)S(1)}, u32[]{:S(2)}, u32[]{:S(2)}) %collective-permute-start.25) | collective-permute-done | bytes 262176 | tf_op jit(solution)/shard_map/ppermute | solution.py:206
  120.0 6.1 %collective-permute-done.26 = bf16[1,512,128]{2,1,0:T(8,128)(2,1)S(1)} collective-permute-done((bf16[1,512,128]{2,1,0:T(8,128)(2,1)S(1)}, bf16[1,512,128]{2,1,0:T(8,128)(2,1)S(1)}, u32[]{:S(2)}, u32[]{:S(2)}) %collective-permute-start.26) | collective-permute-done | bytes 131104 | tf_op jit(solution)/shard_map/ppermute | solution.py:206
  (116 shorter events, 40.6 us)
Async XLA Ops:
  0.7 27.6 %collective-permute-start.2 = (bf16[512,512]{1,0:T(8,128)(2,1)}, bf16[512,512]{1,0:T(8,128)(2,1)S(1)}, u32[]{:S(2)}, u32[]{:S(2)}) collective-permute-start(bf16[512,512]{1,0:T(8,128)(2,1)} %own.1), channel_id=1, source_target_pairs={{0,8},{2,10},{4,12},{6,14},{8,0},{10,2},{12,4},{14,6},{1,9},{3,11}... | collective-permute-start | bytes 1572872 | tf_op jit(solution)/shard_map/ppermute | solution.py:206
  11.2 9.2 %collective-permute-start = (bf16[256,512]{1,0:T(8,128)(2,1)}, bf16[256,512]{1,0:T(8,128)(2,1)}, u32[]{:S(2)}, u32[]{:S(2)}) collective-permute-start(bf16[256,512]{1,0:T(8,128)(2,1)} %get-tuple-element.90), channel_id=1, source_target_pairs={{0,1},{1,0},{2,3},{3,2},{4,5},{5,4},{6,7},{7,6},{8,9},{9,8},{10,11... | collective-permute-start | bytes 786440 | tf_op jit(solution)/shard_map/ppermute | solution.py:203
  11.2 9.8 %collective-permute-start.1 = (bf16[512,1024]{1,0:T(8,128)(2,1)S(1)}, bf16[512,1024]{1,0:T(8,128)(2,1)}, u32[]{:S(2)}, u32[]{:S(2)}) collective-permute-start(bf16[512,1024]{1,0:T(8,128)(2,1)S(1)} %copy-done.2), channel_id=1, source_target_pairs={{0,1},{1,0},{2,3},{3,2},{4,5},{5,4},{6,7},{7,6},{8,9},{9,8},{10,11... | collective-permute-start | bytes 3145736 | tf_op jit(solution)/shard_map/ppermute | solution.py:203
  11.7 18.3 %collective-permute-start.3 = (bf16[256,512]{1,0:T(8,128)(2,1)}, bf16[256,512]{1,0:T(8,128)(2,1)}, u32[]{:S(2)}, u32[]{:S(2)}) collective-permute-start(bf16[256,512]{1,0:T(8,128)(2,1)} %get-tuple-element.89), channel_id=1, source_target_pairs={{0,2},{2,0},{4,6},{6,4},{8,10},{10,8},{12,14},{14,12},{1,3},{3,1},... | collective-permute-start | bytes 786440 | tf_op jit(solution)/shard_map/ppermute | solution.py:206
  13.1 19.6 %collective-permute-start.4 = (bf16[256,512]{1,0:T(8,128)(2,1)}, bf16[256,512]{1,0:T(8,128)(2,1)}, u32[]{:S(2)}, u32[]{:S(2)}) collective-permute-start(bf16[256,512]{1,0:T(8,128)(2,1)} %get-tuple-element.88), channel_id=1, source_target_pairs={{0,4},{2,6},{4,0},{6,2},{8,12},{10,14},{12,8},{14,10},{1,5},{3,7},... | collective-permute-start | bytes 786440 | tf_op jit(solution)/shard_map/ppermute | solution.py:206
  20.4 18.0 %collective-permute-start.5 = (bf16[256,512]{1,0:T(8,128)(2,1)}, bf16[256,512]{1,0:T(8,128)(2,1)S(1)}, u32[]{:S(2)}, u32[]{:S(2)}) collective-permute-start(bf16[256,512]{1,0:T(8,128)(2,1)} %get-tuple-element.87), channel_id=1, source_target_pairs={{0,6},{2,4},{4,2},{6,0},{8,14},{10,12},{12,10},{14,8},{1,7},{3,5},... | collective-permute-start | bytes 786440 | tf_op jit(solution)/shard_map/ppermute | solution.py:206
  21.0 28.6 %collective-permute-start.10 = (bf16[512,1024]{1,0:T(8,128)(2,1)S(1)}, bf16[512,1024]{1,0:T(8,128)(2,1)S(1)}, u32[]{:S(2)}, u32[]{:S(2)}) collective-permute-start(bf16[512,1024]{1,0:T(8,128)(2,1)S(1)} %copy-done.7), channel_id=1, source_target_pairs={{0,1},{1,0},{2,3},{3,2},{4,5},{5,4},{6,7},{7,6},{8,9},{9,8},{10,11... | collective-permute-start | bytes 3145736 | tf_op jit(solution)/shard_map/ppermute | solution.py:203
  28.3 13.8 %collective-permute-start.6 = (bf16[256,512]{1,0:T(8,128)(2,1)S(1)}, bf16[256,512]{1,0:T(8,128)(2,1)S(1)}, u32[]{:S(2)}, u32[]{:S(2)}) collective-permute-start(bf16[256,512]{1,0:T(8,128)(2,1)S(1)} %get-tuple-element.86), channel_id=1, source_target_pairs={{0,2},{2,0},{4,6},{6,4},{8,10},{10,8},{12,14},{14,12},{1,3},{3,1},... | collective-permute-start | bytes 786440 | tf_op jit(solution)/shard_map/ppermute | solution.py:206
  30.0 13.9 %collective-permute-start.7 = (bf16[256,512]{1,0:T(8,128)(2,1)S(1)}, bf16[256,512]{1,0:T(8,128)(2,1)S(1)}, u32[]{:S(2)}, u32[]{:S(2)}) collective-permute-start(bf16[256,512]{1,0:T(8,128)(2,1)S(1)} %get-tuple-element.85), channel_id=1, source_target_pairs={{0,4},{2,6},{4,0},{6,2},{8,12},{10,14},{12,8},{14,10},{1,5},{3,7},... | collective-permute-start | bytes 786440 | tf_op jit(solution)/shard_map/ppermute | solution.py:206
  32.6 15.7 %collective-permute-start.8 = (bf16[256,512]{1,0:T(8,128)(2,1)S(1)}, bf16[256,512]{1,0:T(8,128)(2,1)S(1)}, u32[]{:S(2)}, u32[]{:S(2)}) collective-permute-start(bf16[256,512]{1,0:T(8,128)(2,1)S(1)} %get-tuple-element.84), channel_id=1, source_target_pairs={{0,6},{2,4},{4,2},{6,0},{8,14},{10,12},{12,10},{14,8},{1,7},{3,5},... | collective-permute-start | bytes 786440 | tf_op jit(solution)/shard_map/ppermute | solution.py:206
  38.3 11.3 %collective-permute-start.11 = (bf16[256,512]{1,0:T(8,128)(2,1)S(1)}, bf16[256,512]{1,0:T(8,128)(2,1)S(1)}, u32[]{:S(2)}, u32[]{:S(2)}) collective-permute-start(bf16[256,512]{1,0:T(8,128)(2,1)S(1)} %get-tuple-element.82), channel_id=1, source_target_pairs={{0,1},{1,0},{2,3},{3,2},{4,5},{5,4},{6,7},{7,6},{8,9},{9,8},{10,11... | collective-permute-start | bytes 786440 | tf_op jit(solution)/shard_map/ppermute | solution.py:203
  58.6 8.6 %collective-permute-start.13 = (bf16[256,512]{1,0:T(8,128)(2,1)}, bf16[256,512]{1,0:T(8,128)(2,1)S(1)}, u32[]{:S(2)}, u32[]{:S(2)}) collective-permute-start(bf16[256,512]{1,0:T(8,128)(2,1)} %get-tuple-element.52), channel_id=1, source_target_pairs={{0,2},{2,0},{4,6},{6,4},{8,10},{10,8},{12,14},{14,12},{1,3},{3,1},... | collective-permute-start | bytes 786440 | tf_op jit(solution)/shard_map/ppermute | solution.py:206
  60.0 9.4 %collective-permute-start.14 = (bf16[256,512]{1,0:T(8,128)(2,1)}, bf16[256,512]{1,0:T(8,128)(2,1)S(1)}, u32[]{:S(2)}, u32[]{:S(2)}) collective-permute-start(bf16[256,512]{1,0:T(8,128)(2,1)} %get-tuple-element.53), channel_id=1, source_target_pairs={{0,4},{2,6},{4,0},{6,2},{8,12},{10,14},{12,8},{14,10},{1,5},{3,7},... | collective-permute-start | bytes 786440 | tf_op jit(solution)/shard_map/ppermute | solution.py:206
  60.0 14.0 %collective-permute-start.15 = (bf16[256,512]{1,0:T(8,128)(2,1)}, bf16[256,512]{1,0:T(8,128)(2,1)S(1)}, u32[]{:S(2)}, u32[]{:S(2)}) collective-permute-start(bf16[256,512]{1,0:T(8,128)(2,1)} %get-tuple-element.54), channel_id=1, source_target_pairs={{0,6},{2,4},{4,2},{6,0},{8,14},{10,12},{12,10},{14,8},{1,7},{3,5},... | collective-permute-start | bytes 786440 | tf_op jit(solution)/shard_map/ppermute | solution.py:206
  74.0 20.4 %collective-permute-start.17 = (bf16[4,512,128]{2,1,0:T(8,128)(2,1)S(1)}, bf16[4,512,128]{2,1,0:T(8,128)(2,1)S(1)}, u32[]{:S(2)}, u32[]{:S(2)}) collective-permute-start(bf16[4,512,128]{2,1,0:T(8,128)(2,1)S(1)} %get-tuple-element.58), channel_id=1, source_target_pairs={{0,2},{2,0},{4,6},{6,4},{8,10},{10,8},{12,14},{14,12},{1,3},{3,1},... | collective-permute-start | bytes 1572872 | tf_op jit(solution)/shard_map/ppermute | solution.py:206
  76.2 26.9 %collective-permute-start.19 = (bf16[512,512]{1,0:T(8,128)(2,1)S(1)}, bf16[512,512]{1,0:T(8,128)(2,1)S(1)}, u32[]{:S(2)}, u32[]{:S(2)}) collective-permute-start(bf16[512,512]{1,0:T(8,128)(2,1)S(1)} %shard_map.109), channel_id=1, source_target_pairs={{0,8},{2,10},{4,12},{6,14},{8,0},{10,2},{12,4},{14,6},{1,9},{3,11}... | collective-permute-start | bytes 1572872 | tf_op jit(solution)/shard_map/ppermute | solution.py:206
  77.6 18.0 %collective-permute-start.20 = (bf16[256,512]{1,0:T(8,128)(2,1)S(1)}, bf16[256,512]{1,0:T(8,128)(2,1)S(1)}, u32[]{:S(2)}, u32[]{:S(2)}) collective-permute-start(bf16[256,512]{1,0:T(8,128)(2,1)S(1)} %copy-done.17), channel_id=1, source_target_pairs={{0,4},{2,6},{4,0},{6,2},{8,12},{10,14},{12,8},{14,10},{1,5},{3,7},... | collective-permute-start | bytes 786440 | tf_op jit(solution)/shard_map/ppermute | solution.py:206
  79.3 22.1 %collective-permute-start.21 = (bf16[256,512]{1,0:T(8,128)(2,1)S(1)}, bf16[256,512]{1,0:T(8,128)(2,1)S(1)}, u32[]{:S(2)}, u32[]{:S(2)}) collective-permute-start(bf16[256,512]{1,0:T(8,128)(2,1)S(1)} %copy-done.16), channel_id=1, source_target_pairs={{0,6},{2,4},{4,2},{6,0},{8,14},{10,12},{12,10},{14,8},{1,7},{3,5},... | collective-permute-start | bytes 786440 | tf_op jit(solution)/shard_map/ppermute | solution.py:206
  79.6 26.1 %collective-permute-start.16 = (bf16[4,512,128]{2,1,0:T(8,128)(2,1)S(1)}, bf16[4,512,128]{2,1,0:T(8,128)(2,1)S(1)}, u32[]{:S(2)}, u32[]{:S(2)}) collective-permute-start(bf16[4,512,128]{2,1,0:T(8,128)(2,1)S(1)} %get-tuple-element.55), channel_id=1, source_target_pairs={{0,2},{2,0},{4,6},{6,4},{8,10},{10,8},{12,14},{14,12},{1,3},{3,1},... | collective-permute-start | bytes 1572872 | tf_op jit(solution)/shard_map/ppermute | solution.py:206
  94.6 12.3 %collective-permute-start.18 = (bf16[2,512,128]{2,1,0:T(8,128)(2,1)S(1)}, bf16[2,512,128]{2,1,0:T(8,128)(2,1)S(1)}, u32[]{:S(2)}, u32[]{:S(2)}) collective-permute-start(bf16[2,512,128]{2,1,0:T(8,128)(2,1)S(1)} %slice.80), channel_id=1, source_target_pairs={{0,4},{2,6},{4,0},{6,2},{8,12},{10,14},{12,8},{14,10},{1,5},{3,7},... | collective-permute-start | bytes 786440 | tf_op jit(solution)/shard_map/ppermute | solution.py:206
  95.6 14.5 %collective-permute-start.22 = (bf16[256,512]{1,0:T(8,128)(2,1)S(1)}, bf16[256,512]{1,0:T(8,128)(2,1)S(1)}, u32[]{:S(2)}, u32[]{:S(2)}) collective-permute-start(bf16[256,512]{1,0:T(8,128)(2,1)S(1)} %get-tuple-element.66), channel_id=1, source_target_pairs={{0,1},{1,0},{2,3},{3,2},{4,5},{5,4},{6,7},{7,6},{8,9},{9,8},{10,11... | collective-permute-start | bytes 786440 | tf_op jit(solution)/shard_map/ppermute | solution.py:203
  101.4 11.2 %collective-permute-start.23 = (bf16[256,512]{1,0:T(8,128)(2,1)S(1)}, bf16[256,512]{1,0:T(8,128)(2,1)S(1)}, u32[]{:S(2)}, u32[]{:S(2)}) collective-permute-start(bf16[256,512]{1,0:T(8,128)(2,1)S(1)} %copy-done.15), channel_id=1, source_target_pairs={{0,2},{2,0},{4,6},{6,4},{8,10},{10,8},{12,14},{14,12},{1,3},{3,1},... | collective-permute-start | bytes 786440 | tf_op jit(solution)/shard_map/ppermute | solution.py:206
  107.1 10.8 %collective-permute-start.25 = (bf16[2,512,128]{2,1,0:T(8,128)(2,1)S(1)}, bf16[2,512,128]{2,1,0:T(8,128)(2,1)S(1)}, u32[]{:S(2)}, u32[]{:S(2)}) collective-permute-start(bf16[2,512,128]{2,1,0:T(8,128)(2,1)S(1)} %slice.85), channel_id=1, source_target_pairs={{0,4},{2,6},{4,0},{6,2},{8,12},{10,14},{12,8},{14,10},{1,5},{3,7},... | collective-permute-start | bytes 786440 | tf_op jit(solution)/shard_map/ppermute | solution.py:206
  118.0 8.1 %collective-permute-start.26 = (bf16[1,512,128]{2,1,0:T(8,128)(2,1)S(1)}, bf16[1,512,128]{2,1,0:T(8,128)(2,1)S(1)}, u32[]{:S(2)}, u32[]{:S(2)}) collective-permute-start(bf16[1,512,128]{2,1,0:T(8,128)(2,1)S(1)} %slice.118), channel_id=1, source_target_pairs={{0,8},{2,10},{4,12},{6,14},{8,0},{10,2},{12,4},{14,6},{1,9},{3,11}... | collective-permute-start | bytes 393224 | tf_op jit(solution)/shard_map/ppermute | solution.py:206
  (21 other events, 175.3 us)
